TPU v7x, 32 devices: a whole 2x2x4 slice. The times are simulated.
32 devices in a mesh: ctx: 4 (over y, core), dp: 8 (over z, x).
Axes of the slice: x: 2, y: 2, z: 4, core: 2. Of those that a mesh axis runs over, the one named last changes fastest.
Arguments:
- token_ids: int32 [8, 512], P('dp', 'ctx'), may hold values from 0 to 511
- feature_table: bfloat16 [3072, 512], replicated, may hold values from -6 to 6
- short_weight: float32 [3072, 7], replicated, may hold values from -3 to 3
- residue: float32 [1024, 16], replicated, may hold values from -0.1875 to 0.1875
- rates: float32 [16], replicated, may hold values from 0.3 to 16
- skip_gain: float32 [1024], replicated, may hold values from 0.5 to 1.5
- grad_out: bfloat16 [8, 1024, 512], P('dp', None, 'ctx'), may hold values from -0.01171875 to 0.01171875
Outputs:
- mixed: bfloat16 [8, 1024, 512], P('dp', None, 'ctx')
- grad_residue: float32 [1024, 16], replicated
- grad_rate: float32 [16], replicated
All inputs are finite; a program needn't handle non-finite values.
Results may differ from a plain program's by a relative error of at most 0.0065.
Values may be sent and summed in bfloat16 or wider, within the bound.
No kernel may reach another device: no remote copies, remote signals or barrier semaphores. Data moves between devices by JAX's collectives and lax.ppermute only.
A program may use at most 64 MiB of HBM per device.

v0:
```python
import math

import jax
import jax.numpy as jnp
from jax import lax
from jax.sharding import PartitionSpec as P

HIGHEST = lax.Precision.HIGHEST


def from_behind(block, axis, distance):
    devices = range(lax.axis_size(axis))
    route = [((i - distance) % len(devices), i) for i in devices]
    return lax.ppermute(block, axis, route)


def split_table(table):
    upper = table.astype(jnp.bfloat16)
    lower = (table - upper.astype(jnp.float32)).astype(jnp.bfloat16)
    return (upper, lower)


def split_dot(data, halves):
    return jnp.dot(data, halves[0], preferred_element_type=jnp.float32) + jnp.dot(
        data, halves[1], preferred_element_type=jnp.float32
    )


def dft_tables(block_len):
    period = 2 * block_len
    sample = jnp.arange(period, dtype=jnp.int32)[:, None]
    harmonic = jnp.arange(block_len, dtype=jnp.int32)[None, :]
    phase = (sample * harmonic % period).astype(jnp.float32) * (2.0 * math.pi / period)
    parity = 1.0 - 2.0 * (sample % 2).astype(jnp.float32)
    forward = jnp.concatenate(
        [jnp.cos(phase), jnp.where(harmonic == 0, parity, -jnp.sin(phase))], axis=1
    )
    outputs = block_len + jnp.arange(block_len, dtype=jnp.int32)[None, :]
    column = jnp.arange(block_len, dtype=jnp.int32)[:, None]
    angle = (column * outputs % period).astype(jnp.float32) * (2.0 * math.pi / period)
    leading = column == 0
    real_rows = jnp.where(leading, 1.0, 2.0) / period * jnp.cos(angle)
    out_parity = (1.0 - 2.0 * (outputs % 2).astype(jnp.float32)) / period
    imag_rows = jnp.where(leading, out_parity, -2.0 / period * jnp.sin(angle))
    inverse = jnp.concatenate([real_rows, imag_rows], axis=0)
    parseval = jnp.where(jnp.arange(period) % block_len == 0, 1.0, 2.0) / period
    return (forward, inverse, parseval)


def packed_product(left, right, conjugate):
    half = left.shape[-1] // 2
    left_re = left[..., :half]
    left_im = left[..., half:]
    right_re = right[..., :half]
    right_im = right[..., half:]
    leading = jnp.arange(half) == 0
    if conjugate:
        real_part = jnp.where(leading, left_re * right_re, left_re * right_re + left_im * right_im)
        imag_part = jnp.where(leading, left_im * right_im, left_re * right_im - left_im * right_re)
    else:
        real_part = jnp.where(leading, left_re * right_re, left_re * right_re - left_im * right_im)
        imag_part = jnp.where(leading, left_im * right_im, left_re * right_im + left_im * right_re)
    return jnp.concatenate([real_part, imag_part], axis=-1)


def per_device(token_ids, feature_table, short_weight, residue, rates, skip_gain, grad_out):
    block_len = token_ids.shape[1]
    blocks = lax.axis_size("ctx")
    own_index = lax.axis_index("ctx")
    seq_len = block_len * blocks
    channels = residue.shape[0]
    modes = residue.shape[1]
    vocab_size = feature_table.shape[1]
    taps_short = short_weight.shape[1]
    ids_row = token_ids[0]
    previous = from_behind(ids_row[block_len - (taps_short - 1) :], "ctx", 1)
    vocab_column = jnp.arange(vocab_size, dtype=jnp.int32)[:, None]
    onehot_own = (vocab_column == ids_row[None, :]).astype(jnp.bfloat16)
    onehot_prev = (vocab_column == previous[None, :]).astype(jnp.bfloat16)
    feature_own = jnp.dot(feature_table, onehot_own, preferred_element_type=jnp.float32)
    feature_prev = jnp.dot(feature_table, onehot_prev, preferred_element_type=jnp.float32)
    padded = jnp.concatenate([feature_prev, feature_own], axis=1)
    mixer = jnp.zeros(feature_own.shape, jnp.float32)
    for offset in range(taps_short):
        mixer = (
            mixer + short_weight[:, offset : offset + 1] * padded[:, offset : offset + block_len]
        )
    queries = mixer[:channels]
    gated = (mixer[channels : 2 * channels] * mixer[2 * channels :]).astype(jnp.bfloat16)
    gated_f = gated.astype(jnp.float32)
    forward, inverse, parseval = dft_tables(block_len)
    forward_low = split_table(forward[:block_len])
    forward_high = forward[block_len:]
    dconv = queries * grad_out[0].astype(jnp.float32)
    dconv_spec = jnp.dot(dconv, forward_high, precision=HIGHEST)
    sample = jnp.arange(2 * block_len, dtype=jnp.int32)
    mode_index = jnp.arange(modes, dtype=jnp.int32)[:, None] + 1
    period = 2 * modes + 2

    def mode_spectra(offset):
        delay = (offset * block_len - block_len + sample) % seq_len
        delay_f = delay.astype(jnp.float32)
        cycle_step = mode_index * delay[None, :] % period
        oscillation = jnp.cos(cycle_step.astype(jnp.float32) * (2.0 * math.pi / period))
        power = jnp.exp(-rates[:, None] * delay_f[None, :] / seq_len) * oscillation
        slope = power * (-delay_f[None, :] / seq_len)
        stacked = jnp.concatenate([power, slope], axis=0)
        return jnp.dot(stacked, forward, precision=HIGHEST)

    def pair_terms(block, source):
        offset = (own_index - source) % blocks
        block_spec = split_dot(block, forward_low)
        spectra = mode_spectra(offset)
        filt_spec = jnp.dot(residue, spectra[:modes], precision=HIGHEST)
        out_spec = packed_product(filt_spec, block_spec, False)
        cross_spec = packed_product(block_spec, dconv_spec, True) * parseval[None, :]
        grad_terms = jnp.dot(cross_spec, spectra.T, precision=HIGHEST)
        return (out_spec, grad_terms)

    def process(carry, block, source):
        out_spec, grad_terms = pair_terms(block, source)
        return (carry[0] + out_spec, carry[1] + grad_terms)

    start = (
        jnp.zeros((channels, 2 * block_len), jnp.float32),
        jnp.zeros((channels, 2 * modes), jnp.float32),
    )
    totals = process(start, gated, own_index)

    def loop_step(step, carry):
        moved = from_behind(carry[2], "ctx", 1)
        source = (own_index - step) % blocks
        summed = process((carry[0], carry[1]), moved, source)
        return (summed[0], summed[1], moved)

    result = lax.fori_loop(1, blocks, loop_step, (totals[0], totals[1], gated))
    totals = (result[0], result[1])
    conv = jnp.dot(totals[0], inverse, precision=HIGHEST)
    mixed = (queries * (conv + skip_gain[:, None] * gated_f)).astype(jnp.bfloat16)[None]
    grad_part = totals[1][:, :modes]
    rate_part = jnp.sum(residue * totals[1][:, modes:], axis=0)
    grad_residue, grad_rate = lax.psum((grad_part, rate_part), ("ctx", "dp"))
    return (mixed, grad_residue, grad_rate)


def solution(mesh):
    return jax.shard_map(
        per_device,
        mesh=mesh,
        in_specs=(P("dp", "ctx"), P(), P(), P(), P(), P(), P("dp", None, "ctx")),
        out_specs=(P("dp", None, "ctx"), P(), P()),
        check_vma=False,
    )
```

profile of v0, /device:TPU:0, one launch (start us, length us, event | category | flops | bytes accessed | tf_op | source)
XLA Modules:
  0.0 196.3 jit_solution(18297518088232909008)
XLA Ops:
  7.2 1.4 slice_bitcast_fusion
  12.8 2.1 %fusion.108 = (f32[3072,1]{0,1:T(1,128)S(1)}, f32[3072,1]{0,1:T(1,128)}, f32[3072,1]{0,1:T(1,128)}, f32[3072,1]{0,1:T(1,128)}, f32[3072,1]{0,1:T(1,128)}, /*index=5*/f32[3072,1]{0,1:T(1,128)}, f32[3072,1]{0,1:T(1,128)}) fusion(f32[3072,7]{0,1:T(8,128)} %param.11), kind=kLoop, calls=%fused_computation.185 | loop fusion | bytes 172032 | tf_op jit(solution)/shard_map/slice | solution.py:86
  14.9 1.8 copy.10
  16.8 1.2 convolution_bitcast_fusion.1
  18.4 2.0 %convolution_bitcast_fusion.3 = f32[1024,256]{0,1:T(8,128)} fusion(f32[1024,16]{0,1:T(8,128)S(1)} %copy-done.9, f32[32,256]{1,0:T(8,128)S(1)} %fusion.79), kind=kOutput, calls=%fused_computation.74 | convolution fusion | flops 50331648 | bytes 1130496 | tf_op jit(solution)/shard_map/dot_general | solution.py:114
  20.4 1.0 cosine_multiply_fusion
  21.5 1.5 convolution_bitcast_fusion.2
  23.1 1.4 fusion.30
  24.5 1.2 copy-done.5
  26.6 1.2 fusion.110
  27.8 2.1 %fusion.50 = f32[1024,256]{0,1:T(8,128)S(1)} fusion(f32[3072,128]{0,1:T(8,128)} %copy-done.5, bf16[1,1024,128]{1,2,0:T(8,128)(2,1)} %copy.10, f32[256,128]{1,0:T(8,128)} %copy-done.8, f32[256,128]{1,0:T(8,128)S(1)} %get-tuple-element.482), kind=kOutput, calls=%fused_computation.90 | convolution fusion | flops 402948096 | bytes 2097152 | tf_op jit(solution)/shard_map/dot_general | solution.py:95
  30.3 1.2 copy-done.7
  32.2 1.1 pad_maximum_fusion.1
  34.1 32.5 %while.21 = (s32[]{:T(128)}, f32[1024,256]{0,1:T(8,128)}, f32[1024,32]{0,1:T(8,128)S(1)}, bf16[1024,128]{1,0:T(8,128)(2,1)}, f32[16,1]{0,1:T(1,128)S(1)}, /*inde...) while((s32[]{:T(128)}, f32[1024,256]{0,1:T(8,128)}, ...), condition=%wide.region_1.2_spmd.clone, body=%wide.region_0.1_spmd.clone.sunk | while | flops 313890176 | bytes 29451272 | solution.py:136
  34.1 2.7 %collective-permute-start = (bf16[1024,128]{1,0:T(8,128)(2,1)}, bf16[1024,128]{1,0:T(8,128)(2,1)S(1)}, u32[]{:S(2)}, u32[]{:S(2)}) collective-permute-start(bf16[1024,128]{1,0:T(8,128)(2,1)} %get-tuple-element.591), channel_id=1, source_target_pairs={{24,0},{0,8},{8,16},{16,24},{25,1},{1,9},{9,17},{17,25},{26,2},{2,... | collective-permute-start | bytes 786440 | tf_op jit(solution)/shard_map/while/body/eval_jaxpr/ppermute | solution.py:14
  37.0 1.2 fusion.151
  38.2 1.9 convolution_bitcast_fusion.5
  40.4 1.3 fusion.149
  45.4 1.2 fusion.151
  46.6 1.9 convolution_bitcast_fusion.5
  48.5 2.7 %collective-permute-done = bf16[1024,128]{1,0:T(8,128)(2,1)S(1)} collective-permute-done((bf16[1024,128]{1,0:T(8,128)(2,1)}, bf16[1024,128]{1,0:T(8,128)(2,1)S(1)}, u32[]{:S(2)}, u32[]{:S(2)}) %collective-permute-start) | collective-permute-done | bytes 262176 | tf_op jit(solution)/shard_map/while/body/eval_jaxpr/ppermute | solution.py:14
  51.1 1.3 fusion.149
  54.3 0.9 convolution_add_fusion.7
  56.1 1.2 fusion.151
  57.3 1.9 convolution_bitcast_fusion.5
  59.2 2.7 %collective-permute-done = bf16[1024,128]{1,0:T(8,128)(2,1)S(1)} collective-permute-done((bf16[1024,128]{1,0:T(8,128)(2,1)}, bf16[1024,128]{1,0:T(8,128)(2,1)S(1)}, u32[]{:S(2)}, u32[]{:S(2)}) %collective-permute-start) | collective-permute-done | bytes 262176 | tf_op jit(solution)/shard_map/while/body/eval_jaxpr/ppermute | solution.py:14
  61.9 1.3 fusion.149
  66.6 1.6 multiply_reduce_fusion
  68.3 2.2 %fusion.45 = bf16[1,1024,128]{1,2,0:T(8,128)(2,1)S(1)} fusion(f32[1024,256]{0,1:T(8,128)} %get-tuple-element.385, bf16[1024,128]{0,1:T(8,128)(2,1)} %copy-done.6, f32[3072,128]{0,1:T(8,128)} %copy-done.5, f32[1024]{0:T(1024)S(1)} %copy-done.23, f32[128,128]{1,0:T(8,128)} %get-tuple-element.479, f32[128,128]{1,0:T(8,128)} %get-tuple-element.478), kind=kOutput, calls=%fused_computation.79 | convolution fusion | flops 403341312 | bytes 2232320 | tf_op jit(solution)/shard_map/dot_general | solution.py:138
  70.5 41.4 %psum.15 = f32[16]{0:T(128)} all-reduce(f32[16]{0:T(128)S(1)} %get-tuple-element.467), channel_id=1, replica_groups=mesh['ctx'=4,'dp'=8] {'ctx','dp'}, use_global_device_ids=true, to_apply=%region_4.5 | all-reduce | flops 16 | bytes 128 | tf_op jit(solution)/shard_map/psum | solution.py:142
  112.7 75.3 %all-reduce.2.cloned.1.call-done = f32[1024,16]{0,1:T(8,128)} async-done(((f32[1024,16]{0,1:T(8,128)}), f32[1024,16]{0,1:T(8,128)}) %all-reduce.2.cloned.1.call-update) | async-done | bytes 65552 | tf_op jit(solution)/shard_map/psum | solution.py:142
  188.0 1.5 copy.28
  (133 shorter events, 18.7 us)
Async XLA Ops:
  7.2 9.6 %copy-start = (bf16[3072,512]{1,0:T(8,128)(2,1)S(1)}, bf16[3072,512]{1,0:T(8,128)(2,1)}, u32[]{:S(2)}) copy-start(bf16[3072,512]{1,0:T(8,128)(2,1)} %param.10) | copy-start | bytes 9437188
  7.2 9.6 %copy-start.25 = (s32[1,128]{1,0:T(1,128)S(1)}, s32[1,128]{1,0:T(1,128)}, u32[]{:S(2)}) copy-start(s32[1,128]{1,0:T(1,128)} %param.9) | copy-start | bytes 1540
  7.2 9.6 %copy-start.29 = (f32[16]{0:T(128)S(1)}, f32[16]{0:T(128)}, u32[]{:S(2)}) copy-start(f32[16]{0:T(128)} %param.13) | copy-start | bytes 196
  7.2 180.8 %all-reduce.2.cloned.1.call-start = ((), (), s32[]{:S(2)}) async-start(), calls=%async_computation | async-start | bytes 131072 | tf_op jit(solution)/shard_map/psum | solution.py:142
  8.6 12.8 %collective-permute-start.1 = (s32[6]{0:T(128)}, s32[6]{0:T(128)}, u32[]{:S(2)}, u32[]{:S(2)}) collective-permute-start(s32[6]{0:T(128)} %slice_bitcast_fusion), channel_id=1, source_target_pairs={{24,0},{0,8},{8,16},{16,24},{25,1},{1,9},{9,17},{17,25},{26,2},{2,... | collective-permute-start | bytes 80 | tf_op jit(solution)/shard_map/ppermute | solution.py:14
  9.1 7.7 %copy-start.20 = (pred[128]{0:T(512)(128)(4,1)}, pred[128]{0:T(512)(128)(4,1)S(1)}, u32[]{:S(2)}) copy-start(pred[128]{0:T(512)(128)(4,1)S(1)} %iota_compare_fusion.3) | copy-start | bytes 388
  10.3 7.9 %copy-start.8 = (f32[256,128]{1,0:T(8,128)}, f32[256,128]{1,0:T(8,128)S(1)}, u32[]{:S(2)}) copy-start(f32[256,128]{1,0:T(8,128)S(1)} %get-tuple-element.483) | copy-start | bytes 393220
  16.8 1.6 copy-start.9
  16.8 3.7 %copy-start.21 = (pred[128]{0:T(512)(128)(4,1)S(1)}, pred[128]{0:T(512)(128)(4,1)}, u32[]{:S(2)}) copy-start(pred[128]{0:T(512)(128)(4,1)} %copy-done.20) | copy-start | bytes 388
  16.8 3.6 %copy-start.26 = (f32[128]{0:T(128)S(1)}, f32[128]{0:T(128)}, u32[]{:S(2)}) copy-start(f32[128]{0:T(128)} %get-tuple-element.486) | copy-start | bytes 1540
  16.8 3.6 %copy-start.27 = (f32[128]{0:T(128)S(1)}, f32[128]{0:T(128)}, u32[]{:S(2)}) copy-start(f32[128]{0:T(128)} %get-tuple-element.487) | copy-start | bytes 1540
  16.8 3.6 %copy-start.28 = (s32[128]{0:T(128)S(1)}, s32[128]{0:T(128)}, u32[]{:S(2)}) copy-start(s32[128]{0:T(128)} %iota_add_fusion.1) | copy-start | bytes 1540
  18.4 4.6 %copy-start.12 = (f32[32,256]{1,0:T(8,128)}, f32[32,256]{1,0:T(8,128)S(1)}, u32[]{:S(2)}) copy-start(f32[32,256]{1,0:T(8,128)S(1)} %fusion.79) | copy-start | bytes 98308
  21.4 1.6 copy-start.16
  21.4 1.6 copy-start.17
  21.4 1.6 copy-start.18
  21.4 1.6 copy-start.19
  25.7 4.3 %copy-start.6 = (bf16[1024,128]{0,1:T(8,128)(2,1)}, bf16[1024,128]{0,1:T(8,128)(2,1)S(1)}, u32[]{:S(2)}) copy-start(bf16[1024,128]{0,1:T(8,128)(2,1)S(1)} %fusion.49) | copy-start | bytes 786436
  26.6 3.4 %copy-start.11 = (bf16[128,256]{1,0:T(8,128)(2,1)S(1)}, bf16[128,256]{1,0:T(8,128)(2,1)}, u32[]{:S(2)}) copy-start(bf16[128,256]{1,0:T(8,128)(2,1)} %get-tuple-element.580) | copy-start | bytes 196612
  29.9 2.2 %copy-start.3 = (f32[1024,256]{0,1:T(8,128)}, f32[1024,256]{0,1:T(8,128)S(1)}, u32[]{:S(2)}) copy-start(f32[1024,256]{0,1:T(8,128)S(1)} %fusion.50) | copy-start | bytes 3145732
  34.1 34.2 %copy-start.23 = (f32[1024]{0:T(1024)S(1)}, f32[1024]{0:T(1024)}, u32[]{:S(2)}) copy-start(f32[1024]{0:T(1024)} %param.14) | copy-start | bytes 12292
  34.1 6.3 %collective-permute-start = (bf16[1024,128]{1,0:T(8,128)(2,1)}, bf16[1024,128]{1,0:T(8,128)(2,1)S(1)}, u32[]{:S(2)}, u32[]{:S(2)}) collective-permute-start(bf16[1024,128]{1,0:T(8,128)(2,1)} %get-tuple-element.591), channel_id=1, source_target_pairs={{24,0},{0,8},{8,16},{16,24},{25,1},{1,9},{9,17},{17,25},{26,2},{2,... | collective-permute-start | bytes 786440 | tf_op jit(solution)/shard_map/while/body/eval_jaxpr/ppermute | solution.py:14
  36.8 4.9 %copy-start.10 = (bf16[128,256]{1,0:T(8,128)(2,1)S(1)}, bf16[128,256]{1,0:T(8,128)(2,1)}, u32[]{:S(2)}) copy-start(bf16[128,256]{1,0:T(8,128)(2,1)} %get-tuple-element.613) | copy-start | bytes 196612 | tf_op jit(solution)/shard_map/while
  40.4 1.6 copy-start.4
  45.1 6.0 %collective-permute-start = (bf16[1024,128]{1,0:T(8,128)(2,1)}, bf16[1024,128]{1,0:T(8,128)(2,1)S(1)}, u32[]{:S(2)}, u32[]{:S(2)}) collective-permute-start(bf16[1024,128]{1,0:T(8,128)(2,1)} %get-tuple-element.591), channel_id=1, source_target_pairs={{24,0},{0,8},{8,16},{16,24},{25,1},{1,9},{9,17},{17,25},{26,2},{2,... | collective-permute-start | bytes 786440 | tf_op jit(solution)/shard_map/while/body/eval_jaxpr/ppermute | solution.py:14
  45.2 7.2 %copy-start.10 = (bf16[128,256]{1,0:T(8,128)(2,1)S(1)}, bf16[128,256]{1,0:T(8,128)(2,1)}, u32[]{:S(2)}) copy-start(bf16[128,256]{1,0:T(8,128)(2,1)} %get-tuple-element.613) | copy-start | bytes 196612 | tf_op jit(solution)/shard_map/while
  51.1 1.6 copy-start.4
  54.3 1.6 copy-start.2
  55.9 6.0 %collective-permute-start = (bf16[1024,128]{1,0:T(8,128)(2,1)}, bf16[1024,128]{1,0:T(8,128)(2,1)S(1)}, u32[]{:S(2)}, u32[]{:S(2)}) collective-permute-start(bf16[1024,128]{1,0:T(8,128)(2,1)} %get-tuple-element.591), channel_id=1, source_target_pairs={{24,0},{0,8},{8,16},{16,24},{25,1},{1,9},{9,17},{17,25},{26,2},{2,... | collective-permute-start | bytes 786440 | tf_op jit(solution)/shard_map/while/body/eval_jaxpr/ppermute | solution.py:14
  55.9 7.2 %copy-start.10 = (bf16[128,256]{1,0:T(8,128)(2,1)S(1)}, bf16[128,256]{1,0:T(8,128)(2,1)}, u32[]{:S(2)}) copy-start(bf16[128,256]{1,0:T(8,128)(2,1)} %get-tuple-element.613) | copy-start | bytes 196612 | tf_op jit(solution)/shard_map/while
  61.9 1.6 copy-start.4
  65.0 1.6 copy-start.2
  (11 other events, 15.0 us)
Sparse Core Ops, SparseCore 0:
  68.4 119.5 all-reduce.1
where the time goes:
time: 198 us; the launch traced here: 196 us
  waiting for transfers between devices  81 us (41%)
  blocking collectives  41.4 us (21%)
  matrix products  28.2 us (14%)
  local copies, waits for them, and re-layouts  15.1 us (8%)
  between operations  14.4 us (7%)
  other arithmetic  12.7 us (6%)
  starting transfers between devices  3.23 us (2%)
    psum x1, waiting for transfers between devices, per_device(): grad_residue, grad_rate = lax.psum((grad_part, rate_part), ('ctx', 'dp'))  75.3 us
    psum x1, blocking collectives, per_device(): grad_residue, grad_rate = lax.psum((grad_part, rate_part), ('ctx', 'dp'))  41.4 us
    dot_general x4, matrix products, pair_terms(): filt_spec = jnp.dot(residue, spectra[:modes], precision=HIGHEST)  7.6 us
    unnamed x56, local copies, waits for them, and re-layouts  7.5 us
    ppermute x4, waiting for transfers between devices, from_behind(): return lax.ppermute(block, axis, route)  5.7 us
    dot_general x4, matrix products, split_dot(): jnp.dot(data, halves[1], preferred_element_type=jnp.float32)  4.12 us
    while x27, local copies, waits for them, and re-layouts  4.09 us
  transfers between devices with their start and end apart: 5, of which 4 were waited for; matrix products, arithmetic and copies ran while one was open for 13% of the time, Pallas kernels for 0%

commit v1 on v0

v1 whole, which is shorter than its diff:
```python
import functools
import math

import jax
import jax.numpy as jnp
import numpy as np
from jax import lax
from jax.experimental import pallas as pl
from jax.experimental.pallas import tpu as pltpu
from jax.sharding import PartitionSpec as P

F32 = jnp.float32
BF16 = jnp.bfloat16
GROUP = 256
HALO = 8
LANES = 128


def xor_permute(block, axis, mask):
    return lax.ppermute(block, axis, [(i, i ^ mask) for i in range(lax.axis_size(axis))])


def masks_of(size):
    return [1 << bit for bit in range(size.bit_length() - 1)]


def halves(table):
    upper = table.astype(BF16)
    return upper, (table - upper.astype(F32)).astype(BF16)


def dot(left, right):
    return jnp.dot(left, right, preferred_element_type=F32)


def dft_tables(block_len):
    period = 2 * block_len
    column = np.arange(block_len)[:, None]
    sample = np.arange(period)[None, :]
    angle = (column * sample % period) * (2.0 * math.pi / period)
    parity = 1.0 - 2.0 * (sample % 2)
    imag = np.where(column == 0, parity, -np.sin(angle))
    forward = np.concatenate([np.cos(angle), imag], axis=0)
    weight = np.where(np.arange(period) % block_len == 0, 1.0, 2.0) / period
    inverse = (forward[:, :block_len] * weight[:, None]).T
    return forward, inverse, weight


def np_halves(table):
    upper = table.astype(np.float32).astype(jnp.bfloat16)
    lower = (table - upper.astype(np.float64)).astype(np.float32).astype(jnp.bfloat16)
    return upper, lower


def mode_constants(block_len, seq_len, modes):
    near = np.arange(2 * block_len)
    near = np.where(near < block_len, near, seq_len - 2 * block_len + near)
    far = seq_len - block_len - np.arange(seq_len - block_len)
    here = np.arange(block_len)
    delay = np.concatenate([near, far, here])[:, None]
    period = 2 * modes + 2
    angle = (delay * (np.arange(modes)[None, :] + 1) % period) * (2.0 * math.pi / period)
    ratio = delay / seq_len
    parts = [np.cos(angle), np.sin(angle), -ratio * np.cos(angle), -ratio * np.sin(angle)]
    wave = np.concatenate(parts, axis=1)
    wave = np.pad(wave, ((0, 0), (0, LANES - wave.shape[1])))
    return wave.astype(np.float32), (-ratio).astype(np.float32)


def tables_kernel(modes, block_len, seq_len, rates_ref, wave_ref, ratio_ref, fwd_ref, weight_ref, res_ref, grad_ref,
                  far_ref, here_ref, here_t_ref, near_ref, filt_ref, grad_t_ref, rate_row):
    rate_row[...] = jnp.zeros_like(rate_row)
    rate_row[:, :modes] = rates_ref[...]
    rates = rate_row[...]
    for shift in (modes, 2 * modes):
        rates = rates + pltpu.roll(rates, shift, 1)
    table = jnp.exp(ratio_ref[...] * rates) * wave_ref[...]
    near = table[: 2 * block_len]
    far = table[2 * block_len : 2 * block_len + seq_len - block_len]
    here = table[2 * block_len + seq_len - block_len :]
    used = 4 * modes
    far_t = halves(far.T[:used])
    far_ref[...] = jnp.concatenate(far_t, axis=0)
    here_t = halves(here.T[:used])
    here_ref[...] = jnp.concatenate(here_t, axis=0)
    here_t_ref[...] = here
    near_hi, near_lo = halves(near)
    fwd = fwd_ref[...]
    fwd_hi = fwd[: 2 * block_len]
    fwd_lo = fwd[2 * block_len :]
    spec = dot(fwd_hi, near_hi) + dot(fwd_hi, near_lo) + dot(fwd_lo, near_hi)
    spec_t = (spec * weight_ref[...]).T
    grad_rows = jnp.concatenate([spec_t[:modes], spec_t[2 * modes : 3 * modes]], axis=0)
    near_ref[...] = jnp.concatenate(halves(grad_rows), axis=0)
    spec_hi, spec_lo = halves(spec[:, :modes])
    res_hi, res_lo = halves(res_ref[...])
    filt_ref[...] = dot(spec_hi, res_hi) + dot(spec_hi, res_lo) + dot(spec_lo, res_hi)
    grad_t_ref[...] = grad_ref[...].astype(F32).T


def main_kernel(modes, blocks, block_len, taps, channels, ids_ref, table_ref, short_ref, res_ref, fwd_ref, far_ref,
                here_ref, near_ref, grad_t_ref, part_ref, query_ref, gated_ref, spec_ref, state_ref,
                onehot, feat_k, feat_v, feat_q):
    seq_len = blocks * block_len
    vocab = table_ref.shape[1]
    own = lax.axis_index("ctx")
    for place in range(blocks):
        source = lax.rem(own + 1 + place, blocks)
        row = ids_ref[pl.ds(source ^ own, 1), :]
        column = jnp.broadcast_to(row, (block_len, block_len)).T
        lane = lax.broadcasted_iota(jnp.int32, (block_len, block_len), 1)
        for piece in range(vocab // block_len):
            match = column == lane + piece * block_len
            onehot[pl.ds(place * block_len, block_len), pl.ds(piece * block_len, block_len)] = jnp.where(
                match, 1.0, 0.0
            ).astype(BF16)
    hot = onehot[...]
    first = HALO - (taps - 1)
    body = seq_len - block_len
    period = 2 * block_len
    rate = jnp.zeros((modes, 1), F32)
    groups = channels // GROUP

    def gather(rows, hot):
        block = table_ref[pl.ds(rows, GROUP), :]
        return lax.dot_general(hot, block, (((1,), (1,)), ((), ())), preferred_element_type=F32)

    def short_conv(feat, rows, length, side):
        total = None
        for tap in range(taps):
            weight = short_ref[tap : tap + 1, pl.ds(rows + side * LANES, LANES)]
            term = weight * feat[side, pl.ds(first + tap, length), :]
            total = term if total is None else total + term
        return total

    def one_group(base, rate):
        for feat, offset in ((feat_k, channels), (feat_v, 2 * channels)):
            values = gather(offset + base, hot)
            for side in range(GROUP // LANES):
                cols = values[:, side * LANES : (side + 1) * LANES]
                feat[side, HALO:, :] = cols
                feat[side, :HALO, :] = cols[seq_len - HALO :]
        values = gather(base, hot[body - HALO if blocks > 1 else 0 :])
        for side in range(GROUP // LANES):
            feat_q[side, :, :] = values[:, side * LANES : (side + 1) * LANES]
        gated = []
        query = []
        for side in range(GROUP // LANES):
            keys = short_conv(feat_k, channels + base, seq_len, side)
            vals = short_conv(feat_v, 2 * channels + base, seq_len, side)
            gated.append((keys * vals).astype(BF16))
            query.append(short_conv(feat_q, base, block_len, side))
        gated = jnp.concatenate(gated, axis=1)
        query = jnp.concatenate(query, axis=1)
        span = pl.ds(base, GROUP)
        query_ref[:, span] = query
        gated_own = gated[body:]
        gated_ref[:, span] = gated_own
        dconv = query * grad_t_ref[:, span]
        dconv_both = jnp.concatenate(halves(dconv), axis=0)
        spec = dot(fwd_ref[...], gated_own)
        spec = spec[:period] + spec[period:]
        spec_ref[:, span] = spec
        left = jnp.concatenate([fwd_ref[...], here_ref[...]], axis=0)
        dspec = dot(jnp.concatenate([left, left], axis=1), dconv_both)
        dstate = dspec[2 * period :]
        dspec = dspec[:period] + dspec[period : 2 * period]
        dstate = dstate[: 4 * modes] + dstate[4 * modes :]
        state = dot(far_ref[...], gated[:body])
        state = state[: 4 * modes] + state[4 * modes :]
        left_re, left_im = spec[:block_len], spec[block_len:]
        right_re, right_im = dspec[:block_len], dspec[block_len:]
        leading = lax.broadcasted_iota(jnp.int32, (block_len, GROUP), 0) == 0
        rere, imim = left_re * right_re, left_im * right_im
        cross_re = jnp.where(leading, rere, rere + imim)
        cross_im = jnp.where(leading, imim, left_re * right_im - left_im * right_re)
        cross = jnp.concatenate([cross_re, cross_im], axis=0)
        cross_hi, cross_lo = halves(cross)
        near = near_ref[...]
        terms = dot(near, cross_hi) + dot(near, cross_lo)
        terms = terms[: 2 * modes] + terms[2 * modes :]
        sc, ss, sc1, ss1 = (state[i * modes : (i + 1) * modes] for i in range(4))
        dc, ds, dc1, ds1 = (dstate[i * modes : (i + 1) * modes] for i in range(4))
        grad = terms[:modes] + dc * sc - ds * ss
        slope = terms[modes:] + dc1 * sc + dc * sc1 - ds1 * ss - ds * ss1
        res = res_ref[:, span]
        state_ref[:modes, span] = res * sc
        state_ref[modes:, span] = -(res * ss)
        for side in range(GROUP // LANES):
            at = (base + side * LANES) // LANES * modes
            part_ref[pl.ds(at, modes), :] = grad[:, side * LANES : (side + 1) * LANES]
        return rate + jnp.sum(res * slope, axis=1, keepdims=True)

    if blocks <= 4:
        for group in range(groups):
            rate = one_group(group * GROUP, rate)
    else:
        rate = lax.fori_loop(0, groups, lambda g, r: one_group(pl.multiple_of(g * GROUP, GROUP), r), rate)
    wide = jnp.broadcast_to(rate, (modes, LANES))
    square = jnp.concatenate([wide, jnp.zeros((LANES - modes, LANES), F32)], axis=0).T
    part_ref[pl.ds(channels // LANES * modes, 8), :] = square[:8]


def mixed_kernel(modes, block_len, query_ref, gated_ref, spec_ref, filt_ref, state_ref, here_t_ref, inv_ref, skip_ref,
                 out_ref):
    channels = query_ref.shape[1]
    period = 2 * block_len
    leading = lax.broadcasted_iota(jnp.int32, (block_len, GROUP), 0) == 0
    inv = inv_ref[...]
    inv_hi, inv_lo = inv[:block_len], inv[block_len:]
    here_hi, here_lo = halves(here_t_ref[:, : 2 * modes])
    for base in range(0, channels, GROUP):
        span = pl.ds(base, GROUP)
        left_re, left_im = filt_ref[:block_len, span], filt_ref[block_len:, span]
        right_re, right_im = spec_ref[:block_len, span], spec_ref[block_len:, span]
        rere, imim = left_re * right_re, left_im * right_im
        out_re = jnp.where(leading, rere, rere - imim)
        out_im = jnp.where(leading, imim, left_re * right_im + left_im * right_re)
        prod_hi, prod_lo = halves(jnp.concatenate([out_re, out_im], axis=0))
        conv = dot(inv_hi, prod_hi) + dot(inv_hi, prod_lo) + dot(inv_lo, prod_hi)
        state_hi, state_lo = halves(state_ref[:, span])
        conv = conv + dot(here_hi, state_hi) + dot(here_hi, state_lo) + dot(here_lo, state_hi)
        mixed = query_ref[:, span] * (conv + skip_ref[:, span] * gated_ref[:, span].astype(F32))
        out_ref[pl.ds(base, GROUP), :] = mixed.T.astype(BF16)


def vmem_call(kernel, outs, scratch, args, flops, moved):
    return pl.pallas_call(
        kernel,
        out_shape=[jax.ShapeDtypeStruct(shape, dtype) for shape, dtype in outs],
        in_specs=[pl.BlockSpec(memory_space=pltpu.VMEM)] * len(args),
        out_specs=[pl.BlockSpec(memory_space=pltpu.VMEM)] * len(outs),
        scratch_shapes=scratch,
        compiler_params=pltpu.CompilerParams(vmem_limit_bytes=40 * 1024 * 1024),
        cost_estimate=pl.CostEstimate(flops=flops, bytes_accessed=moved, transcendentals=0),
    )(*args)


def per_device(token_ids, feature_table, short_weight, residue, rates, skip_gain, grad_out):
    block_len = token_ids.shape[1]
    blocks = lax.axis_size("ctx")
    seq_len = block_len * blocks
    channels, modes = residue.shape
    taps = short_weight.shape[1]
    vocab = feature_table.shape[1]
    period = 2 * block_len
    forward, inverse, weight = dft_tables(block_len)
    fwd_hi, fwd_lo = np_halves(forward)
    fwd_all = np.concatenate([fwd_hi, fwd_lo], axis=0)
    inv_all = np.concatenate(np_halves(inverse), axis=0)
    wave, ratio = mode_constants(block_len, seq_len, modes)
    res_t = residue.T

    ids = token_ids
    for mask in masks_of(blocks):
        ids = jnp.concatenate([ids, xor_permute(ids, "ctx", mask)], axis=0)

    far, here, here_t, near, filt, grad_t = vmem_call(
        functools.partial(tables_kernel, modes, block_len, seq_len),
        [
            ((8 * modes, seq_len - block_len), BF16),
            ((8 * modes, block_len), BF16),
            ((block_len, LANES), F32),
            ((4 * modes, period), BF16),
            ((period, channels), F32),
            ((block_len, channels), F32),
        ],
        [pltpu.VMEM((1, LANES), F32)],
        [
            rates[None],
            jnp.asarray(wave),
            jnp.asarray(ratio),
            jnp.asarray(fwd_all),
            jnp.asarray(weight[:, None].astype(np.float32)),
            res_t,
            grad_out[0],
        ],
        100_000_000,
        2_000_000,
    )
    part, query, gated, spec, state = vmem_call(
        functools.partial(main_kernel, modes, blocks, block_len, taps, channels),
        [
            ((channels // LANES * modes + 8, LANES), F32),
            ((block_len, channels), F32),
            ((block_len, channels), BF16),
            ((period, channels), F32),
            ((2 * modes, channels), F32),
        ],
        [
            pltpu.VMEM((seq_len, vocab), BF16),
            pltpu.VMEM((GROUP // LANES, seq_len + HALO, LANES), F32),
            pltpu.VMEM((GROUP // LANES, seq_len + HALO, LANES), F32),
            pltpu.VMEM((GROUP // LANES, block_len + HALO, LANES), F32),
        ],
        [
            ids,
            feature_table,
            short_weight.T,
            res_t,
            jnp.asarray(fwd_all[:, :block_len]),
            far,
            here,
            near,
            grad_t,
        ],
        2 * seq_len * vocab * 3 * channels,
        6_000_000,
    )
    (mixed,) = vmem_call(
        functools.partial(mixed_kernel, modes, block_len),
        [((channels, block_len), BF16)],
        [],
        [query, gated, spec, filt, state, here_t, jnp.asarray(inv_all), skip_gain[None]],
        300_000_000,
        3_000_000,
    )
    for axis in ("ctx", "dp"):
        for mask in masks_of(lax.axis_size(axis)):
            part = part + xor_permute(part, axis, mask)
    rows = channels // LANES * modes
    grad_res = part[:rows].reshape(channels // LANES, modes, LANES).transpose(0, 2, 1).reshape(channels, modes)
    return (mixed[None], grad_res, part[rows, :modes])


def solution(mesh):
    return jax.shard_map(
        per_device,
        mesh=mesh,
        in_specs=(P("dp", "ctx"), P(), P(), P(), P(), P(), P("dp", None, "ctx")),
        out_specs=(P("dp", None, "ctx"), P(), P()),
        check_vma=False,
    )
```

time: 198 us -> 45.6 us (0.23)
  waiting for transfers between devices: 81 us -> 13.6 us
  blocking collectives: 41.4 us -> 0 us
  matrix products: 28.2 us -> 0 us
  between operations: 14.4 us -> 0.69 us
  other arithmetic: 12.7 us -> 1.38 us
  Pallas kernels: 0 us -> 7.47 us
  starting transfers between devices: 3.23 us -> 10 us
  local copies, waits for them, and re-layouts: 15.1 us -> 12 us
    psum x1 -> x0, waiting for transfers between devices: 75.3 us -> none  [per_device(): grad_residue, grad_rate = lax.psum((grad_part, rate_part), ('ctx', 'dp'))]
    psum x1 -> x0, blocking collectives: 41.4 us -> none  [per_device(): grad_residue, grad_rate = lax.psum((grad_part, rate_part), ('ctx', 'dp'))]
    dot_general x24 -> x0, matrix products: 28.2 us -> none  [the longest x4 7.6 us: pair_terms(): filt_spec = jnp.dot(residue, spectra[:modes], precision=HIGHEST)]
    ppermute x4 -> x7, waiting for transfers between devices: 5.7 us -> 13.6 us  [xor_permute(): lax.ppermute(block, axis, [(i, i ^ mask) for i in range(lax.axis_size(axi...]
    pallas_call x0 -> x3, Pallas kernels: none -> 7.47 us  [vmem_call(): pl.pallas_call(kernel, out_shape=[jax.ShapeDtypeStruct(shape, dtype) for...]
    ppermute x4 -> x7, starting transfers between devices: 3.19 us -> 10 us  [xor_permute(): lax.ppermute(block, axis, [(i, i ^ mask) for i in range(lax.axis_size(axi...]
    while x27 -> x0, local copies, waits for them, and re-layouts: 4.09 us -> none
    slice x2 -> x1, local copies, waits for them, and re-layouts: 3.49 us -> 0.01 us  [per_device(): part[:rows].reshape(channels // LANES, modes, LANES).transpose(0, 2, 1)]
  transfers between devices with their start and end apart: 5 -> 7, of which waited for: 4 -> 6; matrix products, arithmetic and copies ran while one was open for 13% -> 0% of each run, Pallas kernels for 0% -> 5%
where the time goes in v1:
time: 45.6 us; the launch traced here: 45.1 us
  waiting for transfers between devices  13.6 us (30%)
  local copies, waits for them, and re-layouts  12 us (26%)
  starting transfers between devices  10 us (22%)
  Pallas kernels  7.47 us (16%)
  other arithmetic  1.38 us (3%)
  between operations  0.69 us (2%)
    ppermute x7, waiting for transfers between devices, xor_permute(): lax.ppermute(block, axis, [(i, i ^ mask) for i in range(lax.axis_size(axi...  13.6 us
    unnamed x26, local copies, waits for them, and re-layouts  10.8 us
    ppermute x7, starting transfers between devices, xor_permute(): lax.ppermute(block, axis, [(i, i ^ mask) for i in range(lax.axis_size(axi...  10 us
    pallas_call x3, Pallas kernels, vmem_call(): pl.pallas_call(kernel, out_shape=[jax.ShapeDtypeStruct(shape, dtype) for...  7.47 us
    concatenate x2, other arithmetic, per_device(): ids = jnp.concatenate([ids, xor_permute(ids, 'ctx', mask)], axis=0)  1.33 us
  transfers between devices with their start and end apart: 7, of which 6 were waited for; matrix products, arithmetic and copies ran while one was open for 0% of the time, Pallas kernels for 5%

profile of v1, /device:TPU:0, one launch (start us, length us, event | category | flops | bytes accessed | tf_op | source)
XLA Modules:
  0.0 45.1 jit_solution(12817826274864294436)
XLA Ops:
  0.6 0.5 %collective-permute-start = (s32[1,128]{1,0:T(1,128)}, s32[1,128]{1,0:T(1,128)S(1)}, u32[]{:S(2)}, u32[]{:S(2)}) collective-permute-start(s32[1,128]{1,0:T(1,128)} %param.13), channel_id=1, source_target_pairs={{0,8},{8,0},{16,24},{24,16},{1,9},{9,1},{17,25},{25,17},{2,10},{10... | collective-permute-start | bytes 1544 | tf_op jit(solution)/shard_map/ppermute | solution.py:20
  1.1 1.0 %collective-permute-done = s32[1,128]{1,0:T(1,128)S(1)} collective-permute-done((s32[1,128]{1,0:T(1,128)}, s32[1,128]{1,0:T(1,128)S(1)}, u32[]{:S(2)}, u32[]{:S(2)}) %collective-permute-start) | collective-permute-done | bytes 544 | tf_op jit(solution)/shard_map/ppermute | solution.py:20
  2.1 0.7 %pad_add_fusion.1 = s32[2,128]{1,0:T(2,128)S(1)} fusion(s32[1,128]{1,0:T(1,128)S(1)} %collective-permute-done, s32[1,128]{1,0:T(1,128)} %param.13), kind=kLoop, calls=%fused_computation.2 | loop fusion | flops 256 | bytes 2048 | tf_op jit(solution)/shard_map/concatenate | solution.py:256
  2.8 2.8 %collective-permute-start.1 = (s32[2,128]{1,0:T(2,128)S(1)}, s32[2,128]{1,0:T(2,128)S(1)}, u32[]{:S(2)}, u32[]{:S(2)}) collective-permute-start(s32[2,128]{1,0:T(2,128)S(1)} %pad_add_fusion.1), channel_id=1, source_target_pairs={{0,16},{8,24},{16,0},{24,8},{1,17},{9,25},{17,1},{25,9},{2,18},{10... | collective-permute-start | bytes 3080 | tf_op jit(solution)/shard_map/ppermute | solution.py:20
  5.6 1.0 %copy-done = f32[768,1]{1,0:T(8,128)S(1)} copy-done((f32[768,1]{1,0:T(8,128)S(1)}, f32[768,1]{1,0:T(8,128)}, u32[]{:S(2)}) %copy-start) | copy-done | bytes 3096
  6.6 1.0 %copy-done.1 = f32[768,128]{1,0:T(8,128)S(1)} copy-done((f32[768,128]{1,0:T(8,128)S(1)}, f32[768,128]{1,0:T(8,128)}, u32[]{:S(2)}) %copy-start.1) | copy-done | bytes 393240
  7.6 0.9 %copy-done.2 = bf16[1,1024,128]{2,1,0:T(8,128)(2,1)S(1)} copy-done((bf16[1,1024,128]{2,1,0:T(8,128)(2,1)S(1)}, bf16[1,1024,128]{2,1,0:T(8,128)(2,1)}, u32[]{:S(2)}) %copy-start.2) | copy-done | bytes 262168
  8.5 0.9 %copy-done.3 = bf16[512,256]{1,0:T(8,128)(2,1)S(1)} copy-done((bf16[512,256]{1,0:T(8,128)(2,1)S(1)}, bf16[512,256]{1,0:T(8,128)(2,1)}, u32[]{:S(2)}) %copy-start.3) | copy-done | bytes 262168
  9.5 0.9 %copy-done.4 = f32[256,1]{1,0:T(8,128)S(1)} copy-done((f32[256,1]{1,0:T(8,128)S(1)}, f32[256,1]{1,0:T(8,128)}, u32[]{:S(2)}) %copy-start.4) | copy-done | bytes 1048
  10.4 0.8 %copy-done.6 = f32[1024,16]{0,1:T(8,128)S(1)} copy-done((f32[1024,16]{0,1:T(8,128)S(1)}, f32[1024,16]{0,1:T(8,128)}, u32[]{:S(2)}) %copy-start.6) | copy-done | bytes 65560
  11.2 0.7 %copy-done.9 = f32[16]{0:T(128)S(1)} copy-done((f32[16]{0:T(128)S(1)}, f32[16]{0:T(128)}, u32[]{:S(2)}) %copy-start.9) | copy-done | bytes 88
  11.9 0.9 %shard_map.148 = (bf16[128,384]{1,0:T(8,128)(2,1)S(1)}, bf16[128,128]{1,0:T(8,128)(2,1)S(1)}, f32[128,128]{1,0:T(8,128)S(1)}, bf16[64,256]{1,0:T(8,128)(2,1)S(1)...) custom-call(f32[1,16]{1,0:T(1,128)S(1)} %bitcast.19, f32[768,128]{1,0:T(8,128)S(1)} %copy-done.1, ...), custom_call_target="tpu_custom_call" | custom-call | flops 100000000 | bytes 2000000 | tf_op jit(solution)/shard_map/pallas_call | solution.py:228
  12.8 0.0 collective-permute-done.1
  12.8 0.7 %pad_add_fusion.ids_ref = s32[4,128]{1,0:T(4,128)S(1)} fusion(s32[2,128]{1,0:T(2,128)S(1)} %collective-permute-done.1, s32[1,128]{1,0:T(1,128)S(1)} %collective-permute-done, s32[1,128]{1,0:T(1,128)} %param.13), kind=kLoop, calls=%fused_computation.1 | loop fusion | flops 1024 | bytes 4096 | tf_op jit(solution)/shard_map/concatenate | solution.py:256
  13.5 0.8 %copy-done.7 = f32[1024,16]{0,1:T(8,128)S(1)} copy-done((f32[1024,16]{0,1:T(8,128)S(1)}, f32[1024,16]{0,1:T(8,128)}, u32[]{:S(2)}) %copy-start.7) | copy-done | bytes 65560
  14.3 1.9 %copy-done.10 = bf16[3072,512]{1,0:T(8,128)(2,1)S(1)} copy-done((bf16[3072,512]{1,0:T(8,128)(2,1)S(1)}, bf16[3072,512]{1,0:T(8,128)(2,1)}, u32[]{:S(2)}) %copy-start.10) | copy-done | bytes 3145752
  16.2 0.9 %copy-done.11 = f32[3072,7]{0,1:T(8,128)S(1)} copy-done((f32[3072,7]{0,1:T(8,128)S(1)}, f32[3072,7]{0,1:T(8,128)}, u32[]{:S(2)}) %copy-start.11) | copy-done | bytes 86040
  17.1 0.9 %copy-done.12 = bf16[512,128]{1,0:T(8,128)(2,1)S(1)} copy-done((bf16[512,128]{1,0:T(8,128)(2,1)S(1)}, bf16[512,128]{1,0:T(8,128)(2,1)}, u32[]{:S(2)}) %copy-start.12) | copy-done | bytes 131096
  18.0 5.0 %shard_map.149 = (f32[136,128]{1,0:T(8,128)S(1)}, f32[128,1024]{1,0:T(8,128)S(1)}, bf16[128,1024]{1,0:T(8,128)(2,1)S(1)}, f32[256,1024]{1,0:T(8,128)S(1)}, f32[32,1024]{1,0:T(8,128)S(1)}) custom-call(s32[4,128]{1,0:T(4,128)S(1)} %pad_add_fusion.ids_ref, bf16[3072,512]{1,0:T(8,128)(2,1)S(1)} %copy-done.10, f32[7,3072]{1,0:T(8,128)S(1)} %bitcast.20, ...), custom_call_target="tpu_custom_call" | custom-call | flops 1610612736 | bytes 6000000 | tf_op jit(solution)/shard_map/pallas_call | solution.py:228
  23.0 0.0 collective-permute-start.2
  23.0 1.3 %collective-permute-done.2 = f32[136,128]{1,0:T(8,128)S(1)} collective-permute-done((f32[136,128]{1,0:T(8,128)S(1)}, f32[136,128]{1,0:T(8,128)S(1)}, u32[]{:S(2)}, u32[]{:S(2)}) %collective-permute-start.2) | collective-permute-done | bytes 69664 | tf_op jit(solution)/shard_map/ppermute | solution.py:20
  24.3 0.1 collective-permute-start.3
  24.4 4.3 %collective-permute-done.3 = f32[136,128]{1,0:T(8,128)S(1)} collective-permute-done((f32[136,128]{1,0:T(8,128)S(1)}, f32[136,128]{1,0:T(8,128)S(1)}, u32[]{:S(2)}, u32[]{:S(2)}) %collective-permute-start.3) | collective-permute-done | bytes 69664 | tf_op jit(solution)/shard_map/ppermute | solution.py:20
  28.7 1.6 %collective-permute-start.4 = (f32[136,128]{1,0:T(8,128)S(1)}, f32[136,128]{1,0:T(8,128)S(1)}, u32[]{:S(2)}, u32[]{:S(2)}) collective-permute-start(f32[136,128]{1,0:T(8,128)S(1)} %add.16), channel_id=1, source_target_pairs={{0,1},{1,0},{2,3},{3,2},{4,5},{5,4},{6,7},{7,6},{8,9},{9,8},{10,11... | collective-permute-start | bytes 208904 | tf_op jit(solution)/shard_map/ppermute | solution.py:20
  30.3 2.8 %collective-permute-done.4 = f32[136,128]{1,0:T(8,128)S(1)} collective-permute-done((f32[136,128]{1,0:T(8,128)S(1)}, f32[136,128]{1,0:T(8,128)S(1)}, u32[]{:S(2)}, u32[]{:S(2)}) %collective-permute-start.4) | collective-permute-done | bytes 69664 | tf_op jit(solution)/shard_map/ppermute | solution.py:20
  33.1 1.7 %collective-permute-start.5 = (f32[136,128]{1,0:T(8,128)S(1)}, f32[136,128]{1,0:T(8,128)S(1)}, u32[]{:S(2)}, u32[]{:S(2)}) collective-permute-start(f32[136,128]{1,0:T(8,128)S(1)} %add.17), channel_id=1, source_target_pairs={{0,2},{1,3},{2,0},{3,1},{4,6},{5,7},{6,4},{7,5},{8,10},{9,11},{10,... | collective-permute-start | bytes 208904 | tf_op jit(solution)/shard_map/ppermute | solution.py:20
  34.7 2.7 %collective-permute-done.5 = f32[136,128]{1,0:T(8,128)S(1)} collective-permute-done((f32[136,128]{1,0:T(8,128)S(1)}, f32[136,128]{1,0:T(8,128)S(1)}, u32[]{:S(2)}, u32[]{:S(2)}) %collective-permute-start.5) | collective-permute-done | bytes 69664 | tf_op jit(solution)/shard_map/ppermute | solution.py:20
  37.5 3.4 %collective-permute-start.6 = (f32[136,128]{1,0:T(8,128)S(1)}, f32[136,128]{1,0:T(8,128)S(1)}, u32[]{:S(2)}, u32[]{:S(2)}) collective-permute-start(f32[136,128]{1,0:T(8,128)S(1)} %add.18), channel_id=1, source_target_pairs={{0,4},{1,5},{2,6},{3,7},{4,0},{5,1},{6,2},{7,3},{8,12},{9,13},{10,... | collective-permute-start | bytes 208904 | tf_op jit(solution)/shard_map/ppermute | solution.py:20
  40.9 1.5 %shard_map.150 = bf16[1024,128]{1,0:T(8,128)(2,1)} custom-call(f32[128,1024]{1,0:T(8,128)S(1)} %get-tuple-element.18.query_ref, bf16[128,1024]{1,0:T(8,128)(2,1)S(1)} %get-tuple-element.19.gated_ref, f32[256,1024]{1,0:T(8,128)S(1)} %get-tuple-element.20.spec_ref, f32[256,1024]{1,0:T(8,128)S(1)} %get-tuple-element.21.filt_ref, ...), custom_call_target="tpu_custom_call" | custom-call | flops 300000000 | bytes 3000000 | tf_op jit(solution)/shard_map/pallas_call | solution.py:228
  42.4 1.5 %collective-permute-done.6 = f32[136,128]{1,0:T(8,128)S(1)} collective-permute-done((f32[136,128]{1,0:T(8,128)S(1)}, f32[136,128]{1,0:T(8,128)S(1)}, u32[]{:S(2)}, u32[]{:S(2)}) %collective-permute-start.6) | collective-permute-done | bytes 69664 | tf_op jit(solution)/shard_map/ppermute | solution.py:20
  43.9 0.5 %slice_bitcast_fusion = f32[16]{0:T(128)} fusion(f32[136,128]{1,0:T(8,128)S(1)} %add.19), kind=kLoop, calls=%fused_computation.3 | loop fusion | bytes 128 | tf_op jit(solution)/shard_map/squeeze | solution.py:323
  44.4 0.6 %copy.19 = f32[8,2,8,128]{3,2,0,1:T(8,128)} copy(f32[8,2,8,128]{3,2,1,0:T(8,128)S(1)} %bitcast.21) | data formatting | bytes 131072 | tf_op jit(solution)/shard_map/reshape | solution.py:322
  (21 shorter events, 0.1 us)
Async XLA Ops:
  0.6 1.5 %collective-permute-start = (s32[1,128]{1,0:T(1,128)}, s32[1,128]{1,0:T(1,128)S(1)}, u32[]{:S(2)}, u32[]{:S(2)}) collective-permute-start(s32[1,128]{1,0:T(1,128)} %param.13), channel_id=1, source_target_pairs={{0,8},{8,0},{16,24},{24,16},{1,9},{9,1},{17,25},{25,17},{2,10},{10... | collective-permute-start | bytes 1544 | tf_op jit(solution)/shard_map/ppermute | solution.py:20
  2.8 10.0 %collective-permute-start.1 = (s32[2,128]{1,0:T(2,128)S(1)}, s32[2,128]{1,0:T(2,128)S(1)}, u32[]{:S(2)}, u32[]{:S(2)}) collective-permute-start(s32[2,128]{1,0:T(2,128)S(1)} %pad_add_fusion.1), channel_id=1, source_target_pairs={{0,16},{8,24},{16,0},{24,8},{1,17},{9,25},{17,1},{25,9},{2,18},{10... | collective-permute-start | bytes 3080 | tf_op jit(solution)/shard_map/ppermute | solution.py:20
  5.6 1.0 %copy-start = (f32[768,1]{1,0:T(8,128)S(1)}, f32[768,1]{1,0:T(8,128)}, u32[]{:S(2)}) copy-start(f32[768,1]{1,0:T(8,128)} %constant.13.clone.ratio_ref) | copy-start | bytes 9220
  6.6 1.0 %copy-start.1 = (f32[768,128]{1,0:T(8,128)S(1)}, f32[768,128]{1,0:T(8,128)}, u32[]{:S(2)}) copy-start(f32[768,128]{1,0:T(8,128)} %constant.12.clone.wave_ref) | copy-start | bytes 1179652
  7.6 0.9 %copy-start.2 = (bf16[1,1024,128]{2,1,0:T(8,128)(2,1)S(1)}, bf16[1,1024,128]{2,1,0:T(8,128)(2,1)}, u32[]{:S(2)}) copy-start(bf16[1,1024,128]{2,1,0:T(8,128)(2,1)} %param.19) | copy-start | bytes 786436
  8.5 0.9 %copy-start.3 = (bf16[512,256]{1,0:T(8,128)(2,1)S(1)}, bf16[512,256]{1,0:T(8,128)(2,1)}, u32[]{:S(2)}) copy-start(bf16[512,256]{1,0:T(8,128)(2,1)} %constant.14.clone.fwd_ref) | copy-start | bytes 786436
  9.5 0.9 %copy-start.4 = (f32[256,1]{1,0:T(8,128)S(1)}, f32[256,1]{1,0:T(8,128)}, u32[]{:S(2)}) copy-start(f32[256,1]{1,0:T(8,128)} %constant.15.clone.weight_ref) | copy-start | bytes 3076
  10.4 0.8 %copy-start.6 = (f32[1024,16]{0,1:T(8,128)S(1)}, f32[1024,16]{0,1:T(8,128)}, u32[]{:S(2)}) copy-start(f32[1024,16]{0,1:T(8,128)} %param.16) | copy-start | bytes 196612
  11.2 0.7 %copy-start.9 = (f32[16]{0:T(128)S(1)}, f32[16]{0:T(128)}, u32[]{:S(2)}) copy-start(f32[16]{0:T(128)} %param.17) | copy-start | bytes 196
  13.5 0.8 %copy-start.7 = (f32[1024,16]{0,1:T(8,128)S(1)}, f32[1024,16]{0,1:T(8,128)}, u32[]{:S(2)}) copy-start(f32[1024,16]{0,1:T(8,128)} %param.16) | copy-start | bytes 196612
  14.3 1.9 %copy-start.10 = (bf16[3072,512]{1,0:T(8,128)(2,1)S(1)}, bf16[3072,512]{1,0:T(8,128)(2,1)}, u32[]{:S(2)}) copy-start(bf16[3072,512]{1,0:T(8,128)(2,1)} %table_ref.1) | copy-start | bytes 9437188
  16.2 0.9 %copy-start.11 = (f32[3072,7]{0,1:T(8,128)S(1)}, f32[3072,7]{0,1:T(8,128)}, u32[]{:S(2)}) copy-start(f32[3072,7]{0,1:T(8,128)} %param.15) | copy-start | bytes 258052
  17.1 0.9 %copy-start.12 = (bf16[512,128]{1,0:T(8,128)(2,1)S(1)}, bf16[512,128]{1,0:T(8,128)(2,1)}, u32[]{:S(2)}) copy-start(bf16[512,128]{1,0:T(8,128)(2,1)} %constant.16.clone.fwd_ref) | copy-start | bytes 393220
  18.0 22.9 %copy-start.5 = (bf16[256,256]{1,0:T(8,128)(2,1)S(1)}, bf16[256,256]{1,0:T(8,128)(2,1)}, u32[]{:S(2)}) copy-start(bf16[256,256]{1,0:T(8,128)(2,1)} %constant.17.clone.inv_ref) | copy-start | bytes 393220
  18.0 22.9 %copy-start.8 = (f32[1024]{0:T(1024)S(1)}, f32[1024]{0:T(1024)}, u32[]{:S(2)}) copy-start(f32[1024]{0:T(1024)} %param.18) | copy-start | bytes 12292
  23.0 1.3 %collective-permute-start.2 = (f32[136,128]{1,0:T(8,128)S(1)}, f32[136,128]{1,0:T(8,128)S(1)}, u32[]{:S(2)}, u32[]{:S(2)}) collective-permute-start(f32[136,128]{1,0:T(8,128)S(1)} %get-tuple-element.24), channel_id=1, source_target_pairs={{0,8},{8,0},{16,24},{24,16},{1,9},{9,1},{17,25},{25,17},{2,10},{10... | collective-permute-start | bytes 208904 | tf_op jit(solution)/shard_map/ppermute | solution.py:20
  24.3 4.4 %collective-permute-start.3 = (f32[136,128]{1,0:T(8,128)S(1)}, f32[136,128]{1,0:T(8,128)S(1)}, u32[]{:S(2)}, u32[]{:S(2)}) collective-permute-start(f32[136,128]{1,0:T(8,128)S(1)} %add.15), channel_id=1, source_target_pairs={{0,16},{8,24},{16,0},{24,8},{1,17},{9,25},{17,1},{25,9},{2,18},{10... | collective-permute-start | bytes 208904 | tf_op jit(solution)/shard_map/ppermute | solution.py:20
  28.7 4.4 %collective-permute-start.4 = (f32[136,128]{1,0:T(8,128)S(1)}, f32[136,128]{1,0:T(8,128)S(1)}, u32[]{:S(2)}, u32[]{:S(2)}) collective-permute-start(f32[136,128]{1,0:T(8,128)S(1)} %add.16), channel_id=1, source_target_pairs={{0,1},{1,0},{2,3},{3,2},{4,5},{5,4},{6,7},{7,6},{8,9},{9,8},{10,11... | collective-permute-start | bytes 208904 | tf_op jit(solution)/shard_map/ppermute | solution.py:20
  33.1 4.4 %collective-permute-start.5 = (f32[136,128]{1,0:T(8,128)S(1)}, f32[136,128]{1,0:T(8,128)S(1)}, u32[]{:S(2)}, u32[]{:S(2)}) collective-permute-start(f32[136,128]{1,0:T(8,128)S(1)} %add.17), channel_id=1, source_target_pairs={{0,2},{1,3},{2,0},{3,1},{4,6},{5,7},{6,4},{7,5},{8,10},{9,11},{10,... | collective-permute-start | bytes 208904 | tf_op jit(solution)/shard_map/ppermute | solution.py:20
  37.5 6.4 %collective-permute-start.6 = (f32[136,128]{1,0:T(8,128)S(1)}, f32[136,128]{1,0:T(8,128)S(1)}, u32[]{:S(2)}, u32[]{:S(2)}) collective-permute-start(f32[136,128]{1,0:T(8,128)S(1)} %add.18), channel_id=1, source_target_pairs={{0,4},{1,5},{2,6},{3,7},{4,0},{5,1},{6,2},{7,3},{8,12},{9,13},{10,... | collective-permute-start | bytes 208904 | tf_op jit(solution)/shard_map/ppermute | solution.py:20

commit v2 on v1

--- a/solution.py
+++ b/solution.py
@@ -17,7 +17,8 @@
 
 
 def xor_permute(block, axis, mask):
-    return lax.ppermute(block, axis, [(i, i ^ mask) for i in range(lax.axis_size(axis))])
+    size = math.prod(lax.axis_size(name) for name in axis)
+    return lax.ppermute(block, axis, [(i, i ^ mask) for i in range(size)])
 
 
 def masks_of(size):
@@ -43,13 +44,7 @@
     forward = np.concatenate([np.cos(angle), imag], axis=0)
     weight = np.where(np.arange(period) % block_len == 0, 1.0, 2.0) / period
     inverse = (forward[:, :block_len] * weight[:, None]).T
-    return forward, inverse, weight
-
-
-def np_halves(table):
-    upper = table.astype(np.float32).astype(jnp.bfloat16)
-    lower = (table - upper.astype(np.float64)).astype(np.float32).astype(jnp.bfloat16)
-    return upper, lower
+    return forward, inverse
 
 
 def mode_constants(block_len, seq_len, modes):
@@ -63,50 +58,79 @@
     ratio = delay / seq_len
     parts = [np.cos(angle), np.sin(angle), -ratio * np.cos(angle), -ratio * np.sin(angle)]
     wave = np.concatenate(parts, axis=1)
-    wave = np.pad(wave, ((0, 0), (0, LANES - wave.shape[1])))
-    return wave.astype(np.float32), (-ratio).astype(np.float32)
-
-
-def tables_kernel(modes, block_len, seq_len, rates_ref, wave_ref, ratio_ref, fwd_ref, weight_ref, res_ref, grad_ref,
-                  far_ref, here_ref, here_t_ref, near_ref, filt_ref, grad_t_ref, rate_row):
+    return np.pad(wave, ((0, 0), (0, LANES - wave.shape[1]))).astype(np.float32)
+
+
+def tables_kernel(modes, block_len, seq_len, *refs):
+    sources, outs, scratch = refs[:10], refs[10:23], refs[23:]
+    (ids_out, table_out, short_out, res_out, skip_out, fwd_out, inv_out, far_ref, here_ref, here_t_ref, near_ref,
+     filt_ref, grad_t_ref) = outs
+    few, rate_row, wave, fwd, inv, grad, copied = scratch
     rate_row[...] = jnp.zeros_like(rate_row)
-    rate_row[:, :modes] = rates_ref[...]
+    targets = [wave, few, fwd, res_out, grad, inv, ids_out, short_out, skip_out, table_out]
+    copies = [
+        pltpu.make_async_copy(source, target, copied.at[i])
+        for i, (source, target) in enumerate(zip(sources, targets, strict=True))
+    ]
+    for copy in copies:
+        copy.start()
+    period = 2 * block_len
+    body = seq_len - block_len
+    copies[0].wait()
+    copies[1].wait()
+    rate_row[:, :modes] = few[...]
     rates = rate_row[...]
     for shift in (modes, 2 * modes):
         rates = rates + pltpu.roll(rates, shift, 1)
-    table = jnp.exp(ratio_ref[...] * rates) * wave_ref[...]
-    near = table[: 2 * block_len]
-    far = table[2 * block_len : 2 * block_len + seq_len - block_len]
-    here = table[2 * block_len + seq_len - block_len :]
+
+    def table_of(start, length, delay):
+        place = lax.broadcasted_iota(jnp.int32, (length, LANES), 0)
+        return jnp.exp(delay(place).astype(F32) * (-1.0 / seq_len) * rates) * wave[pl.ds(start, length), :]
+
+    near = table_of(0, period, lambda n: jnp.where(n < block_len, n, n + (seq_len - period)))
+    far = table_of(period, body, lambda n: body - n)
+    here = table_of(period + body, block_len, lambda n: n)
     used = 4 * modes
-    far_t = halves(far.T[:used])
-    far_ref[...] = jnp.concatenate(far_t, axis=0)
-    here_t = halves(here.T[:used])
-    here_ref[...] = jnp.concatenate(here_t, axis=0)
+    far_ref[...] = jnp.concatenate(halves(far.T[:used]), axis=0)
+    here_ref[...] = jnp.concatenate(halves(here.T[:used]), axis=0)
     here_t_ref[...] = here
     near_hi, near_lo = halves(near)
-    fwd = fwd_ref[...]
-    fwd_hi = fwd[: 2 * block_len]
-    fwd_lo = fwd[2 * block_len :]
+    copies[2].wait()
+    fwd_hi, fwd_lo = halves(fwd[...])
+    fwd_out[:period, :] = fwd_hi[:, :block_len]
+    fwd_out[period:, :] = fwd_lo[:, :block_len]
     spec = dot(fwd_hi, near_hi) + dot(fwd_hi, near_lo) + dot(fwd_lo, near_hi)
-    spec_t = (spec * weight_ref[...]).T
+    place = lax.broadcasted_iota(jnp.int32, (period, LANES), 0)
+    weight = jnp.where(lax.rem(place, block_len) == 0, 1.0 / period, 2.0 / period)
+    spec_t = (spec * weight).T
     grad_rows = jnp.concatenate([spec_t[:modes], spec_t[2 * modes : 3 * modes]], axis=0)
     near_ref[...] = jnp.concatenate(halves(grad_rows), axis=0)
+    copies[3].wait()
     spec_hi, spec_lo = halves(spec[:, :modes])
-    res_hi, res_lo = halves(res_ref[...])
+    res_hi, res_lo = halves(res_out[...])
     filt_ref[...] = dot(spec_hi, res_hi) + dot(spec_hi, res_lo) + dot(spec_lo, res_hi)
-    grad_t_ref[...] = grad_ref[...].astype(F32).T
+    copies[4].wait()
+    grad_t_ref[...] = grad[...].astype(F32).T
+    copies[5].wait()
+    inv_out[...] = jnp.concatenate(halves(inv[...]), axis=0)
+    for copy in copies[6:]:
+        copy.wait()
 
 
 def main_kernel(modes, blocks, block_len, taps, channels, ids_ref, table_ref, short_ref, res_ref, fwd_ref, far_ref,
-                here_ref, near_ref, grad_t_ref, part_ref, query_ref, gated_ref, spec_ref, state_ref,
+                here_ref, near_ref, grad_t_ref, part_ref, rate_ref, query_ref, gated_ref, spec_ref, state_ref,
                 onehot, feat_k, feat_v, feat_q):
     seq_len = blocks * block_len
     vocab = table_ref.shape[1]
     own = lax.axis_index("ctx")
+    bits = blocks.bit_length() - 1
     for place in range(blocks):
         source = lax.rem(own + 1 + place, blocks)
-        row = ids_ref[pl.ds(source ^ own, 1), :]
+        place_of = source ^ own
+        flags = [(place_of >> bit) & 1 for bit in range(bits)]
+        slot = sum(flag << (bits - 1 - bit) for bit, flag in enumerate(flags) if bit > 0)
+        slot = slot | (functools.reduce(lambda a, b: a ^ b, flags) << (bits - 1))
+        row = ids_ref[pl.ds(slot, 1), :]
         column = jnp.broadcast_to(row, (block_len, block_len)).T
         lane = lax.broadcasted_iota(jnp.int32, (block_len, block_len), 1)
         for piece in range(vocab // block_len):
@@ -198,7 +222,7 @@
         rate = lax.fori_loop(0, groups, lambda g, r: one_group(pl.multiple_of(g * GROUP, GROUP), r), rate)
     wide = jnp.broadcast_to(rate, (modes, LANES))
     square = jnp.concatenate([wide, jnp.zeros((LANES - modes, LANES), F32)], axis=0).T
-    part_ref[pl.ds(channels // LANES * modes, 8), :] = square[:8]
+    rate_ref[...] = square[:8]
 
 
 def mixed_kernel(modes, block_len, query_ref, gated_ref, spec_ref, filt_ref, state_ref, here_t_ref, inv_ref, skip_ref,
@@ -224,16 +248,30 @@
         out_ref[pl.ds(base, GROUP), :] = mixed.T.astype(BF16)
 
 
-def vmem_call(kernel, outs, scratch, args, flops, moved):
+def call(kernel, outs, scratch, args, cost, space=pltpu.VMEM):
     return pl.pallas_call(
         kernel,
         out_shape=[jax.ShapeDtypeStruct(shape, dtype) for shape, dtype in outs],
-        in_specs=[pl.BlockSpec(memory_space=pltpu.VMEM)] * len(args),
+        in_specs=[pl.BlockSpec(memory_space=space)] * len(args),
         out_specs=[pl.BlockSpec(memory_space=pltpu.VMEM)] * len(outs),
         scratch_shapes=scratch,
         compiler_params=pltpu.CompilerParams(vmem_limit_bytes=40 * 1024 * 1024),
-        cost_estimate=pl.CostEstimate(flops=flops, bytes_accessed=moved, transcendentals=0),
+        cost_estimate=pl.CostEstimate(flops=cost[0], bytes_accessed=cost[1], transcendentals=0),
     )(*args)
+
+
+def sum_kernel(modes, part_ref, moved_ref, grad_ref, rate_ref):
+    tiles = grad_ref.shape[1] // LANES
+    for tile in range(tiles):
+        rows = pl.ds(tile * modes, modes)
+        grad_ref[:, tile * LANES : (tile + 1) * LANES] = part_ref[rows, :] + moved_ref[rows, :].astype(F32)
+    rest = moved_ref[tiles * modes : tiles * modes + 16, :].astype(F32)
+    rate = part_ref[tiles * modes : tiles * modes + 1, :] + rest[:1] + rest[1:2]
+    rate_ref[...] = rate[:, :modes]
+
+
+def rounded(value):
+    return lax.reduce_precision(value, 8, 7)
 
 
 def per_device(token_ids, feature_table, short_weight, residue, rates, skip_gain, grad_out):
@@ -244,20 +282,34 @@
     taps = short_weight.shape[1]
     vocab = feature_table.shape[1]
     period = 2 * block_len
-    forward, inverse, weight = dft_tables(block_len)
-    fwd_hi, fwd_lo = np_halves(forward)
-    fwd_all = np.concatenate([fwd_hi, fwd_lo], axis=0)
-    inv_all = np.concatenate(np_halves(inverse), axis=0)
-    wave, ratio = mode_constants(block_len, seq_len, modes)
-    res_t = residue.T
-
-    ids = token_ids
-    for mask in masks_of(blocks):
-        ids = jnp.concatenate([ids, xor_permute(ids, "ctx", mask)], axis=0)
-
-    far, here, here_t, near, filt, grad_t = vmem_call(
+    forward, inverse = dft_tables(block_len)
+    wave = mode_constants(block_len, seq_len, modes)
+    rows = channels // LANES * modes
+
+    masks = [mask | 1 for mask in masks_of(blocks)[:0:-1]] + [1]
+    first = xor_permute(token_ids, ("ctx",), masks[0])
+    sources = [
+        jnp.asarray(wave),
+        rates[None],
+        jnp.asarray(forward.astype(np.float32)),
+        residue.T,
+        grad_out[0],
+        jnp.asarray(inverse.astype(np.float32)),
+        token_ids,
+        short_weight.T,
+        skip_gain[None],
+        feature_table,
+    ]
+    ids, table, short, res, skip, fwd, inv, far, here, here_t, near, filt, grad_t = call(
         functools.partial(tables_kernel, modes, block_len, seq_len),
         [
+            ((1, block_len), jnp.int32),
+            (feature_table.shape, BF16),
+            (short_weight.shape[::-1], F32),
+            ((modes, channels), F32),
+            ((1, channels), F32),
+            ((2 * period, block_len), BF16),
+            ((2 * block_len, period), BF16),
             ((8 * modes, seq_len - block_len), BF16),
             ((8 * modes, block_len), BF16),
             ((block_len, LANES), F32),
@@ -265,23 +317,27 @@
             ((period, channels), F32),
             ((block_len, channels), F32),
         ],
-        [pltpu.VMEM((1, LANES), F32)],
         [
-            rates[None],
-            jnp.asarray(wave),
-            jnp.asarray(ratio),
-            jnp.asarray(fwd_all),
-            jnp.asarray(weight[:, None].astype(np.float32)),
-            res_t,
-            grad_out[0],
+            pltpu.VMEM((1, modes), F32),
+            pltpu.VMEM((1, LANES), F32),
+            pltpu.VMEM(wave.shape, F32),
+            pltpu.VMEM(forward.shape, F32),
+            pltpu.VMEM(inverse.shape, F32),
+            pltpu.VMEM(grad_out.shape[1:], BF16),
+            pltpu.SemaphoreType.DMA((len(sources),)),
         ],
-        100_000_000,
-        2_000_000,
-    )
-    part, query, gated, spec, state = vmem_call(
+        [pltpu.with_memory_space_constraint(source, pltpu.HBM) for source in sources],
+        (200_000_000, 5_000_000),
+        pltpu.HBM,
+    )
+    ids = jnp.concatenate([ids, first], axis=0)
+    for mask in masks[1:]:
+        ids = jnp.concatenate([ids, xor_permute(ids, ("ctx",), mask)], axis=0)
+    part, rate, query, gated, spec, state = call(
         functools.partial(main_kernel, modes, blocks, block_len, taps, channels),
         [
-            ((channels // LANES * modes + 8, LANES), F32),
+            ((rows, LANES), F32),
+            ((8, LANES), F32),
             ((block_len, channels), F32),
             ((block_len, channels), BF16),
             ((period, channels), F32),
@@ -293,34 +349,38 @@
             pltpu.VMEM((GROUP // LANES, seq_len + HALO, LANES), F32),
             pltpu.VMEM((GROUP // LANES, block_len + HALO, LANES), F32),
         ],
-        [
-            ids,
-            feature_table,
-            short_weight.T,
-            res_t,
-            jnp.asarray(fwd_all[:, :block_len]),
-            far,
-            here,
-            near,
-            grad_t,
-        ],
-        2 * seq_len * vocab * 3 * channels,
-        6_000_000,
-    )
-    (mixed,) = vmem_call(
+        [ids, table, short, res, fwd, far, here, near, grad_t],
+        (2 * seq_len * vocab * 3 * channels, 6_000_000),
+    )
+    (mixed,) = call(
         functools.partial(mixed_kernel, modes, block_len),
         [((channels, block_len), BF16)],
         [],
-        [query, gated, spec, filt, state, here_t, jnp.asarray(inv_all), skip_gain[None]],
-        300_000_000,
-        3_000_000,
-    )
-    for axis in ("ctx", "dp"):
-        for mask in masks_of(lax.axis_size(axis)):
-            part = part + xor_permute(part, axis, mask)
-    rows = channels // LANES * modes
-    grad_res = part[:rows].reshape(channels // LANES, modes, LANES).transpose(0, 2, 1).reshape(channels, modes)
-    return (mixed[None], grad_res, part[rows, :modes])
+        [query, gated, spec, filt, state, here_t, inv, skip],
+        (300_000_000, 3_000_000),
+    )
+    replicas = lax.axis_size("dp")
+    core = replicas
+    hops = [core] + [core | mask for mask in masks_of(blocks * replicas) if mask != core]
+    filler = jnp.zeros((14, LANES), BF16)
+    for mask in hops:
+        part = rounded(part)
+        upper = rounded(rate[:1])
+        lower = rounded(rate[:1] - upper)
+        sent = jnp.concatenate([part.astype(BF16), upper.astype(BF16), lower.astype(BF16), filler], axis=0)
+        moved = xor_permute(sent, ("ctx", "dp"), mask)
+        if mask != hops[-1]:
+            part = part + moved[:rows].astype(F32)
+            rate = upper + lower + (moved[rows : rows + 1].astype(F32) + moved[rows + 1 : rows + 2].astype(F32))
+    kept = jnp.concatenate([part, upper + lower], axis=0)
+    grad, rate = call(
+        functools.partial(sum_kernel, modes),
+        [((modes, channels), F32), ((1, modes), F32)],
+        [],
+        [kept, moved],
+        (0, 200_000),
+    )
+    return (mixed[None], grad.T, rate[0])
 
 
 def solution(mesh):

time: 45.6 us -> 29.6 us (0.65)
  local copies, waits for them, and re-layouts: 12 us -> 0.08 us
  waiting for transfers between devices: 13.6 us -> 8.28 us
  Pallas kernels: 7.47 us -> 9.61 us
  other arithmetic: 1.38 us -> 0.63 us
    unnamed x26 -> x0, local copies, waits for them, and re-layouts: 10.8 us -> none
    ppermute x7, waiting for transfers between devices: 13.6 us -> 8.28 us  [xor_permute(): return lax.ppermute(block, axis, [(i, i ^ mask) for i in range(size)])]
    pallas_call x3 -> x4, Pallas kernels: 7.47 us -> 9.61 us  [call(): pl.pallas_call(kernel, out_shape=[jax.ShapeDtypeStruct(shape, dtype) for...]
    concatenate x2 -> x8, other arithmetic: 1.33 us -> 0.45 us  [the longest x5 0.42 us: per_device(): jnp.concatenate([part.astype(BF16), upper.astype(BF16), lower.astype(BF16...]
    reshape x1 -> x0, local copies, waits for them, and re-layouts: 0.63 us -> none  [per_device(): part[:rows].reshape(channels // LANES, modes, LANES).transpose(0, 2, 1)]
    squeeze x1 -> x0, local copies, waits for them, and re-layouts: 0.51 us -> none  [per_device(): return (mixed[None], grad_res, part[rows, :modes])]
  transfers between devices with their start and end apart: 7 -> 7, of which waited for: 6 -> 6; matrix products, arithmetic and copies ran while one was open for 0% -> 0% of each run, Pallas kernels for 5% -> 13%
where the time goes in v2:
time: 29.6 us; the launch traced here: 29.5 us
  starting transfers between devices  10.1 us (34%)
  Pallas kernels  9.61 us (32%)
  waiting for transfers between devices  8.28 us (28%)
  between operations  0.73 us (2%)
  other arithmetic  0.63 us (2%)
    ppermute x7, starting transfers between devices, xor_permute(): return lax.ppermute(block, axis, [(i, i ^ mask) for i in range(size)])  10.1 us
    pallas_call x4, Pallas kernels, call(): pl.pallas_call(kernel, out_shape=[jax.ShapeDtypeStruct(shape, dtype) for...  9.61 us
    ppermute x7, waiting for transfers between devices, xor_permute(): return lax.ppermute(block, axis, [(i, i ^ mask) for i in range(size)])  8.28 us
  transfers between devices with their start and end apart: 7, of which 6 were waited for; matrix products, arithmetic and copies ran while one was open for 0% of the time, Pallas kernels for 13%

profile of v2, /device:TPU:0, one launch (start us, length us, event | category | flops | bytes accessed | tf_op | source)
XLA Modules:
  0.0 29.5 jit_solution(13203928606541101155)
XLA Ops:
  0.6 2.5 %collective-permute-start = (s32[1,128]{1,0:T(1,128)}, s32[1,128]{1,0:T(1,128)S(1)}, u32[]{:S(2)}, u32[]{:S(2)}) collective-permute-start(s32[1,128]{1,0:T(1,128)} %refs_6_.1), channel_id=1, source_target_pairs={{0,24},{8,16},{16,8},{24,0},{1,25},{9,17},{17,9},{25,1},{2,26},{10... | collective-permute-start | bytes 1544 | tf_op jit(solution)/shard_map/ppermute | solution.py:21
  3.1 2.4 %shard_map.121 = (s32[1,128]{1,0:T(1,128)S(1)}, bf16[3072,512]{1,0:T(8,128)(2,1)S(1)}, f32[7,3072]{1,0:T(8,128)S(1)}, f32[16,1024]{1,0:T(8,128)S(1)}, f32[1,1024...) custom-call(f32[768,128]{1,0:T(8,128)} %constant.8.clone.refs_0_, ...), custom_call_target="tpu_custom_call" | custom-call | flops 200000000 | bytes 5000000 | tf_op jit(solution)/shard_map/pallas_call | solution.py:252
  5.5 0.0 collective-permute-done
  5.5 0.7 %collective-permute-start.1 = (s32[2,128]{1,0:T(2,128)S(1)}, s32[2,128]{1,0:T(2,128)S(1)}, u32[]{:S(2)}, u32[]{:S(2)}) collective-permute-start(s32[2,128]{1,0:T(2,128)S(1)} %pad_add_fusion.1), channel_id=1, source_target_pairs={{0,8},{8,0},{16,24},{24,16},{1,9},{9,1},{17,25},{25,17},{2,10},{10... | collective-permute-start | bytes 3080 | tf_op jit(solution)/shard_map/ppermute | solution.py:21
  6.3 0.1 pad.21.clone
  6.4 0.7 %collective-permute-done.1 = s32[2,128]{1,0:T(2,128)S(1)} collective-permute-done((s32[2,128]{1,0:T(2,128)S(1)}, s32[2,128]{1,0:T(2,128)S(1)}, u32[]{:S(2)}, u32[]{:S(2)}) %collective-permute-start.1) | collective-permute-done | bytes 1056 | tf_op jit(solution)/shard_map/ppermute | solution.py:21
  7.1 5.1 %shard_map.122 = (f32[128,128]{1,0:T(8,128)S(1)}, f32[8,128]{1,0:T(8,128)S(1)}, f32[128,1024]{1,0:T(8,128)S(1)}, bf16[128,1024]{1,0:T(8,128)(2,1)S(1)}, f32[256,1024]{1,0:T(8,128)S(1)}, /*index=5*/f32[32,1024]{1,0:T(8,128)S(1)}) custom-call(s32[4,128]{1,0:T(4,128)S(1)} %pad_add_fusion.ids_ref, bf16[3072,512]{1,0:T(8,128)(2,1)S(1)} %get-tuple-element.25.table_ref, ...), custom_call_target="tpu_custom_call" | custom-call | flops 1610612736 | bytes 6000000 | tf_op jit(solution)/shard_map/pallas_call | solution.py:252
  12.2 0.1 maximum_maximum_fusion
  12.3 0.4 %collective-permute-start.2 = (bf16[144,128]{1,0:T(8,128)(2,1)S(1)}, bf16[144,128]{1,0:T(8,128)(2,1)S(1)}, u32[]{:S(2)}, u32[]{:S(2)}) collective-permute-start(bf16[144,128]{1,0:T(8,128)(2,1)S(1)} %maximum_maximum_fusion), channel_id=1, source_target_pairs={{0,8},{1,9},{2,10},{3,11},{4,12},{5,13},{6,14},{7,15},{8,0},{9,1},... | collective-permute-start | bytes 110600 | tf_op jit(solution)/shard_map/ppermute | solution.py:21
  12.7 0.9 %collective-permute-done.2 = bf16[144,128]{1,0:T(8,128)(2,1)S(1)} collective-permute-done((bf16[144,128]{1,0:T(8,128)(2,1)S(1)}, bf16[144,128]{1,0:T(8,128)(2,1)S(1)}, u32[]{:S(2)}, u32[]{:S(2)}) %collective-permute-start.2) | collective-permute-done | bytes 36896 | tf_op jit(solution)/shard_map/ppermute | solution.py:21
  13.6 0.1 maximum_maximum_fusion.1
  13.7 1.5 %collective-permute-start.3 = (bf16[144,128]{1,0:T(8,128)(2,1)S(1)}, bf16[144,128]{1,0:T(8,128)(2,1)S(1)}, u32[]{:S(2)}, u32[]{:S(2)}) collective-permute-start(bf16[144,128]{1,0:T(8,128)(2,1)S(1)} %maximum_maximum_fusion.1), channel_id=1, source_target_pairs={{0,9},{1,8},{2,11},{3,10},{4,13},{5,12},{6,15},{7,14},{8,1},{9,0},... | collective-permute-start | bytes 110600 | tf_op jit(solution)/shard_map/ppermute | solution.py:21
  15.2 2.0 %collective-permute-done.3 = bf16[144,128]{1,0:T(8,128)(2,1)S(1)} collective-permute-done((bf16[144,128]{1,0:T(8,128)(2,1)S(1)}, bf16[144,128]{1,0:T(8,128)(2,1)S(1)}, u32[]{:S(2)}, u32[]{:S(2)}) %collective-permute-start.3) | collective-permute-done | bytes 36896 | tf_op jit(solution)/shard_map/ppermute | solution.py:21
  17.2 0.1 maximum_maximum_fusion.2
  17.3 1.6 %collective-permute-start.4 = (bf16[144,128]{1,0:T(8,128)(2,1)S(1)}, bf16[144,128]{1,0:T(8,128)(2,1)S(1)}, u32[]{:S(2)}, u32[]{:S(2)}) collective-permute-start(bf16[144,128]{1,0:T(8,128)(2,1)S(1)} %maximum_maximum_fusion.2), channel_id=1, source_target_pairs={{0,10},{1,11},{2,8},{3,9},{4,14},{5,15},{6,12},{7,13},{8,2},{9,3},... | collective-permute-start | bytes 110600 | tf_op jit(solution)/shard_map/ppermute | solution.py:21
  18.8 1.9 %collective-permute-done.4 = bf16[144,128]{1,0:T(8,128)(2,1)S(1)} collective-permute-done((bf16[144,128]{1,0:T(8,128)(2,1)S(1)}, bf16[144,128]{1,0:T(8,128)(2,1)S(1)}, u32[]{:S(2)}, u32[]{:S(2)}) %collective-permute-start.4) | collective-permute-done | bytes 36896 | tf_op jit(solution)/shard_map/ppermute | solution.py:21
  20.8 0.1 maximum_maximum_fusion.3
  20.9 2.6 %collective-permute-start.5 = (bf16[144,128]{1,0:T(8,128)(2,1)S(1)}, bf16[144,128]{1,0:T(8,128)(2,1)S(1)}, u32[]{:S(2)}, u32[]{:S(2)}) collective-permute-start(bf16[144,128]{1,0:T(8,128)(2,1)S(1)} %maximum_maximum_fusion.3), channel_id=1, source_target_pairs={{0,12},{1,13},{2,14},{3,15},{4,8},{5,9},{6,10},{7,11},{8,4},{9,5},... | collective-permute-start | bytes 110600 | tf_op jit(solution)/shard_map/ppermute | solution.py:21
  23.4 1.5 %shard_map.123 = bf16[1024,128]{1,0:T(8,128)(2,1)} custom-call(f32[128,1024]{1,0:T(8,128)S(1)} %get-tuple-element.33.query_ref, bf16[128,1024]{1,0:T(8,128)(2,1)S(1)} %get-tuple-element.34.gated_ref, f32[256,1024]{1,0:T(8,128)S(1)} %get-tuple-element.35.spec_ref, f32[256,1024]{1,0:T(8,128)S(1)} %get-tuple-element.36.filt_ref, ...), custom_call_target="tpu_custom_call" | custom-call | flops 300000000 | bytes 3000000 | tf_op jit(solution)/shard_map/pallas_call | solution.py:252
  24.9 0.3 collective-permute-done.5
  25.3 0.1 maximum_maximum_fusion.4
  25.4 0.9 %collective-permute-start.6 = (bf16[144,128]{1,0:T(8,128)(2,1)S(1)}, bf16[144,128]{1,0:T(8,128)(2,1)S(1)}, u32[]{:S(2)}, u32[]{:S(2)}) collective-permute-start(bf16[144,128]{1,0:T(8,128)(2,1)S(1)} %maximum_maximum_fusion.4), channel_id=1, source_target_pairs={{0,24},{1,25},{2,26},{3,27},{4,28},{5,29},{6,30},{7,31},{8,16},{9,... | collective-permute-start | bytes 110600 | tf_op jit(solution)/shard_map/ppermute | solution.py:21
  26.3 2.5 %collective-permute-done.6.moved_ref = bf16[144,128]{1,0:T(8,128)(2,1)S(1)} collective-permute-done((bf16[144,128]{1,0:T(8,128)(2,1)S(1)}, bf16[144,128]{1,0:T(8,128)(2,1)S(1)}, u32[]{:S(2)}, u32[]{:S(2)}) %collective-permute-start.6) | collective-permute-done | bytes 36896 | tf_op jit(solution)/shard_map/ppermute | solution.py:21
  28.8 0.6 %shard_map.124 = (f32[16,1024]{1,0:T(8,128)}, f32[1,16]{1,0:T(1,128)}) custom-call(f32[129,128]{1,0:T(8,128)S(1)} %pad_maximum_fusion.part_ref, bf16[144,128]{1,0:T(8,128)(2,1)S(1)} %collective-permute-done.6.moved_ref), custom_call_target="tpu_custom_call" | custom-call | bytes 200000 | tf_op jit(solution)/shard_map/pallas_call | solution.py:252
  (18 shorter events, 0.2 us)
Async XLA Ops:
  0.6 4.9 %collective-permute-start = (s32[1,128]{1,0:T(1,128)}, s32[1,128]{1,0:T(1,128)S(1)}, u32[]{:S(2)}, u32[]{:S(2)}) collective-permute-start(s32[1,128]{1,0:T(1,128)} %refs_6_.1), channel_id=1, source_target_pairs={{0,24},{8,16},{16,8},{24,0},{1,25},{9,17},{17,9},{25,1},{2,26},{10... | collective-permute-start | bytes 1544 | tf_op jit(solution)/shard_map/ppermute | solution.py:21
  5.5 1.6 %collective-permute-start.1 = (s32[2,128]{1,0:T(2,128)S(1)}, s32[2,128]{1,0:T(2,128)S(1)}, u32[]{:S(2)}, u32[]{:S(2)}) collective-permute-start(s32[2,128]{1,0:T(2,128)S(1)} %pad_add_fusion.1), channel_id=1, source_target_pairs={{0,8},{8,0},{16,24},{24,16},{1,9},{9,1},{17,25},{25,17},{2,10},{10... | collective-permute-start | bytes 3080 | tf_op jit(solution)/shard_map/ppermute | solution.py:21
  12.3 1.3 %collective-permute-start.2 = (bf16[144,128]{1,0:T(8,128)(2,1)S(1)}, bf16[144,128]{1,0:T(8,128)(2,1)S(1)}, u32[]{:S(2)}, u32[]{:S(2)}) collective-permute-start(bf16[144,128]{1,0:T(8,128)(2,1)S(1)} %maximum_maximum_fusion), channel_id=1, source_target_pairs={{0,8},{1,9},{2,10},{3,11},{4,12},{5,13},{6,14},{7,15},{8,0},{9,1},... | collective-permute-start | bytes 110600 | tf_op jit(solution)/shard_map/ppermute | solution.py:21
  13.7 3.4 %collective-permute-start.3 = (bf16[144,128]{1,0:T(8,128)(2,1)S(1)}, bf16[144,128]{1,0:T(8,128)(2,1)S(1)}, u32[]{:S(2)}, u32[]{:S(2)}) collective-permute-start(bf16[144,128]{1,0:T(8,128)(2,1)S(1)} %maximum_maximum_fusion.1), channel_id=1, source_target_pairs={{0,9},{1,8},{2,11},{3,10},{4,13},{5,12},{6,15},{7,14},{8,1},{9,0},... | collective-permute-start | bytes 110600 | tf_op jit(solution)/shard_map/ppermute | solution.py:21
  17.3 3.4 %collective-permute-start.4 = (bf16[144,128]{1,0:T(8,128)(2,1)S(1)}, bf16[144,128]{1,0:T(8,128)(2,1)S(1)}, u32[]{:S(2)}, u32[]{:S(2)}) collective-permute-start(bf16[144,128]{1,0:T(8,128)(2,1)S(1)} %maximum_maximum_fusion.2), channel_id=1, source_target_pairs={{0,10},{1,11},{2,8},{3,9},{4,14},{5,15},{6,12},{7,13},{8,2},{9,3},... | collective-permute-start | bytes 110600 | tf_op jit(solution)/shard_map/ppermute | solution.py:21
  20.9 4.3 %collective-permute-start.5 = (bf16[144,128]{1,0:T(8,128)(2,1)S(1)}, bf16[144,128]{1,0:T(8,128)(2,1)S(1)}, u32[]{:S(2)}, u32[]{:S(2)}) collective-permute-start(bf16[144,128]{1,0:T(8,128)(2,1)S(1)} %maximum_maximum_fusion.3), channel_id=1, source_target_pairs={{0,12},{1,13},{2,14},{3,15},{4,8},{5,9},{6,10},{7,11},{8,4},{9,5},... | collective-permute-start | bytes 110600 | tf_op jit(solution)/shard_map/ppermute | solution.py:21
  25.4 3.4 %collective-permute-start.6 = (bf16[144,128]{1,0:T(8,128)(2,1)S(1)}, bf16[144,128]{1,0:T(8,128)(2,1)S(1)}, u32[]{:S(2)}, u32[]{:S(2)}) collective-permute-start(bf16[144,128]{1,0:T(8,128)(2,1)S(1)} %maximum_maximum_fusion.4), channel_id=1, source_target_pairs={{0,24},{1,25},{2,26},{3,27},{4,28},{5,29},{6,30},{7,31},{8,16},{9,... | collective-permute-start | bytes 110600 | tf_op jit(solution)/shard_map/ppermute | solution.py:21

commit v3 on v2

v3 whole, which is shorter than its diff:
```python
import functools
import math

import jax
import jax.numpy as jnp
import numpy as np
from jax import lax
from jax.experimental import pallas as pl
from jax.experimental.pallas import tpu as pltpu
from jax.sharding import PartitionSpec as P

F32 = jnp.float32
BF16 = jnp.bfloat16
GROUP = 256
SUBLANES = 8
LANES = 128
BESIDE = 4


def xor_permute(block, axis, mask):
    size = math.prod(lax.axis_size(name) for name in axis)
    return lax.ppermute(block, axis, [(i, i ^ mask) for i in range(size)])


def masks_of(size):
    return [1 << bit for bit in range(size.bit_length() - 1)]


def halves(table):
    upper = table.astype(BF16)
    return upper, (table - upper.astype(F32)).astype(BF16)


def dot(left, right):
    return jnp.dot(left, right, preferred_element_type=F32)


def row_token(row, block_len):
    return row % SUBLANES * (block_len // SUBLANES) + row // SUBLANES


def order_matrix(block_len, transposed=False):
    row = lax.broadcasted_iota(jnp.int32, (block_len, block_len), 1 if transposed else 0)
    token = lax.broadcasted_iota(jnp.int32, (block_len, block_len), 0 if transposed else 1)
    return jnp.where(row_token(row, block_len) == token, 1.0, 0.0).astype(BF16)


def dft_tables(block_len):
    period = 2 * block_len
    column = np.arange(block_len)[:, None]
    row = np.arange(block_len)
    sample = np.concatenate([row_token(row, block_len), block_len + row_token(row, block_len)])[None, :]
    angle = (column * sample % period) * (2.0 * math.pi / period)
    parity = 1.0 - 2.0 * (sample % 2)
    imag = np.where(column == 0, parity, -np.sin(angle))
    forward = np.concatenate([np.cos(angle), imag], axis=0)
    weight = np.where(np.arange(period) % block_len == 0, 1.0, 2.0) / period
    inverse = (forward[:, :block_len] * weight[:, None]).T
    return forward, inverse


def row_delays(block_len, seq_len, row):
    token = row_token(row % block_len, block_len) + row // block_len * block_len
    period = 2 * block_len
    body = seq_len - block_len

    def near(n):
        return n + (n >= block_len) * (seq_len - period)

    return near, lambda n: body - n, lambda n: n, token


def mode_constants(block_len, seq_len, modes):
    parts = []
    for at, length in enumerate((2 * block_len, seq_len - block_len, block_len)):
        delays = row_delays(block_len, seq_len, np.arange(length))
        parts.append(delays[at](delays[3]))
    delay = np.concatenate(parts)[:, None]
    period = 2 * modes + 2
    angle = (delay * (np.arange(modes)[None, :] + 1) % period) * (2.0 * math.pi / period)
    ratio = delay / seq_len
    parts = [np.cos(angle), np.sin(angle), -ratio * np.cos(angle), -ratio * np.sin(angle)]
    wave = np.concatenate(parts, axis=1)
    return np.pad(wave, ((0, 0), (0, LANES - wave.shape[1]))).astype(np.float32)


def tables_kernel(modes, block_len, seq_len, *refs):
    sources, outs, scratch = refs[:7], refs[7:16], refs[16:]
    ids_out, grad_t_ref, short_out, res_out, fwd_out, far_ref, here_ref, near_ref, spec_ref = outs
    few, rate_row, wave, fwd, grad, copied = scratch
    targets = [few, wave, fwd, grad, ids_out, res_out, short_out]
    pairs = list(zip(sources, targets, strict=True))
    copies = [pltpu.make_async_copy(*pair, copied.at[i]) for i, pair in enumerate(pairs)]
    for copy in copies:
        copy.start()
    rate_row[...] = jnp.zeros_like(rate_row)
    period = 2 * block_len
    body = seq_len - block_len
    copies[0].wait()
    rate_row[:, :modes] = few[...]
    rates = rate_row[...]
    for shift in (modes, 2 * modes):
        rates = rates + pltpu.roll(rates, shift, 1)

    def decay_of(at, length):
        delays = row_delays(block_len, seq_len, lax.broadcasted_iota(jnp.int32, (length, LANES), 0))
        delay = delays[at](delays[3]).astype(F32)
        return jnp.exp(delay * (-1.0 / seq_len) * rates)

    near = decay_of(0, period)
    far = decay_of(1, body)
    here = decay_of(2, block_len)
    copies[1].wait()
    near = near * wave[:period]
    far = far * wave[period : period + body]
    here = here * wave[period + body :]
    used = 4 * modes
    near_hi, near_lo = halves(near)
    copies[2].wait()
    fwd_hi, fwd_lo = halves(fwd[...])
    spec = dot(fwd_hi, near_hi) + dot(fwd_hi, near_lo) + dot(fwd_lo, near_hi)
    fwd_out[:period, :] = fwd_hi[:, :block_len]
    fwd_out[period:, :] = fwd_lo[:, :block_len]
    spec_ref[:period, :] = spec
    spec_ref[period:, :] = here
    far_ref[...] = jnp.concatenate(halves(far.T[:used]), axis=0)
    here_ref[...] = jnp.concatenate(halves(here.T[:used]), axis=0)
    place = lax.broadcasted_iota(jnp.int32, (period, LANES), 0)
    weight = jnp.where(lax.rem(place, block_len) == 0, 1.0 / period, 2.0 / period)
    spec_t = (spec * weight).T
    grad_rows = jnp.concatenate([spec_t[:modes], spec_t[2 * modes : 3 * modes]], axis=0)
    near_ref[...] = jnp.concatenate(halves(grad_rows), axis=0)
    copies[3].wait()
    grad_t_ref[...] = lax.dot_general(
        order_matrix(block_len), grad[...], (((1,), (1,)), ((), ())), preferred_element_type=F32
    )
    for copy in copies[4:]:
        copy.wait()


def main_kernel(modes, blocks, block_len, taps, channels, table_ref, short_ref, res_ref, fwd_ref, far_ref, here_ref,
                near_ref, grad_t_ref, *refs):
    bits = blocks.bit_length() - 1
    ids_refs, refs = refs[: bits + 1], refs[bits + 1 :]
    part_ref, rate_ref, query_ref, gated_ref, spec_ref, state_ref, onehot, ids = refs
    groups = channels // GROUP
    filled = 0
    for ref in ids_refs:
        ids[filled : filled + ref.shape[0], :] = ref[...]
        filled += ref.shape[0]
    seq_len = blocks * block_len
    vocab = table_ref.shape[1]
    own = lax.axis_index("ctx")
    order = order_matrix(block_len)
    order = jnp.concatenate([order * 16, order], axis=1)
    lane = lax.broadcasted_iota(jnp.int32, (block_len, LANES), 1).astype(F32)
    for place in range(blocks):
        source = lax.rem(own + 1 + place, blocks)
        flags = [((source ^ own) >> bit) & 1 for bit in range(bits)]
        slot = sum(flag << (bits - 1 - bit) for bit, flag in enumerate(flags) if bit > 0)
        slot = slot | (functools.reduce(lambda a, b: a ^ b, flags) << (bits - 1))
        row = ids[pl.ds(slot, 1), :]
        digits = jnp.concatenate([row >> 4, row & 15], axis=1).astype(F32)
        digits = jnp.broadcast_to(digits, (LANES, 2 * block_len)).astype(BF16)
        column = lax.dot_general(order, digits, (((1,), (1,)), ((), ())), preferred_element_type=F32)
        for piece in range(vocab // LANES):
            onehot[pl.ds(place * block_len, block_len), pl.ds(piece * LANES, LANES)] = jnp.where(
                column == lane + float(piece * LANES), 1.0, 0.0
            ).astype(BF16)
    body = seq_len - block_len
    period = 2 * block_len
    halo = SUBLANES * (taps - 1)
    rate = jnp.zeros((modes, 1), F32)
    last = lax.broadcasted_iota(jnp.int32, (halo, GROUP), 0) % SUBLANES == SUBLANES - 1

    def gather(group, part, rows):
        block = table_ref[pl.ds(part * channels + group * GROUP, GROUP), :]
        return lax.dot_general(onehot[rows:, :], block, (((1,), (1,)), ((), ())), preferred_element_type=F32)

    def features(group):
        return gather(group, 0, body - halo), gather(group, 1, 0), gather(group, 2, 0)

    def short_conv(tail, block, rows):
        own_tail = block[block_len - halo :]
        ahead = jnp.where(last, tail, own_tail).reshape(taps - 1, SUBLANES, GROUP)
        ahead = pltpu.roll(ahead, 1, 1).reshape(halo, GROUP)
        padded = jnp.concatenate([ahead, block], axis=0)
        total = None
        for tap in range(taps):
            weight = short_ref[tap : tap + 1, pl.ds(rows, GROUP)]
            term = weight * padded[tap * SUBLANES : tap * SUBLANES + block_len]
            total = term if total is None else total + term
        return total

    def one_group(group, own_query, rate):
        base = group * GROUP
        own_query, keys, vals = own_query
        query = short_conv(own_query[:halo], own_query[halo:], base)
        gated = []
        for place in range(blocks):
            at = place * block_len
            before = (at - halo) % seq_len
            mixes = [
                short_conv(feat[before : before + halo], feat[at : at + block_len], rows)
                for feat, rows in ((keys, channels + base), (vals, 2 * channels + base))
            ]
            gated.append((mixes[0] * mixes[1]).astype(BF16))
        gated = jnp.concatenate(gated, axis=0)
        span = pl.ds(base, GROUP)
        query_ref[:, span] = query
        gated_own = gated[body:]
        gated_ref[:, span] = gated_own
        dconv = query * grad_t_ref[:, span]
        dconv_both = jnp.concatenate(halves(dconv), axis=0)
        spec = dot(fwd_ref[...], gated_own)
        spec = spec[:period] + spec[period:]
        spec_ref[:, span] = spec
        left = jnp.concatenate([fwd_ref[...], here_ref[...]], axis=0)
        dspec = dot(jnp.concatenate([left, left], axis=1), dconv_both)
        dstate = dspec[2 * period :]
        dspec = dspec[:period] + dspec[period : 2 * period]
        dstate = dstate[: 4 * modes] + dstate[4 * modes :]
        state = dot(far_ref[...], gated[:body])
        state = state[: 4 * modes] + state[4 * modes :]
        left_re, left_im = spec[:block_len], spec[block_len:]
        right_re, right_im = dspec[:block_len], dspec[block_len:]
        leading = lax.broadcasted_iota(jnp.int32, (block_len, GROUP), 0) == 0
        rere, imim = left_re * right_re, left_im * right_im
        cross_re = jnp.where(leading, rere, rere + imim)
        cross_im = jnp.where(leading, imim, left_re * right_im - left_im * right_re)
        cross = jnp.concatenate([cross_re, cross_im], axis=0)
        cross_hi, cross_lo = halves(cross)
        near = near_ref[...]
        terms = dot(near, cross_hi) + dot(near, cross_lo)
        terms = terms[: 2 * modes] + terms[2 * modes :]
        sc, ss, sc1, ss1 = (state[i * modes : (i + 1) * modes] for i in range(4))
        dc, ds, dc1, ds1 = (dstate[i * modes : (i + 1) * modes] for i in range(4))
        grad = terms[:modes] + dc * sc - ds * ss
        slope = terms[modes:] + dc1 * sc + dc * sc1 - ds1 * ss - ds * ss1
        res = res_ref[:, span]
        state_ref[:modes, span] = res * sc
        state_ref[modes:, span] = -(res * ss)
        for side in range(GROUP // LANES):
            at = (base + side * LANES) // LANES * modes
            part_ref[pl.ds(at, modes), :] = grad[:, side * LANES : (side + 1) * LANES]
        return rate + jnp.sum(res * slope, axis=1, keepdims=True)

    own_query = features(0)
    for group in range(groups):
        ahead = features(group + 1) if group + 1 < groups else None
        rate = one_group(group, own_query, rate)
        own_query = ahead
    wide = jnp.broadcast_to(rate, (modes, LANES))
    square = jnp.concatenate([wide, jnp.zeros((LANES - modes, LANES), F32)], axis=0).T
    rate_ref[...] = square[:8]


def filter_kernel(modes, block_len, spec_ref, res_ref, inv_ref, skip_ref, filt_ref, inv_out, skip_out, inv, copied):
    copies = [
        pltpu.make_async_copy(inv_ref, inv, copied.at[0]),
        pltpu.make_async_copy(skip_ref, skip_out, copied.at[1]),
    ]
    for copy in copies:
        copy.start()
    period = 2 * block_len
    spec_hi, spec_lo = halves(spec_ref[:period, :modes])
    res_hi, res_lo = halves(res_ref[...])
    left = jnp.concatenate([spec_hi, spec_hi, spec_lo], axis=1)
    filt_ref[...] = dot(left, jnp.concatenate([res_hi, res_lo, res_hi], axis=0))
    for copy in copies:
        copy.wait()
    inv_out[:, :period] = inv[...].astype(BF16)
    inv_out[:, period:] = spec_ref[period:, : 2 * modes].astype(BF16)


def mixed_kernel(block_len, query_ref, gated_ref, spec_ref, filt_ref, state_ref, inv_ref, skip_ref, out_ref):
    channels = query_ref.shape[1]
    leading = lax.broadcasted_iota(jnp.int32, (block_len, GROUP), 0) == 0
    order = order_matrix(block_len, True)
    inv = inv_ref[...]
    for base in range(0, channels, GROUP):
        span = pl.ds(base, GROUP)
        left_re, left_im = filt_ref[:block_len, span], filt_ref[block_len:, span]
        right_re, right_im = spec_ref[:block_len, span], spec_ref[block_len:, span]
        rere, imim = left_re * right_re, left_im * right_im
        out_re = jnp.where(leading, rere, rere - imim)
        out_im = jnp.where(leading, imim, left_re * right_im + left_im * right_re)
        conv = dot(inv, jnp.concatenate([out_re, out_im, state_ref[:, span]], axis=0).astype(BF16))
        mixed = query_ref[:, span] * (conv + skip_ref[:, span] * gated_ref[:, span].astype(F32))
        mixed = dot(order, mixed.astype(BF16))
        out_ref[pl.ds(base, GROUP), :] = mixed.T.astype(BF16)


def call(kernel, outs, scratch, args, cost, spaces=None):
    return pl.pallas_call(
        kernel,
        out_shape=[jax.ShapeDtypeStruct(shape, dtype) for shape, dtype in outs],
        in_specs=[pl.BlockSpec(memory_space=space) for space in spaces or [pltpu.VMEM] * len(args)],
        out_specs=[pl.BlockSpec(memory_space=pltpu.VMEM)] * len(outs),
        scratch_shapes=scratch,
        compiler_params=pltpu.CompilerParams(vmem_limit_bytes=40 * 1024 * 1024),
        cost_estimate=pl.CostEstimate(flops=cost[0], bytes_accessed=cost[1], transcendentals=0),
    )(*args)


def sum_kernel(modes, part_ref, moved_ref, grad_ref, rate_ref):
    tiles = grad_ref.shape[1] // LANES
    for tile in range(tiles):
        rows = pl.ds(tile * modes, modes)
        grad_ref[:, tile * LANES : (tile + 1) * LANES] = part_ref[rows, :] + moved_ref[rows, :].astype(F32)
    rest = moved_ref[tiles * modes : tiles * modes + 16, :].astype(F32)
    rate = part_ref[tiles * modes : tiles * modes + 1, :] + (rest[:1] + rest[1:2])
    rate_ref[...] = rate[:, :modes]


def rounded(value):
    return lax.reduce_precision(value, 8, 7)


def per_device(token_ids, feature_table, short_weight, residue, rates, skip_gain, grad_out):
    block_len = token_ids.shape[1]
    blocks = lax.axis_size("ctx")
    seq_len = block_len * blocks
    channels, modes = residue.shape
    taps = short_weight.shape[1]
    vocab = feature_table.shape[1]
    period = 2 * block_len
    forward, inverse = dft_tables(block_len)
    wave = mode_constants(block_len, seq_len, modes)
    rows = channels // LANES * modes

    masks = [mask | 1 for mask in masks_of(blocks)[:0:-1]] + [1]
    moved_ids = [xor_permute(token_ids, ("ctx",), masks[0])]
    def in_hbm(*arrays):
        return [pltpu.with_memory_space_constraint(array, pltpu.HBM) for array in arrays]

    vmem, hbm = pltpu.VMEM, pltpu.HBM
    ids, grad_t, short, res, fwd, far, here, near, table_spec = call(
        functools.partial(tables_kernel, modes, block_len, seq_len),
        [
            ((1, block_len), jnp.int32),
            ((block_len, channels), F32),
            (short_weight.shape[::-1], F32),
            ((modes, channels), F32),
            ((2 * period, block_len), BF16),
            ((8 * modes, seq_len - block_len), BF16),
            ((8 * modes, block_len), BF16),
            ((4 * modes, period), BF16),
            ((period + block_len, LANES), F32),
        ],
        [
            vmem((1, modes), F32),
            vmem((1, LANES), F32),
            vmem(wave.shape, F32),
            vmem(forward.shape, F32),
            vmem(grad_out.shape[1:], BF16),
            pltpu.SemaphoreType.DMA((7,)),
        ],
        in_hbm(
            rates[None],
            jnp.asarray(wave),
            jnp.asarray(forward.astype(np.float32)),
            grad_out[0],
            token_ids,
            residue.T,
            short_weight.T,
        ),
        (10_000_000_000, 40_000_000),
        [hbm] * 7,
    )
    for mask in masks[1:]:
        moved_ids.append(xor_permute(jnp.concatenate([ids, *moved_ids], axis=0), ("ctx",), mask))
    part, rate, query, gated, spec, state = call(
        functools.partial(main_kernel, modes, blocks, block_len, taps, channels),
        [
            ((rows, LANES), F32),
            ((8, LANES), F32),
            ((block_len, channels), F32),
            ((block_len, channels), BF16),
            ((period, channels), F32),
            ((2 * modes, channels), F32),
        ],
        [
            vmem((seq_len, vocab), BF16),
            vmem((blocks, block_len), jnp.int32),
        ],
        [feature_table, short, res, fwd, far, here, near, grad_t, ids, *moved_ids],
        (2 * seq_len * vocab * 3 * channels, 6_000_000),
    )
    core = lax.axis_size("dp")
    stages = [core] + [mask | core for mask in masks_of(blocks * core) if mask != core]
    filler = jnp.zeros((14, LANES), BF16)
    for stage in stages:
        part = rounded(part)
        upper = rounded(rate[:1])
        lower = rounded(rate[:1] - upper)
        sent = jnp.concatenate([part.astype(BF16), upper.astype(BF16), lower.astype(BF16), filler], axis=0)
        if stage == stages[1]:
            sent, res = lax.optimization_barrier((sent, res))
            filt, inv, skip = call(
                functools.partial(filter_kernel, modes, block_len),
                [((period, channels), F32), ((block_len, period + 2 * modes), BF16), ((1, channels), F32)],
                [vmem(inverse.shape, F32), pltpu.SemaphoreType.DMA((2,))],
                [table_spec, res, *in_hbm(jnp.asarray(inverse.astype(np.float32)), skip_gain[None])],
                (50_000_000, 1_500_000),
                [vmem, vmem, hbm, hbm],
            )
        if stage == stages[BESIDE]:
            sent, query = lax.optimization_barrier((sent, query))
            (mixed,) = call(
                functools.partial(mixed_kernel, block_len),
                [((channels, block_len), BF16)],
                [],
                [query, gated, spec, filt, state, inv, skip],
                (300_000_000, 3_000_000),
            )
        moved = xor_permute(sent, ("ctx", "dp"), stage)
        if stage != stages[-1]:
            part = part + moved[:rows].astype(F32)
            rate = upper + lower + (moved[rows : rows + 1].astype(F32) + moved[rows + 1 : rows + 2].astype(F32))
    kept = jnp.concatenate([part, upper + lower], axis=0)
    grad, rate = call(
        functools.partial(sum_kernel, modes),
        [((modes, channels), F32), ((1, modes), F32)],
        [],
        [kept, moved],
        (0, 200_000),
    )
    return (mixed[None], grad.T, rate[0])


def solution(mesh):
    return jax.shard_map(
        per_device,
        mesh=mesh,
        in_specs=(P("dp", "ctx"), P(), P(), P(), P(), P(), P("dp", None, "ctx")),
        out_specs=(P("dp", None, "ctx"), P(), P()),
        check_vma=False,
    )
```

time: 29.6 us -> 28.3 us (0.956)
  waiting for transfers between devices: 8.28 us -> 6.64 us
  starting transfers between devices: 10.1 us -> 10.6 us
    ppermute x7, waiting for transfers between devices: 8.28 us -> 6.64 us  [xor_permute(): return lax.ppermute(block, axis, [(i, i ^ mask) for i in range(size)])]
    ppermute x7, starting transfers between devices: 10.1 us -> 10.6 us  [xor_permute(): return lax.ppermute(block, axis, [(i, i ^ mask) for i in range(size)])]
    pallas_call x4 -> x5, Pallas kernels: 9.61 us -> 9.41 us  [call(): pl.pallas_call(kernel, out_shape=[jax.ShapeDtypeStruct(shape, dtype) for...]
  transfers between devices with their start and end apart: 7 -> 7, of which waited for: 6 -> 6; matrix products, arithmetic and copies ran while one was open for 0% -> 0% of each run, Pallas kernels for 13% -> 16%
where the time goes in v3:
time: 28.3 us; the launch traced here: 28.1 us
  starting transfers between devices  10.6 us (37%)
  Pallas kernels  9.41 us (33%)
  waiting for transfers between devices  6.64 us (23%)
  between operations  0.74 us (3%)
  other arithmetic  0.63 us (2%)
    ppermute x7, starting transfers between devices, xor_permute(): return lax.ppermute(block, axis, [(i, i ^ mask) for i in range(size)])  10.6 us
    pallas_call x5, Pallas kernels, call(): pl.pallas_call(kernel, out_shape=[jax.ShapeDtypeStruct(shape, dtype) for...  9.41 us
    ppermute x7, waiting for transfers between devices, xor_permute(): return lax.ppermute(block, axis, [(i, i ^ mask) for i in range(size)])  6.64 us
  transfers between devices with their start and end apart: 7, of which 6 were waited for; matrix products, arithmetic and copies ran while one was open for 0% of the time, Pallas kernels for 16%

profile of v3, /device:TPU:0, one launch (start us, length us, event | category | flops | bytes accessed | tf_op | source)
XLA Modules:
  0.0 28.1 jit_solution(3214365742830431350)
XLA Ops:
  0.6 2.5 %collective-permute-start = (s32[1,128]{1,0:T(1,128)}, s32[1,128]{1,0:T(1,128)S(1)}, u32[]{:S(2)}, u32[]{:S(2)}) collective-permute-start(s32[1,128]{1,0:T(1,128)} %refs_4_.1), channel_id=1, source_target_pairs={{0,24},{8,16},{16,8},{24,0},{1,25},{9,17},{17,9},{25,1},{2,26},{10... | collective-permute-start | bytes 1544 | tf_op jit(solution)/shard_map/ppermute | solution.py:22
  3.1 0.0 copy-start
  3.1 1.9 %shard_map.121 = (s32[1,128]{1,0:T(1,128)S(1)}, f32[128,1024]{1,0:T(8,128)S(1)}, f32[7,3072]{1,0:T(8,128)S(1)}, f32[16,1024]{1,0:T(8,128)S(1)}, bf16[512,128]{1,...) custom-call(f32[1,16]{1,0:T(1,128)} %bitcast.14, ...), custom_call_target="tpu_custom_call" | custom-call | flops 10000000000 | bytes 40000000 | tf_op jit(solution)/shard_map/pallas_call | solution.py:295
  5.0 0.0 collective-permute-done.refs_1_
  5.0 0.7 %collective-permute-start.1 = (s32[2,128]{1,0:T(2,128)S(1)}, s32[2,128]{1,0:T(2,128)S(1)}, u32[]{:S(2)}, u32[]{:S(2)}) collective-permute-start(s32[2,128]{1,0:T(2,128)S(1)} %pad_add_fusion), channel_id=1, source_target_pairs={{0,8},{8,0},{16,24},{24,16},{1,9},{9,1},{17,25},{25,17},{2,10},{10... | collective-permute-start | bytes 3080 | tf_op jit(solution)/shard_map/ppermute | solution.py:22
  5.8 0.1 pad.21.clone
  5.9 0.7 %collective-permute-done.1.refs_2_ = s32[2,128]{1,0:T(2,128)S(1)} collective-permute-done((s32[2,128]{1,0:T(2,128)S(1)}, s32[2,128]{1,0:T(2,128)S(1)}, u32[]{:S(2)}, u32[]{:S(2)}) %collective-permute-start.1) | collective-permute-done | bytes 1056 | tf_op jit(solution)/shard_map/ppermute | solution.py:22
  6.6 0.0 copy-done
  6.6 4.2 %shard_map.122 = (f32[128,128]{1,0:T(8,128)S(1)}, f32[8,128]{1,0:T(8,128)S(1)}, f32[128,1024]{1,0:T(8,128)S(1)}, bf16[128,1024]{1,0:T(8,128)(2,1)S(1)}, f32[256,1024]{1,0:T(8,128)S(1)}, /*index=5*/f32[32,1024]{1,0:T(8,128)S(1)}) custom-call(bf16[3072,512]{1,0:T(8,128)(2,1)S(1)} %copy-done, f32[7,3072]{1,0:T(8,128)S(1)} %get-tuple-element.27.short_ref, ...), custom_call_target="tpu_custom_call" | custom-call | flops 1610612736 | bytes 6000000 | tf_op jit(solution)/shard_map/pallas_call | solution.py:295
  10.9 0.1 maximum_maximum_fusion
  11.0 0.4 %collective-permute-start.2 = (bf16[144,128]{1,0:T(8,128)(2,1)S(1)}, bf16[144,128]{1,0:T(8,128)(2,1)S(1)}, u32[]{:S(2)}, u32[]{:S(2)}) collective-permute-start(bf16[144,128]{1,0:T(8,128)(2,1)S(1)} %maximum_maximum_fusion), channel_id=1, source_target_pairs={{0,8},{1,9},{2,10},{3,11},{4,12},{5,13},{6,14},{7,15},{8,0},{9,1},... | collective-permute-start | bytes 110600 | tf_op jit(solution)/shard_map/ppermute | solution.py:22
  11.4 0.9 %collective-permute-done.2 = bf16[144,128]{1,0:T(8,128)(2,1)S(1)} collective-permute-done((bf16[144,128]{1,0:T(8,128)(2,1)S(1)}, bf16[144,128]{1,0:T(8,128)(2,1)S(1)}, u32[]{:S(2)}, u32[]{:S(2)}) %collective-permute-start.2) | collective-permute-done | bytes 36896 | tf_op jit(solution)/shard_map/ppermute | solution.py:22
  12.3 0.1 maximum_maximum_fusion.1
  12.4 1.5 %collective-permute-start.3 = (bf16[144,128]{1,0:T(8,128)(2,1)S(1)}, bf16[144,128]{1,0:T(8,128)(2,1)S(1)}, u32[]{:S(2)}, u32[]{:S(2)}) collective-permute-start(bf16[144,128]{1,0:T(8,128)(2,1)S(1)} %maximum_maximum_fusion.1), channel_id=1, source_target_pairs={{0,9},{1,8},{2,11},{3,10},{4,13},{5,12},{6,15},{7,14},{8,1},{9,0},... | collective-permute-start | bytes 110600 | tf_op jit(solution)/shard_map/ppermute | solution.py:22
  13.9 2.0 %collective-permute-done.3 = bf16[144,128]{1,0:T(8,128)(2,1)S(1)} collective-permute-done((bf16[144,128]{1,0:T(8,128)(2,1)S(1)}, bf16[144,128]{1,0:T(8,128)(2,1)S(1)}, u32[]{:S(2)}, u32[]{:S(2)}) %collective-permute-start.3) | collective-permute-done | bytes 36896 | tf_op jit(solution)/shard_map/ppermute | solution.py:22
  15.9 0.1 maximum_maximum_fusion.2
  16.0 1.6 %collective-permute-start.4 = (bf16[144,128]{1,0:T(8,128)(2,1)S(1)}, bf16[144,128]{1,0:T(8,128)(2,1)S(1)}, u32[]{:S(2)}, u32[]{:S(2)}) collective-permute-start(bf16[144,128]{1,0:T(8,128)(2,1)S(1)} %maximum_maximum_fusion.2), channel_id=1, source_target_pairs={{0,10},{1,11},{2,8},{3,9},{4,14},{5,15},{6,12},{7,13},{8,2},{9,3},... | collective-permute-start | bytes 110600 | tf_op jit(solution)/shard_map/ppermute | solution.py:22
  17.5 1.9 %collective-permute-done.4 = bf16[144,128]{1,0:T(8,128)(2,1)S(1)} collective-permute-done((bf16[144,128]{1,0:T(8,128)(2,1)S(1)}, bf16[144,128]{1,0:T(8,128)(2,1)S(1)}, u32[]{:S(2)}, u32[]{:S(2)}) %collective-permute-start.4) | collective-permute-done | bytes 36896 | tf_op jit(solution)/shard_map/ppermute | solution.py:22
  19.5 0.1 maximum_maximum_fusion.3
  19.5 2.6 %collective-permute-start.5 = (bf16[144,128]{1,0:T(8,128)(2,1)S(1)}, bf16[144,128]{1,0:T(8,128)(2,1)S(1)}, u32[]{:S(2)}, u32[]{:S(2)}) collective-permute-start(bf16[144,128]{1,0:T(8,128)(2,1)S(1)} %maximum_maximum_fusion.3), channel_id=1, source_target_pairs={{0,12},{1,13},{2,14},{3,15},{4,8},{5,9},{6,10},{7,11},{8,4},{9,5},... | collective-permute-start | bytes 110600 | tf_op jit(solution)/shard_map/ppermute | solution.py:22
  22.1 0.9 %shard_map.123 = (f32[256,1024]{1,0:T(8,128)S(1)}, bf16[128,288]{1,0:T(8,128)(2,1)S(1)}, f32[1,1024]{1,0:T(1,128)S(1)}) custom-call(f32[384,128]{1,0:T(8,128)S(1)} %get-tuple-element.42.spec_ref, f32[16,1024]{1,0:T(8,128)S(1)} %get-tuple-element.43.res_ref, f32[128,256]{1,0:T(8,128)} %constant.10.clone.inv_ref, f32[1,1024]{1,0:T(1,128)} %bitcast.9), custom_call_target="tpu_custom_call" | custom-call | flops 50000000 | bytes 1500000 | tf_op jit(solution)/shard_map/pallas_call | solution.py:295
  23.1 0.8 %collective-permute-done.5 = bf16[144,128]{1,0:T(8,128)(2,1)S(1)} collective-permute-done((bf16[144,128]{1,0:T(8,128)(2,1)S(1)}, bf16[144,128]{1,0:T(8,128)(2,1)S(1)}, u32[]{:S(2)}, u32[]{:S(2)}) %collective-permute-start.5) | collective-permute-done | bytes 36896 | tf_op jit(solution)/shard_map/ppermute | solution.py:22
  24.0 0.1 maximum_maximum_fusion.4
  24.1 1.4 %collective-permute-start.6 = (bf16[144,128]{1,0:T(8,128)(2,1)S(1)}, bf16[144,128]{1,0:T(8,128)(2,1)S(1)}, u32[]{:S(2)}, u32[]{:S(2)}) collective-permute-start(bf16[144,128]{1,0:T(8,128)(2,1)S(1)} %maximum_maximum_fusion.4), channel_id=1, source_target_pairs={{0,24},{1,25},{2,26},{3,27},{4,28},{5,29},{6,30},{7,31},{8,16},{9,... | collective-permute-start | bytes 110600 | tf_op jit(solution)/shard_map/ppermute | solution.py:22
  25.5 1.7 %shard_map.124 = bf16[1024,128]{1,0:T(8,128)(2,1)} custom-call(f32[128,1024]{1,0:T(8,128)S(1)} %get-tuple-element.39.query_ref, bf16[128,1024]{1,0:T(8,128)(2,1)S(1)} %get-tuple-element.40.gated_ref, f32[256,1024]{1,0:T(8,128)S(1)} %get-tuple-element.41.spec_ref, f32[256,1024]{1,0:T(8,128)S(1)} %get-tuple-element.44.filt_ref, ...), custom_call_target="tpu_custom_call" | custom-call | flops 300000000 | bytes 3000000 | tf_op jit(solution)/shard_map/pallas_call | solution.py:295
  27.2 0.3 %collective-permute-done.6.moved_ref = bf16[144,128]{1,0:T(8,128)(2,1)S(1)} collective-permute-done((bf16[144,128]{1,0:T(8,128)(2,1)S(1)}, bf16[144,128]{1,0:T(8,128)(2,1)S(1)}, u32[]{:S(2)}, u32[]{:S(2)}) %collective-permute-start.6) | collective-permute-done | bytes 36896 | tf_op jit(solution)/shard_map/ppermute | solution.py:22
  27.5 0.6 %shard_map.125 = (f32[16,1024]{1,0:T(8,128)}, f32[1,16]{1,0:T(1,128)}) custom-call(f32[129,128]{1,0:T(8,128)S(1)} %pad_maximum_fusion.part_ref, bf16[144,128]{1,0:T(8,128)(2,1)S(1)} %collective-permute-done.6.moved_ref), custom_call_target="tpu_custom_call" | custom-call | bytes 200000 | tf_op jit(solution)/shard_map/pallas_call | solution.py:295
  (17 shorter events, 0.2 us)
Async XLA Ops:
  0.6 4.4 %collective-permute-start = (s32[1,128]{1,0:T(1,128)}, s32[1,128]{1,0:T(1,128)S(1)}, u32[]{:S(2)}, u32[]{:S(2)}) collective-permute-start(s32[1,128]{1,0:T(1,128)} %refs_4_.1), channel_id=1, source_target_pairs={{0,24},{8,16},{16,8},{24,0},{1,25},{9,17},{17,9},{25,1},{2,26},{10... | collective-permute-start | bytes 1544 | tf_op jit(solution)/shard_map/ppermute | solution.py:22
  3.1 3.5 %copy-start = (bf16[3072,512]{1,0:T(8,128)(2,1)S(1)}, bf16[3072,512]{1,0:T(8,128)(2,1)}, u32[]{:S(2)}) copy-start(bf16[3072,512]{1,0:T(8,128)(2,1)} %table_ref.1) | copy-start | bytes 9437188
  5.0 1.6 %collective-permute-start.1 = (s32[2,128]{1,0:T(2,128)S(1)}, s32[2,128]{1,0:T(2,128)S(1)}, u32[]{:S(2)}, u32[]{:S(2)}) collective-permute-start(s32[2,128]{1,0:T(2,128)S(1)} %pad_add_fusion), channel_id=1, source_target_pairs={{0,8},{8,0},{16,24},{24,16},{1,9},{9,1},{17,25},{25,17},{2,10},{10... | collective-permute-start | bytes 3080 | tf_op jit(solution)/shard_map/ppermute | solution.py:22
  11.0 1.3 %collective-permute-start.2 = (bf16[144,128]{1,0:T(8,128)(2,1)S(1)}, bf16[144,128]{1,0:T(8,128)(2,1)S(1)}, u32[]{:S(2)}, u32[]{:S(2)}) collective-permute-start(bf16[144,128]{1,0:T(8,128)(2,1)S(1)} %maximum_maximum_fusion), channel_id=1, source_target_pairs={{0,8},{1,9},{2,10},{3,11},{4,12},{5,13},{6,14},{7,15},{8,0},{9,1},... | collective-permute-start | bytes 110600 | tf_op jit(solution)/shard_map/ppermute | solution.py:22
  12.4 3.4 %collective-permute-start.3 = (bf16[144,128]{1,0:T(8,128)(2,1)S(1)}, bf16[144,128]{1,0:T(8,128)(2,1)S(1)}, u32[]{:S(2)}, u32[]{:S(2)}) collective-permute-start(bf16[144,128]{1,0:T(8,128)(2,1)S(1)} %maximum_maximum_fusion.1), channel_id=1, source_target_pairs={{0,9},{1,8},{2,11},{3,10},{4,13},{5,12},{6,15},{7,14},{8,1},{9,0},... | collective-permute-start | bytes 110600 | tf_op jit(solution)/shard_map/ppermute | solution.py:22
  16.0 3.4 %collective-permute-start.4 = (bf16[144,128]{1,0:T(8,128)(2,1)S(1)}, bf16[144,128]{1,0:T(8,128)(2,1)S(1)}, u32[]{:S(2)}, u32[]{:S(2)}) collective-permute-start(bf16[144,128]{1,0:T(8,128)(2,1)S(1)} %maximum_maximum_fusion.2), channel_id=1, source_target_pairs={{0,10},{1,11},{2,8},{3,9},{4,14},{5,15},{6,12},{7,13},{8,2},{9,3},... | collective-permute-start | bytes 110600 | tf_op jit(solution)/shard_map/ppermute | solution.py:22
  19.5 4.3 %collective-permute-start.5 = (bf16[144,128]{1,0:T(8,128)(2,1)S(1)}, bf16[144,128]{1,0:T(8,128)(2,1)S(1)}, u32[]{:S(2)}, u32[]{:S(2)}) collective-permute-start(bf16[144,128]{1,0:T(8,128)(2,1)S(1)} %maximum_maximum_fusion.3), channel_id=1, source_target_pairs={{0,12},{1,13},{2,14},{3,15},{4,8},{5,9},{6,10},{7,11},{8,4},{9,5},... | collective-permute-start | bytes 110600 | tf_op jit(solution)/shard_map/ppermute | solution.py:22
  24.1 3.4 %collective-permute-start.6 = (bf16[144,128]{1,0:T(8,128)(2,1)S(1)}, bf16[144,128]{1,0:T(8,128)(2,1)S(1)}, u32[]{:S(2)}, u32[]{:S(2)}) collective-permute-start(bf16[144,128]{1,0:T(8,128)(2,1)S(1)} %maximum_maximum_fusion.4), channel_id=1, source_target_pairs={{0,24},{1,25},{2,26},{3,27},{4,28},{5,29},{6,30},{7,31},{8,16},{9,... | collective-permute-start | bytes 110600 | tf_op jit(solution)/shard_map/ppermute | solution.py:22

commit v4 on v3

v4 whole, which is shorter than its diff:
```python
import functools
import math

import jax
import jax.numpy as jnp
import numpy as np
from jax import lax
from jax.experimental import pallas as pl
from jax.experimental.pallas import tpu as pltpu
from jax.sharding import PartitionSpec as P

F32 = jnp.float32
BF16 = jnp.bfloat16
GROUP = 256
WIDE = 2 * GROUP
SUBLANES = 8
LANES = 128


def xor_permute(block, axis, mask):
    size = math.prod(lax.axis_size(name) for name in axis)
    return lax.ppermute(block, axis, [(i, i ^ mask) for i in range(size)])


def masks_of(size):
    return [1 << bit for bit in range(size.bit_length() - 1)]


def half_index():
    bits = lax.axis_index("ctx") ^ lax.axis_index("dp")
    for shift in (4, 2, 1):
        bits = bits ^ (bits >> shift)
    return bits & 1


def halves(table):
    upper = table.astype(BF16)
    return upper, (table - upper.astype(F32)).astype(BF16)


def dot(left, right):
    return jnp.dot(left, right, preferred_element_type=F32)


def row_token(row, block_len):
    return row % SUBLANES * (block_len // SUBLANES) + row // SUBLANES


def order_matrix(block_len, transposed=False):
    row = lax.broadcasted_iota(jnp.int32, (block_len, block_len), 1 if transposed else 0)
    token = lax.broadcasted_iota(jnp.int32, (block_len, block_len), 0 if transposed else 1)
    return jnp.where(row_token(row, block_len) == token, 1.0, 0.0).astype(BF16)


def dft_tables(block_len):
    period = 2 * block_len
    column = np.arange(block_len)[:, None]
    row = np.arange(block_len)
    sample = np.concatenate([row_token(row, block_len), block_len + row_token(row, block_len)])[None, :]
    angle = (column * sample % period) * (2.0 * math.pi / period)
    parity = 1.0 - 2.0 * (sample % 2)
    imag = np.where(column == 0, parity, -np.sin(angle))
    forward = np.concatenate([np.cos(angle), imag], axis=0)
    weight = np.where(np.arange(period) % block_len == 0, 1.0, 2.0) / period
    inverse = (forward[:, :block_len] * weight[:, None]).T
    return forward, inverse


def row_delays(block_len, seq_len, row):
    token = row_token(row % block_len, block_len) + row // block_len * block_len
    period = 2 * block_len
    body = seq_len - block_len

    def near(n):
        return n + (n >= block_len) * (seq_len - period)

    return near, lambda n: body - n, lambda n: n, token


def mode_constants(block_len, seq_len, modes):
    parts = []
    for at, length in enumerate((2 * block_len, seq_len - block_len, block_len)):
        delays = row_delays(block_len, seq_len, np.arange(length))
        parts.append(delays[at](delays[3]))
    delay = np.concatenate(parts)[:, None]
    period = 2 * modes + 2
    angle = (delay * (np.arange(modes)[None, :] + 1) % period) * (2.0 * math.pi / period)
    ratio = delay / seq_len
    parts = [np.cos(angle), np.sin(angle), -ratio * np.cos(angle), -ratio * np.sin(angle)]
    wave = np.concatenate(parts, axis=1)
    return np.pad(wave, ((0, 0), (0, LANES - wave.shape[1]))).astype(np.float32)


def tables_kernel(modes, block_len, seq_len, *refs):
    sources, outs, scratch = refs[:6], refs[6:14], refs[14:]
    ids_out, short_out, res_out, fwd_out, far_ref, here_ref, near_ref, spec_ref = outs
    few, rate_row, wave, fwd, copied = scratch
    targets = [few, wave, fwd, ids_out, res_out, short_out]
    pairs = list(zip(sources, targets, strict=True))
    copies = [pltpu.make_async_copy(*pair, copied.at[i]) for i, pair in enumerate(pairs)]
    for copy in copies:
        copy.start()
    rate_row[...] = jnp.zeros_like(rate_row)
    period = 2 * block_len
    body = seq_len - block_len
    copies[0].wait()
    rate_row[:, :modes] = few[...]
    rates = rate_row[...]
    for shift in (modes, 2 * modes):
        rates = rates + pltpu.roll(rates, shift, 1)

    def decay_of(at, length):
        delays = row_delays(block_len, seq_len, lax.broadcasted_iota(jnp.int32, (length, LANES), 0))
        delay = delays[at](delays[3]).astype(F32)
        return jnp.exp(delay * (-1.0 / seq_len) * rates)

    near = decay_of(0, period)
    far = decay_of(1, body)
    here = decay_of(2, block_len)
    copies[1].wait()
    near = near * wave[:period]
    far = far * wave[period : period + body]
    here = here * wave[period + body :]
    used = 4 * modes
    near_hi, near_lo = halves(near)
    copies[2].wait()
    fwd_hi, fwd_lo = halves(fwd[...])
    spec = dot(fwd_hi, near_hi) + dot(fwd_hi, near_lo) + dot(fwd_lo, near_hi)
    fwd_out[:period, :] = fwd_hi[:, :block_len]
    fwd_out[period:, :] = fwd_lo[:, :block_len]
    spec_ref[:period, :] = spec
    spec_ref[period:, :] = here
    far_ref[...] = jnp.concatenate(halves(far.T[:used]), axis=0)
    here_ref[...] = jnp.concatenate(halves(here.T[:used]), axis=0)
    place = lax.broadcasted_iota(jnp.int32, (period, LANES), 0)
    weight = jnp.where(lax.rem(place, block_len) == 0, 1.0 / period, 2.0 / period)
    spec_t = (spec * weight).T
    grad_rows = jnp.concatenate([spec_t[:modes], spec_t[2 * modes : 3 * modes]], axis=0)
    near_ref[...] = jnp.concatenate(halves(grad_rows), axis=0)
    for copy in copies[3:]:
        copy.wait()


def main_kernel(modes, blocks, block_len, taps, channels, table_ref, short_ref, res_ref, fwd_ref, far_ref, here_ref,
                near_ref, grad_ref, mate_ref, *refs):
    bits = blocks.bit_length() - 1
    ids_refs, refs = refs[: bits + 1], refs[bits + 1 :]
    part_ref, query_ref, gated_ref, spec_ref, state_ref, onehot, ids = refs
    half = channels // 2
    groups = half // GROUP
    first = half_index() * half
    filled = 0
    for ref in ids_refs:
        ids[filled : filled + ref.shape[0], :] = ref[...]
        filled += ref.shape[0]
    seq_len = blocks * block_len
    vocab = table_ref.shape[1]
    own = lax.axis_index("ctx")
    order_one = order_matrix(block_len)
    order = jnp.concatenate([order_one * 16, order_one], axis=1)
    on_hi = (own & 1) == 1
    lane = lax.broadcasted_iota(jnp.int32, (block_len, LANES), 1).astype(F32)
    for place in range(blocks):
        source = lax.rem((own & -2) + 2 + place, blocks)
        flags = [((source ^ own) >> bit) & 1 for bit in range(bits)]
        slot = sum(flag << (bits - 1 - bit) for bit, flag in enumerate(flags) if bit > 0)
        slot = slot | (functools.reduce(lambda a, b: a ^ b, flags) << (bits - 1))
        row = ids[pl.ds(slot, 1), :]
        digits = jnp.concatenate([row >> 4, row & 15], axis=1).astype(F32)
        digits = jnp.broadcast_to(digits, (LANES, 2 * block_len)).astype(BF16)
        column = lax.dot_general(order, digits, (((1,), (1,)), ((), ())), preferred_element_type=F32)
        for piece in range(vocab // LANES):
            onehot[pl.ds(place * block_len, block_len), pl.ds(piece * LANES, LANES)] = jnp.where(
                column == lane + float(piece * LANES), 1.0, 0.0
            ).astype(BF16)
    body = seq_len - block_len
    period = 2 * block_len
    halo = SUBLANES * (taps - 1)
    rate = jnp.zeros((modes, 1), F32)
    last = lax.broadcasted_iota(jnp.int32, (halo, GROUP), 0) % SUBLANES == SUBLANES - 1

    def gather(group, part, rows):
        block = table_ref[pl.ds(pl.multiple_of(first + part * channels + group * GROUP, GROUP), GROUP), :]
        return lax.dot_general(onehot[rows:, :], block, (((1,), (1,)), ((), ())), preferred_element_type=F32)

    def features(group):
        return gather(group, 0, body - block_len - halo), gather(group, 1, 0), gather(group, 2, 0)

    def short_conv(feat, at, weights):
        tail = feat[(at - halo) % feat.shape[0] :][:halo]
        block = feat[at : at + block_len]
        ahead = jnp.where(last, tail, block[block_len - halo :]).reshape(taps - 1, SUBLANES, GROUP)
        ahead = pltpu.roll(ahead, 1, 1).reshape(halo, GROUP)
        padded = jnp.concatenate([ahead, block], axis=0)
        total = None
        for tap in range(taps):
            term = weights[tap : tap + 1] * padded[tap * SUBLANES : tap * SUBLANES + block_len]
            total = term if total is None else total + term
        return total

    def one_group(group, feats, rate):
        weights = [
            short_ref[:, pl.ds(pl.multiple_of(first + part * channels + group * GROUP, GROUP), GROUP)]
            for part in range(3)
        ]
        query = [short_conv(feats[0], halo + at, weights[0]) for at in (0, block_len)]
        query = jnp.concatenate(query, axis=1)
        gated = []
        for place in range(blocks):
            keys, vals = (short_conv(feats[part], place * block_len, weights[part]) for part in (1, 2))
            gated.append((keys * vals).astype(BF16))
        ahead_lo = jnp.concatenate([gated[-1], *gated[:-2]], axis=0)
        gated_far = jnp.concatenate([ahead_lo, jnp.concatenate(gated[:-1], axis=0)], axis=1)
        gated_own = jnp.concatenate(gated[-2:], axis=1)
        span = pl.ds(group * WIDE, WIDE)
        query_ref[:, span] = query
        gated_ref[:, span] = gated_own
        rows = pl.ds(pl.multiple_of(first + group * GROUP, GROUP), GROUP)
        own_grad, mate_grad = grad_ref[rows, :], mate_ref[rows, :]
        grads = jnp.concatenate(
            [jnp.where(on_hi, mate_grad, own_grad), jnp.where(on_hi, own_grad, mate_grad)], axis=0
        )
        grads = lax.dot_general(order_one, grads, (((1,), (1,)), ((), ())), preferred_element_type=F32)
        dconv = query * grads
        dconv_both = jnp.concatenate(halves(dconv), axis=0)
        spec = dot(fwd_ref[...], gated_own)
        spec = spec[:period] + spec[period:]
        spec_ref[:, span] = spec
        left = jnp.concatenate([fwd_ref[...], here_ref[...]], axis=0)
        dspec = dot(jnp.concatenate([left, left], axis=1), dconv_both)
        dstate = dspec[2 * period :]
        dspec = dspec[:period] + dspec[period : 2 * period]
        dstate = dstate[: 4 * modes] + dstate[4 * modes :]
        state = dot(far_ref[...], gated_far)
        state = state[: 4 * modes] + state[4 * modes :]
        left_re, left_im = spec[:block_len], spec[block_len:]
        right_re, right_im = dspec[:block_len], dspec[block_len:]
        leading = lax.broadcasted_iota(jnp.int32, (block_len, WIDE), 0) == 0
        rere, imim = left_re * right_re, left_im * right_im
        cross_re = jnp.where(leading, rere, rere + imim)
        cross_im = jnp.where(leading, imim, left_re * right_im - left_im * right_re)
        cross = jnp.concatenate([cross_re, cross_im], axis=0)
        cross_hi, cross_lo = halves(cross)
        near = near_ref[...]
        terms = dot(near, cross_hi) + dot(near, cross_lo)
        terms = terms[: 2 * modes] + terms[2 * modes :]
        sc, ss, sc1, ss1 = (state[i * modes : (i + 1) * modes] for i in range(4))
        dc, ds, dc1, ds1 = (dstate[i * modes : (i + 1) * modes] for i in range(4))
        grad = terms[:modes] + dc * sc - ds * ss
        slope = terms[modes:] + dc1 * sc + dc * sc1 - ds1 * ss - ds * ss1
        res = res_ref[:, pl.ds(pl.multiple_of(first + group * GROUP, GROUP), GROUP)]
        both = jnp.concatenate([res, res], axis=1)
        state_ref[:modes, span] = both * sc
        state_ref[modes:, span] = -(both * ss)
        grad = grad[:, :GROUP] + grad[:, GROUP:]
        slope = slope[:, :GROUP] + slope[:, GROUP:]
        for side in range(GROUP // LANES):
            at = (group * GROUP + side * LANES) // LANES * modes
            part_ref[pl.ds(at, modes), :] = grad[:, side * LANES : (side + 1) * LANES]
        return rate + jnp.sum(res * slope, axis=1, keepdims=True)

    feats = features(0)
    for group in range(groups):
        ahead = features(group + 1) if group + 1 < groups else None
        rate = one_group(group, feats, rate)
        feats = ahead
    wide = jnp.broadcast_to(rate, (modes, LANES))
    square = jnp.concatenate([wide, jnp.zeros((LANES - modes, LANES), F32)], axis=0).T
    part_ref[pl.ds(half // LANES * modes, SUBLANES), :] = square[:SUBLANES]


def filter_kernel(modes, block_len, spec_ref, res_ref, inv_ref, skip_ref, filt_ref, inv_out, skip_out, inv, copied):
    copies = [
        pltpu.make_async_copy(inv_ref, inv, copied.at[0]),
        pltpu.make_async_copy(skip_ref, skip_out, copied.at[1]),
    ]
    for copy in copies:
        copy.start()
    period = 2 * block_len
    spec_hi, spec_lo = halves(spec_ref[:period, :modes])
    half = res_ref.shape[1] // 2
    res_hi, res_lo = halves(res_ref[:, pl.ds(pl.multiple_of(half_index() * half, half), half)])
    left = jnp.concatenate([spec_hi, spec_hi, spec_lo], axis=1)
    filt_ref[...] = dot(left, jnp.concatenate([res_hi, res_lo, res_hi], axis=0))
    for copy in copies:
        copy.wait()
    inv_out[:, :period] = inv[...].astype(BF16)
    inv_out[:, period:] = spec_ref[period:, : 2 * modes].astype(BF16)


def mixed_kernel(block_len, query_ref, gated_ref, spec_ref, filt_ref, state_ref, inv_ref, skip_ref, own_ref, mate_ref):
    half = filt_ref.shape[1]
    first = half_index() * half
    on_hi = (lax.axis_index("ctx") & 1) == 1
    leading = lax.broadcasted_iota(jnp.int32, (block_len, WIDE), 0) == 0
    order = order_matrix(block_len, True)
    inv = inv_ref[...]
    for group in range(half // GROUP):
        span = pl.ds(group * WIDE, WIDE)
        rows = pl.ds(group * GROUP, GROUP)
        filt = filt_ref[:, rows]
        filt = jnp.concatenate([filt, filt], axis=1)
        skip = skip_ref[:, pl.ds(pl.multiple_of(first + group * GROUP, GROUP), GROUP)]
        left_re, left_im = filt[:block_len], filt[block_len:]
        right_re, right_im = spec_ref[:block_len, span], spec_ref[block_len:, span]
        rere, imim = left_re * right_re, left_im * right_im
        out_re = jnp.where(leading, rere, rere - imim)
        out_im = jnp.where(leading, imim, left_re * right_im + left_im * right_re)
        conv = dot(inv, jnp.concatenate([out_re, out_im, state_ref[:, span]], axis=0).astype(BF16))
        through = jnp.concatenate([skip, skip], axis=1) * gated_ref[:, span].astype(F32)
        mixed = dot(order, (query_ref[:, span] * (conv + through)).astype(BF16))
        low, high = mixed[:, :GROUP], mixed[:, GROUP:]
        own_ref[rows, :] = jnp.where(on_hi, high, low).T.astype(BF16)
        mate_ref[rows, :] = jnp.where(on_hi, low, high).T.astype(BF16)


def call(kernel, outs, scratch, args, cost, spaces=None, out_spaces=None):
    return pl.pallas_call(
        kernel,
        out_shape=[jax.ShapeDtypeStruct(shape, dtype) for shape, dtype in outs],
        in_specs=[pl.BlockSpec(memory_space=space) for space in spaces or [pltpu.VMEM] * len(args)],
        out_specs=[pl.BlockSpec(memory_space=space) for space in out_spaces or [pltpu.VMEM] * len(outs)],
        scratch_shapes=scratch,
        compiler_params=pltpu.CompilerParams(vmem_limit_bytes=40 * 1024 * 1024),
        cost_estimate=pl.CostEstimate(flops=cost[0], bytes_accessed=cost[1], transcendentals=0),
    )(*args)


def result_kernel(modes, part_ref, moved_ref, own_ref, mate_ref, grad_ref, rate_ref, mixed_ref, copied):
    half = own_ref.shape[0]
    second = half_index()
    copies = []
    for at, (source, place) in enumerate(((own_ref, second), (mate_ref, 1 - second))):
        target = mixed_ref.at[pl.ds(pl.multiple_of(place * half, half), half)]
        copies.append(pltpu.make_async_copy(source, target, copied.at[at]))
    for copy in copies:
        copy.start()
    for tile in range(half // LANES):
        rows = pl.ds(tile * modes, modes)
        part, moved = part_ref[rows, :], moved_ref[rows, :]
        grad_ref[:, pl.ds(tile * LANES, LANES)] = jnp.where(second == 1, moved, part)
        grad_ref[:, pl.ds(half + tile * LANES, LANES)] = jnp.where(second == 1, part, moved)
    last = half // LANES * modes
    rate_ref[...] = (part_ref[last : last + 1, :] + moved_ref[last : last + 1, :])[:, :modes]
    for copy in copies:
        copy.wait()


def per_device(token_ids, feature_table, short_weight, residue, rates, skip_gain, grad_out):
    block_len = token_ids.shape[1]
    blocks = lax.axis_size("ctx")
    seq_len = block_len * blocks
    channels, modes = residue.shape
    taps = short_weight.shape[1]
    vocab = feature_table.shape[1]
    period = 2 * block_len
    forward, inverse = dft_tables(block_len)
    wave = mode_constants(block_len, seq_len, modes)
    half = channels // 2

    masks = [mask | 1 for mask in masks_of(blocks)[:0:-1]] + [1]
    moved_ids = [xor_permute(token_ids, ("ctx",), masks[0])]
    mate_grad = xor_permute(grad_out[0], ("ctx",), 1)

    def in_hbm(*arrays):
        return [pltpu.with_memory_space_constraint(array, pltpu.HBM) for array in arrays]

    vmem, hbm = pltpu.VMEM, pltpu.HBM
    ids, short, res, fwd, far, here, near, table_spec = call(
        functools.partial(tables_kernel, modes, block_len, seq_len),
        [
            ((1, block_len), jnp.int32),
            (short_weight.shape[::-1], F32),
            ((modes, channels), F32),
            ((2 * period, block_len), BF16),
            ((8 * modes, seq_len - block_len), BF16),
            ((8 * modes, block_len), BF16),
            ((4 * modes, period), BF16),
            ((period + block_len, LANES), F32),
        ],
        [
            vmem((1, modes), F32),
            vmem((1, LANES), F32),
            vmem(wave.shape, F32),
            vmem(forward.shape, F32),
            pltpu.SemaphoreType.DMA((6,)),
        ],
        in_hbm(
            rates[None],
            jnp.asarray(wave),
            jnp.asarray(forward.astype(np.float32)),
            token_ids,
            residue.T,
            short_weight.T,
        ),
        (10_000_000_000, 40_000_000),
        [hbm] * 6,
    )
    for mask in masks[1:]:
        moved_ids.append(xor_permute(jnp.concatenate([ids, *moved_ids], axis=0), ("ctx",), mask))
    part, query, gated, spec, state = call(
        functools.partial(main_kernel, modes, blocks, block_len, taps, channels),
        [
            ((half // LANES * modes + SUBLANES, LANES), F32),
            ((block_len, channels), F32),
            ((block_len, channels), BF16),
            ((period, channels), F32),
            ((2 * modes, channels), F32),
        ],
        [
            vmem((seq_len, vocab), BF16),
            vmem((blocks, block_len), jnp.int32),
        ],
        [feature_table, short, res, fwd, far, here, near, grad_out[0], mate_grad, ids, *moved_ids],
        (4 * seq_len * vocab * channels, 6_000_000),
    )
    core = lax.axis_size("dp")
    hops = [mask | core for mask in masks_of(blocks * core) if mask != core]
    for hop in hops:
        if hop == hops[0]:
            part, res = lax.optimization_barrier((part, res))
            filt, inv, skip = call(
                functools.partial(filter_kernel, modes, block_len),
                [((period, half), F32), ((block_len, period + 2 * modes), BF16), ((1, channels), F32)],
                [vmem(inverse.shape, F32), pltpu.SemaphoreType.DMA((2,))],
                [table_spec, res, *in_hbm(jnp.asarray(inverse.astype(np.float32)), skip_gain[None])],
                (50_000_000, 1_500_000),
                [vmem, vmem, hbm, hbm],
            )
        if hop == hops[1]:
            part, query = lax.optimization_barrier((part, query))
            mixed_own, mixed_mate = call(
                functools.partial(mixed_kernel, block_len),
                [((half, block_len), BF16)] * 2,
                [],
                [query, gated, spec, filt, state, inv, skip],
                (300_000_000, 3_000_000),
            )
        if hop == hops[2]:
            part, mixed_mate = lax.optimization_barrier((part, mixed_mate))
            mixed_moved = xor_permute(mixed_mate, ("ctx", "dp"), core)
        part = part + xor_permute(part, ("ctx", "dp"), hop)
    grad, rate, mixed = call(
        functools.partial(result_kernel, modes),
        [((modes, channels), F32), ((1, modes), F32), ((channels, block_len), BF16)],
        [pltpu.SemaphoreType.DMA((2,))],
        [part, xor_permute(part, ("ctx", "dp"), core), mixed_own, mixed_moved],
        (0, 800_000),
        out_spaces=[vmem, vmem, hbm],
    )
    return (mixed[None], grad.T, rate[0])


def solution(mesh):
    return jax.shard_map(
        per_device,
        mesh=mesh,
        in_specs=(P("dp", "ctx"), P(), P(), P(), P(), P(), P("dp", None, "ctx")),
        out_specs=(P("dp", None, "ctx"), P(), P()),
        check_vma=False,
    )
```

time: 28.3 us -> 27.2 us (0.961)
  waiting for transfers between devices: 6.64 us -> 8.54 us
  Pallas kernels: 9.41 us -> 7.64 us
  other arithmetic: 0.63 us -> 0.03 us
  starting transfers between devices: 10.6 us -> 10.1 us
    ppermute x7 -> x9, waiting for transfers between devices: 6.64 us -> 8.54 us  [xor_permute(): return lax.ppermute(block, axis, [(i, i ^ mask) for i in range(size)])]
    pallas_call x5, Pallas kernels: 9.41 us -> 7.64 us  [call(): pl.pallas_call(kernel, out_shape=[jax.ShapeDtypeStruct(shape, dtype) for...]
    ppermute x7 -> x9, starting transfers between devices: 10.6 us -> 10.1 us  [xor_permute(): return lax.ppermute(block, axis, [(i, i ^ mask) for i in range(size)])]
    concatenate x6 -> x0, other arithmetic: 0.43 us -> none  [the longest x5 0.42 us: per_device(): jnp.concatenate([part.astype(BF16), upper.astype(BF16), lower.astype(BF16...]
  transfers between devices with their start and end apart: 7 -> 9, of which waited for: 6 -> 6; matrix products, arithmetic and copies ran while one was open for 0% -> 0% of each run, Pallas kernels for 16% -> 12%
where the time goes in v4:
time: 27.2 us; the launch traced here: 27 us
  starting transfers between devices  10.1 us (37%)
  waiting for transfers between devices  8.54 us (31%)
  Pallas kernels  7.64 us (28%)
  between operations  0.69 us (3%)
    ppermute x9, starting transfers between devices, xor_permute(): return lax.ppermute(block, axis, [(i, i ^ mask) for i in range(size)])  10.1 us
    ppermute x9, waiting for transfers between devices, xor_permute(): return lax.ppermute(block, axis, [(i, i ^ mask) for i in range(size)])  8.54 us
    pallas_call x5, Pallas kernels, call(): pl.pallas_call(kernel, out_shape=[jax.ShapeDtypeStruct(shape, dtype) for...  7.64 us
  transfers between devices with their start and end apart: 9, of which 6 were waited for; matrix products, arithmetic and copies ran while one was open for 0% of the time, Pallas kernels for 12%

profile of v4, /device:TPU:0, one launch (start us, length us, event | category | flops | bytes accessed | tf_op | source)
XLA Modules:
  0.0 27.0 jit_solution(2809913185511977491)
XLA Ops:
  0.6 2.5 %collective-permute-start.1 = (s32[1,128]{1,0:T(1,128)}, s32[1,128]{1,0:T(1,128)S(1)}, u32[]{:S(2)}, u32[]{:S(2)}) collective-permute-start(s32[1,128]{1,0:T(1,128)} %refs_3_.1), channel_id=1, source_target_pairs={{0,24},{8,16},{16,8},{24,0},{1,25},{9,17},{17,9},{25,1},{2,26},{10... | collective-permute-start | bytes 1544 | tf_op jit(solution)/shard_map/ppermute | solution.py:22
  3.1 0.7 %collective-permute-start = (bf16[1024,128]{1,0:T(8,128)(2,1)}, bf16[1024,128]{1,0:T(8,128)(2,1)S(1)}, u32[]{:S(2)}, u32[]{:S(2)}) collective-permute-start(bf16[1024,128]{1,0:T(8,128)(2,1)} %bitcast.8), channel_id=1, source_target_pairs={{0,8},{8,0},{16,24},{24,16},{1,9},{9,1},{17,25},{25,17},{2,10},{10... | collective-permute-start | bytes 786440 | tf_op jit(solution)/shard_map/ppermute | solution.py:22
  3.8 0.0 copy-start
  3.8 0.0 copy-start.1
  3.8 1.6 %shard_map.121 = (s32[1,128]{1,0:T(1,128)S(1)}, f32[7,3072]{1,0:T(8,128)S(1)}, f32[16,1024]{1,0:T(8,128)S(1)}, bf16[512,128]{1,0:T(8,128)(2,1)S(1)}, bf16[128,38...) custom-call(f32[1,16]{1,0:T(1,128)} %bitcast.15, ...), custom_call_target="tpu_custom_call" | custom-call | flops 10000000000 | bytes 40000000 | tf_op jit(solution)/shard_map/pallas_call | solution.py:318
  5.4 0.0 collective-permute-done.1.refs_1_
  5.4 0.1 collective-permute-start.2
  5.5 1.1 %collective-permute-done.2.refs_2_ = s32[2,128]{1,0:T(2,128)S(1)} collective-permute-done((s32[2,128]{1,0:T(2,128)S(1)}, s32[2,128]{1,0:T(2,128)S(1)}, u32[]{:S(2)}, u32[]{:S(2)}) %collective-permute-start.2) | collective-permute-done | bytes 1056 | tf_op jit(solution)/shard_map/ppermute | solution.py:22
  6.6 0.0 collective-permute-done.mate_ref
  6.6 0.0 copy-done
  6.6 0.0 copy-done.1
  6.6 3.0 %shard_map.122 = (f32[72,128]{1,0:T(8,128)S(1)}, f32[128,1024]{1,0:T(8,128)S(1)}, bf16[128,1024]{1,0:T(8,128)(2,1)S(1)}, f32[256,1024]{1,0:T(8,128)S(1)}, f32[32,1024]{1,0:T(8,128)S(1)}) custom-call(bf16[3072,512]{1,0:T(8,128)(2,1)S(1)} %copy-done, f32[7,3072]{1,0:T(8,128)S(1)} %get-tuple-element.30.short_ref, f32[16,1024]{1,0:T(8,128)S(1)} %get-tuple-element.45.res_ref, ...), custom_call_target="tpu_custom_call" | custom-call | flops 1073741824 | bytes 6000000 | tf_op jit(solution)/shard_map/pallas_call | solution.py:318
  9.6 1.3 %collective-permute-start.3 = (f32[72,128]{1,0:T(8,128)S(1)}, f32[72,128]{1,0:T(8,128)S(1)}, u32[]{:S(2)}, u32[]{:S(2)}) collective-permute-start(f32[72,128]{1,0:T(8,128)S(1)} %get-tuple-element.38), channel_id=1, source_target_pairs={{0,9},{1,8},{2,11},{3,10},{4,13},{5,12},{6,15},{7,14},{8,1},{9,0},... | collective-permute-start | bytes 110600 | tf_op jit(solution)/shard_map/ppermute | solution.py:22
  10.9 2.2 %collective-permute-done.3 = f32[72,128]{1,0:T(8,128)S(1)} collective-permute-done((f32[72,128]{1,0:T(8,128)S(1)}, f32[72,128]{1,0:T(8,128)S(1)}, u32[]{:S(2)}, u32[]{:S(2)}) %collective-permute-start.3) | collective-permute-done | bytes 36896 | tf_op jit(solution)/shard_map/ppermute | solution.py:22
  13.1 1.3 %collective-permute-start.4 = (f32[72,128]{1,0:T(8,128)S(1)}, f32[72,128]{1,0:T(8,128)S(1)}, u32[]{:S(2)}, u32[]{:S(2)}) collective-permute-start(f32[72,128]{1,0:T(8,128)S(1)} %add.12), channel_id=1, source_target_pairs={{0,10},{1,11},{2,8},{3,9},{4,14},{5,15},{6,12},{7,13},{8,2},{9,3},... | collective-permute-start | bytes 110600 | tf_op jit(solution)/shard_map/ppermute | solution.py:22
  14.4 1.0 %shard_map.123 = (f32[256,512]{1,0:T(8,128)S(1)}, bf16[128,288]{1,0:T(8,128)(2,1)S(1)}, f32[1,1024]{1,0:T(1,128)S(1)}) custom-call(f32[384,128]{1,0:T(8,128)S(1)} %get-tuple-element.44.spec_ref, f32[16,1024]{1,0:T(8,128)S(1)} %get-tuple-element.45.res_ref, f32[128,256]{1,0:T(8,128)} %constant.8.clone.inv_ref, f32[1,1024]{1,0:T(1,128)} %bitcast.10), custom_call_target="tpu_custom_call" | custom-call | flops 50000000 | bytes 1500000 | tf_op jit(solution)/shard_map/pallas_call | solution.py:318
  15.4 0.8 %shard_map.124 = (bf16[512,128]{1,0:T(8,128)(2,1)S(1)}, bf16[512,128]{1,0:T(8,128)(2,1)S(1)}) custom-call(f32[128,1024]{1,0:T(8,128)S(1)} %get-tuple-element.41.query_ref, bf16[128,1024]{1,0:T(8,128)(2,1)S(1)} %get-tuple-element.42.gated_ref, f32[256,1024]{1,0:T(8,128)S(1)} %get-tuple-element.43.spec_ref, f32[256,512]{1,0:T(8,128)S(1)} %get-tuple-element.46.filt_ref, ...), custom_call_target="tpu_custom_call" | custom-call | flops 300000000 | bytes 3000000 | tf_op jit(solution)/shard_map/pallas_call | solution.py:318
  16.2 0.4 %collective-permute-done.4 = f32[72,128]{1,0:T(8,128)S(1)} collective-permute-done((f32[72,128]{1,0:T(8,128)S(1)}, f32[72,128]{1,0:T(8,128)S(1)}, u32[]{:S(2)}, u32[]{:S(2)}) %collective-permute-start.4) | collective-permute-done | bytes 36896 | tf_op jit(solution)/shard_map/ppermute | solution.py:22
  16.6 0.1 collective-permute-start.8
  16.7 2.6 %collective-permute-start.5 = (f32[72,128]{1,0:T(8,128)S(1)}, f32[72,128]{1,0:T(8,128)S(1)}, u32[]{:S(2)}, u32[]{:S(2)}) collective-permute-start(f32[72,128]{1,0:T(8,128)S(1)} %add.13), channel_id=1, source_target_pairs={{0,12},{1,13},{2,14},{3,15},{4,8},{5,9},{6,10},{7,11},{8,4},{9,5},... | collective-permute-start | bytes 110600 | tf_op jit(solution)/shard_map/ppermute | solution.py:22
  19.3 1.7 %collective-permute-done.5 = f32[72,128]{1,0:T(8,128)S(1)} collective-permute-done((f32[72,128]{1,0:T(8,128)S(1)}, f32[72,128]{1,0:T(8,128)S(1)}, u32[]{:S(2)}, u32[]{:S(2)}) %collective-permute-start.5) | collective-permute-done | bytes 36896 | tf_op jit(solution)/shard_map/ppermute | solution.py:22
  21.0 1.3 %collective-permute-start.6 = (f32[72,128]{1,0:T(8,128)S(1)}, f32[72,128]{1,0:T(8,128)S(1)}, u32[]{:S(2)}, u32[]{:S(2)}) collective-permute-start(f32[72,128]{1,0:T(8,128)S(1)} %add.14), channel_id=1, source_target_pairs={{0,24},{1,25},{2,26},{3,27},{4,28},{5,29},{6,30},{7,31},{8,16},{9,... | collective-permute-start | bytes 110600 | tf_op jit(solution)/shard_map/ppermute | solution.py:22
  22.3 2.1 %collective-permute-done.6 = f32[72,128]{1,0:T(8,128)S(1)} collective-permute-done((f32[72,128]{1,0:T(8,128)S(1)}, f32[72,128]{1,0:T(8,128)S(1)}, u32[]{:S(2)}, u32[]{:S(2)}) %collective-permute-start.6) | collective-permute-done | bytes 36896 | tf_op jit(solution)/shard_map/ppermute | solution.py:22
  24.4 0.3 %collective-permute-start.7 = (f32[72,128]{1,0:T(8,128)S(1)}, f32[72,128]{1,0:T(8,128)S(1)}, u32[]{:S(2)}, u32[]{:S(2)}) collective-permute-start(f32[72,128]{1,0:T(8,128)S(1)} %add.15.part_ref), channel_id=1, source_target_pairs={{0,8},{1,9},{2,10},{3,11},{4,12},{5,13},{6,14},{7,15},{8,0},{9,1},... | collective-permute-start | bytes 110600 | tf_op jit(solution)/shard_map/ppermute | solution.py:22
  24.8 0.9 %collective-permute-done.7.moved_ref = f32[72,128]{1,0:T(8,128)S(1)} collective-permute-done((f32[72,128]{1,0:T(8,128)S(1)}, f32[72,128]{1,0:T(8,128)S(1)}, u32[]{:S(2)}, u32[]{:S(2)}) %collective-permute-start.7) | collective-permute-done | bytes 36896 | tf_op jit(solution)/shard_map/ppermute | solution.py:22
  25.7 0.0 collective-permute-done.8.mate_ref
  25.7 1.4 %shard_map.125 = (f32[16,1024]{1,0:T(8,128)}, f32[1,16]{1,0:T(1,128)}, bf16[1024,128]{1,0:T(8,128)(2,1)}) custom-call(f32[72,128]{1,0:T(8,128)S(1)} %add.15.part_ref, f32[72,128]{1,0:T(8,128)S(1)} %collective-permute-done.7.moved_ref, bf16[512,128]{1,0:T(8,128)(2,1)S(1)} %get-tuple-element.52.own_ref, bf16[512,128]{1,0:T(8,128)(2,1)S(1)} %collective-permute-done.8.mate_ref), custom_call_target="tpu_custom_call" | custom-call | bytes 800000 | tf_op jit(solution)/shard_map/pallas_call | solution.py:318
  (5 shorter events, 0.0 us)
Async XLA Ops:
  0.6 4.8 %collective-permute-start.1 = (s32[1,128]{1,0:T(1,128)}, s32[1,128]{1,0:T(1,128)S(1)}, u32[]{:S(2)}, u32[]{:S(2)}) collective-permute-start(s32[1,128]{1,0:T(1,128)} %refs_3_.1), channel_id=1, source_target_pairs={{0,24},{8,16},{16,8},{24,0},{1,25},{9,17},{17,9},{25,1},{2,26},{10... | collective-permute-start | bytes 1544 | tf_op jit(solution)/shard_map/ppermute | solution.py:22
  3.1 3.5 %collective-permute-start = (bf16[1024,128]{1,0:T(8,128)(2,1)}, bf16[1024,128]{1,0:T(8,128)(2,1)S(1)}, u32[]{:S(2)}, u32[]{:S(2)}) collective-permute-start(bf16[1024,128]{1,0:T(8,128)(2,1)} %bitcast.8), channel_id=1, source_target_pairs={{0,8},{8,0},{16,24},{24,16},{1,9},{9,1},{17,25},{25,17},{2,10},{10... | collective-permute-start | bytes 786440 | tf_op jit(solution)/shard_map/ppermute | solution.py:22
  3.8 2.8 %copy-start = (bf16[3072,512]{1,0:T(8,128)(2,1)S(1)}, bf16[3072,512]{1,0:T(8,128)(2,1)}, u32[]{:S(2)}) copy-start(bf16[3072,512]{1,0:T(8,128)(2,1)} %table_ref.1) | copy-start | bytes 9437188
  3.8 2.8 %copy-start.1 = (bf16[1,1024,128]{2,1,0:T(8,128)(2,1)S(1)}, bf16[1,1024,128]{2,1,0:T(8,128)(2,1)}, u32[]{:S(2)}) copy-start(bf16[1,1024,128]{2,1,0:T(8,128)(2,1)} %param.16) | copy-start | bytes 786436
  5.4 1.2 %collective-permute-start.2 = (s32[2,128]{1,0:T(2,128)S(1)}, s32[2,128]{1,0:T(2,128)S(1)}, u32[]{:S(2)}, u32[]{:S(2)}) collective-permute-start(s32[2,128]{1,0:T(2,128)S(1)} %pad_add_fusion), channel_id=1, source_target_pairs={{0,8},{8,0},{16,24},{24,16},{1,9},{9,1},{17,25},{25,17},{2,10},{10... | collective-permute-start | bytes 3080 | tf_op jit(solution)/shard_map/ppermute | solution.py:22
  9.6 3.5 %collective-permute-start.3 = (f32[72,128]{1,0:T(8,128)S(1)}, f32[72,128]{1,0:T(8,128)S(1)}, u32[]{:S(2)}, u32[]{:S(2)}) collective-permute-start(f32[72,128]{1,0:T(8,128)S(1)} %get-tuple-element.38), channel_id=1, source_target_pairs={{0,9},{1,8},{2,11},{3,10},{4,13},{5,12},{6,15},{7,14},{8,1},{9,0},... | collective-permute-start | bytes 110600 | tf_op jit(solution)/shard_map/ppermute | solution.py:22
  13.1 3.5 %collective-permute-start.4 = (f32[72,128]{1,0:T(8,128)S(1)}, f32[72,128]{1,0:T(8,128)S(1)}, u32[]{:S(2)}, u32[]{:S(2)}) collective-permute-start(f32[72,128]{1,0:T(8,128)S(1)} %add.12), channel_id=1, source_target_pairs={{0,10},{1,11},{2,8},{3,9},{4,14},{5,15},{6,12},{7,13},{8,2},{9,3},... | collective-permute-start | bytes 110600 | tf_op jit(solution)/shard_map/ppermute | solution.py:22
  16.6 9.1 %collective-permute-start.8 = (bf16[512,128]{1,0:T(8,128)(2,1)S(1)}, bf16[512,128]{1,0:T(8,128)(2,1)S(1)}, u32[]{:S(2)}, u32[]{:S(2)}) collective-permute-start(bf16[512,128]{1,0:T(8,128)(2,1)S(1)} %get-tuple-element.53), channel_id=1, source_target_pairs={{0,8},{1,9},{2,10},{3,11},{4,12},{5,13},{6,14},{7,15},{8,0},{9,1},... | collective-permute-start | bytes 393224 | tf_op jit(solution)/shard_map/ppermute | solution.py:22
  16.7 4.3 %collective-permute-start.5 = (f32[72,128]{1,0:T(8,128)S(1)}, f32[72,128]{1,0:T(8,128)S(1)}, u32[]{:S(2)}, u32[]{:S(2)}) collective-permute-start(f32[72,128]{1,0:T(8,128)S(1)} %add.13), channel_id=1, source_target_pairs={{0,12},{1,13},{2,14},{3,15},{4,8},{5,9},{6,10},{7,11},{8,4},{9,5},... | collective-permute-start | bytes 110600 | tf_op jit(solution)/shard_map/ppermute | solution.py:22
  21.0 3.4 %collective-permute-start.6 = (f32[72,128]{1,0:T(8,128)S(1)}, f32[72,128]{1,0:T(8,128)S(1)}, u32[]{:S(2)}, u32[]{:S(2)}) collective-permute-start(f32[72,128]{1,0:T(8,128)S(1)} %add.14), channel_id=1, source_target_pairs={{0,24},{1,25},{2,26},{3,27},{4,28},{5,29},{6,30},{7,31},{8,16},{9,... | collective-permute-start | bytes 110600 | tf_op jit(solution)/shard_map/ppermute | solution.py:22
  24.4 1.2 %collective-permute-start.7 = (f32[72,128]{1,0:T(8,128)S(1)}, f32[72,128]{1,0:T(8,128)S(1)}, u32[]{:S(2)}, u32[]{:S(2)}) collective-permute-start(f32[72,128]{1,0:T(8,128)S(1)} %add.15.part_ref), channel_id=1, source_target_pairs={{0,8},{1,9},{2,10},{3,11},{4,12},{5,13},{6,14},{7,15},{8,0},{9,1},... | collective-permute-start | bytes 110600 | tf_op jit(solution)/shard_map/ppermute | solution.py:22

commit v5 on v4

--- a/solution.py
+++ b/solution.py
@@ -91,54 +91,55 @@
     return np.pad(wave, ((0, 0), (0, LANES - wave.shape[1]))).astype(np.float32)
 
 
-def tables_kernel(modes, block_len, seq_len, *refs):
-    sources, outs, scratch = refs[:6], refs[6:14], refs[14:]
-    ids_out, short_out, res_out, fwd_out, far_ref, here_ref, near_ref, spec_ref = outs
-    few, rate_row, wave, fwd, copied = scratch
-    targets = [few, wave, fwd, ids_out, res_out, short_out]
-    pairs = list(zip(sources, targets, strict=True))
+def inputs_kernel(modes, block_len, seq_len, *refs):
+    sources, outs, scratch = refs[:7], refs[7:14], refs[14:]
+    ids_out, short_out, res_out, fwd_out, table_ref, keep_ref, send_ref = outs
+    few, rate_row, wave, copied = scratch
+    half = keep_ref.shape[0]
+    second = half_index()
+    grads = [sources[6].at[pl.ds(pl.multiple_of(place * half, half), half)] for place in (1 - second, second)]
+    targets = [few, wave, send_ref, fwd_out, ids_out, res_out, short_out, keep_ref]
+    pairs = zip([*sources[:2], grads[0], *sources[2:6], grads[1]], targets, strict=True)
     copies = [pltpu.make_async_copy(*pair, copied.at[i]) for i, pair in enumerate(pairs)]
     for copy in copies:
         copy.start()
     rate_row[...] = jnp.zeros_like(rate_row)
-    period = 2 * block_len
-    body = seq_len - block_len
     copies[0].wait()
     rate_row[:, :modes] = few[...]
     rates = rate_row[...]
     for shift in (modes, 2 * modes):
         rates = rates + pltpu.roll(rates, shift, 1)
-
-    def decay_of(at, length):
+    start = 0
+    decays = []
+    for at, length in enumerate((2 * block_len, seq_len - block_len, block_len)):
         delays = row_delays(block_len, seq_len, lax.broadcasted_iota(jnp.int32, (length, LANES), 0))
-        delay = delays[at](delays[3]).astype(F32)
-        return jnp.exp(delay * (-1.0 / seq_len) * rates)
-
-    near = decay_of(0, period)
-    far = decay_of(1, body)
-    here = decay_of(2, block_len)
+        decays.append(jnp.exp(delays[at](delays[3]).astype(F32) * (-1.0 / seq_len) * rates))
     copies[1].wait()
-    near = near * wave[:period]
-    far = far * wave[period : period + body]
-    here = here * wave[period + body :]
+    for decay in decays:
+        rows = pl.ds(start, decay.shape[0])
+        table_ref[rows, :] = decay * wave[rows, :]
+        start += decay.shape[0]
+    for copy in copies[2:]:
+        copy.wait()
+
+
+def tables_kernel(modes, block_len, table_ref, fwd_ref, fwd_out, far_ref, here_ref, near_ref, spec_ref):
+    period = 2 * block_len
     used = 4 * modes
-    near_hi, near_lo = halves(near)
-    copies[2].wait()
-    fwd_hi, fwd_lo = halves(fwd[...])
+    near_hi, near_lo = halves(table_ref[:period, :])
+    fwd_hi, fwd_lo = halves(fwd_ref[...])
     spec = dot(fwd_hi, near_hi) + dot(fwd_hi, near_lo) + dot(fwd_lo, near_hi)
     fwd_out[:period, :] = fwd_hi[:, :block_len]
     fwd_out[period:, :] = fwd_lo[:, :block_len]
-    spec_ref[:period, :] = spec
-    spec_ref[period:, :] = here
-    far_ref[...] = jnp.concatenate(halves(far.T[:used]), axis=0)
-    here_ref[...] = jnp.concatenate(halves(here.T[:used]), axis=0)
+    spec_ref[...] = spec
+    body = table_ref.shape[0] - block_len
+    far_ref[...] = jnp.concatenate(halves(table_ref[period:body, :].T[:used]), axis=0)
+    here_ref[...] = jnp.concatenate(halves(table_ref[body:, :].T[:used]), axis=0)
     place = lax.broadcasted_iota(jnp.int32, (period, LANES), 0)
     weight = jnp.where(lax.rem(place, block_len) == 0, 1.0 / period, 2.0 / period)
     spec_t = (spec * weight).T
     grad_rows = jnp.concatenate([spec_t[:modes], spec_t[2 * modes : 3 * modes]], axis=0)
     near_ref[...] = jnp.concatenate(halves(grad_rows), axis=0)
-    for copy in copies[3:]:
-        copy.wait()
 
 
 def main_kernel(modes, blocks, block_len, taps, channels, table_ref, short_ref, res_ref, fwd_ref, far_ref, here_ref,
@@ -215,7 +216,7 @@
         span = pl.ds(group * WIDE, WIDE)
         query_ref[:, span] = query
         gated_ref[:, span] = gated_own
-        rows = pl.ds(pl.multiple_of(first + group * GROUP, GROUP), GROUP)
+        rows = pl.ds(group * GROUP, GROUP)
         own_grad, mate_grad = grad_ref[rows, :], mate_ref[rows, :]
         grads = jnp.concatenate(
             [jnp.where(on_hi, mate_grad, own_grad), jnp.where(on_hi, own_grad, mate_grad)], axis=0
@@ -269,7 +270,7 @@
     part_ref[pl.ds(half // LANES * modes, SUBLANES), :] = square[:SUBLANES]
 
 
-def filter_kernel(modes, block_len, spec_ref, res_ref, inv_ref, skip_ref, filt_ref, inv_out, skip_out, inv, copied):
+def filter_kernel(modes, block_len, spec_ref, table_ref, res_ref, inv_ref, skip_ref, filt_ref, inv_out, skip_out, inv, copied):
     copies = [
         pltpu.make_async_copy(inv_ref, inv, copied.at[0]),
         pltpu.make_async_copy(skip_ref, skip_out, copied.at[1]),
@@ -277,15 +278,16 @@
     for copy in copies:
         copy.start()
     period = 2 * block_len
-    spec_hi, spec_lo = halves(spec_ref[:period, :modes])
+    spec_hi, spec_lo = halves(spec_ref[:, :modes])
     half = res_ref.shape[1] // 2
     res_hi, res_lo = halves(res_ref[:, pl.ds(pl.multiple_of(half_index() * half, half), half)])
     left = jnp.concatenate([spec_hi, spec_hi, spec_lo], axis=1)
     filt_ref[...] = dot(left, jnp.concatenate([res_hi, res_lo, res_hi], axis=0))
     for copy in copies:
         copy.wait()
-    inv_out[:, :period] = inv[...].astype(BF16)
-    inv_out[:, period:] = spec_ref[period:, : 2 * modes].astype(BF16)
+    here = table_ref[table_ref.shape[0] - block_len :, : 2 * modes]
+    inv_hi, inv_lo = halves(jnp.concatenate([inv[...], here], axis=1))
+    inv_out[...] = jnp.concatenate([inv_hi, inv_lo], axis=0)
 
 
 def mixed_kernel(block_len, query_ref, gated_ref, spec_ref, filt_ref, state_ref, inv_ref, skip_ref, own_ref, mate_ref):
@@ -306,7 +308,9 @@
         rere, imim = left_re * right_re, left_im * right_im
         out_re = jnp.where(leading, rere, rere - imim)
         out_im = jnp.where(leading, imim, left_re * right_im + left_im * right_re)
-        conv = dot(inv, jnp.concatenate([out_re, out_im, state_ref[:, span]], axis=0).astype(BF16))
+        spec_hi, spec_lo = halves(jnp.concatenate([out_re, out_im, state_ref[:, span]], axis=0))
+        conv = dot(inv, spec_hi)
+        conv = conv[:block_len] + conv[block_len:] + dot(inv[:block_len], spec_lo)
         through = jnp.concatenate([skip, skip], axis=1) * gated_ref[:, span].astype(F32)
         mixed = dot(order, (query_ref[:, span] * (conv + through)).astype(BF16))
         low, high = mixed[:, :GROUP], mixed[:, GROUP:]
@@ -326,7 +330,7 @@
     )(*args)
 
 
-def result_kernel(modes, part_ref, moved_ref, own_ref, mate_ref, grad_ref, rate_ref, mixed_ref, copied):
+def output_kernel(own_ref, mate_ref, mixed_ref, copied):
     half = own_ref.shape[0]
     second = half_index()
     copies = []
@@ -335,6 +339,13 @@
         copies.append(pltpu.make_async_copy(source, target, copied.at[at]))
     for copy in copies:
         copy.start()
+    for copy in copies:
+        copy.wait()
+
+
+def result_kernel(modes, part_ref, moved_ref, grad_ref, rate_ref):
+    half = grad_ref.shape[1] // 2
+    second = half_index()
     for tile in range(half // LANES):
         rows = pl.ds(tile * modes, modes)
         part, moved = part_ref[rows, :], moved_ref[rows, :]
@@ -342,8 +353,6 @@
         grad_ref[:, pl.ds(half + tile * LANES, LANES)] = jnp.where(second == 1, part, moved)
     last = half // LANES * modes
     rate_ref[...] = (part_ref[last : last + 1, :] + moved_ref[last : last + 1, :])[:, :modes]
-    for copy in copies:
-        copy.wait()
 
 
 def per_device(token_ids, feature_table, short_weight, residue, rates, skip_gain, grad_out):
@@ -360,30 +369,27 @@
 
     masks = [mask | 1 for mask in masks_of(blocks)[:0:-1]] + [1]
     moved_ids = [xor_permute(token_ids, ("ctx",), masks[0])]
-    mate_grad = xor_permute(grad_out[0], ("ctx",), 1)
 
     def in_hbm(*arrays):
         return [pltpu.with_memory_space_constraint(array, pltpu.HBM) for array in arrays]
 
     vmem, hbm = pltpu.VMEM, pltpu.HBM
-    ids, short, res, fwd, far, here, near, table_spec = call(
-        functools.partial(tables_kernel, modes, block_len, seq_len),
+    ids, short, res, forward, table, keep_grad, send_grad = call(
+        functools.partial(inputs_kernel, modes, block_len, seq_len),
         [
             ((1, block_len), jnp.int32),
             (short_weight.shape[::-1], F32),
             ((modes, channels), F32),
-            ((2 * period, block_len), BF16),
-            ((8 * modes, seq_len - block_len), BF16),
-            ((8 * modes, block_len), BF16),
-            ((4 * modes, period), BF16),
-            ((period + block_len, LANES), F32),
+            (forward.shape, F32),
+            (wave.shape, F32),
+            ((half, block_len), BF16),
+            ((half, block_len), BF16),
         ],
         [
             vmem((1, modes), F32),
             vmem((1, LANES), F32),
             vmem(wave.shape, F32),
-            vmem(forward.shape, F32),
-            pltpu.SemaphoreType.DMA((6,)),
+            pltpu.SemaphoreType.DMA((8,)),
         ],
         in_hbm(
             rates[None],
@@ -392,12 +398,30 @@
             token_ids,
             residue.T,
             short_weight.T,
+            grad_out[0],
         ),
         (10_000_000_000, 40_000_000),
-        [hbm] * 6,
+        [hbm] * 7,
     )
+    mate_grad = xor_permute(send_grad, ("ctx",), 1)
     for mask in masks[1:]:
-        moved_ids.append(xor_permute(jnp.concatenate([ids, *moved_ids], axis=0), ("ctx",), mask))
+        known = jnp.concatenate([ids, *moved_ids], axis=0)
+        if mask == masks[-1]:
+            known, table = lax.optimization_barrier((known, table))
+        moved_ids.append(xor_permute(known, ("ctx",), mask))
+    fwd, far, here, near, table_spec = call(
+        functools.partial(tables_kernel, modes, block_len),
+        [
+            ((2 * period, block_len), BF16),
+            ((8 * modes, seq_len - block_len), BF16),
+            ((8 * modes, block_len), BF16),
+            ((4 * modes, period), BF16),
+            ((period, LANES), F32),
+        ],
+        [],
+        [table, forward],
+        (300_000_000, 1_000_000),
+    )
     part, query, gated, spec, state = call(
         functools.partial(main_kernel, modes, blocks, block_len, taps, channels),
         [
@@ -411,7 +435,7 @@
             vmem((seq_len, vocab), BF16),
             vmem((blocks, block_len), jnp.int32),
         ],
-        [feature_table, short, res, fwd, far, here, near, grad_out[0], mate_grad, ids, *moved_ids],
+        [feature_table, short, res, fwd, far, here, near, keep_grad, mate_grad, ids, *moved_ids],
         (4 * seq_len * vocab * channels, 6_000_000),
     )
     core = lax.axis_size("dp")
@@ -421,14 +445,14 @@
             part, res = lax.optimization_barrier((part, res))
             filt, inv, skip = call(
                 functools.partial(filter_kernel, modes, block_len),
-                [((period, half), F32), ((block_len, period + 2 * modes), BF16), ((1, channels), F32)],
+                [((period, half), F32), ((2 * block_len, period + 2 * modes), BF16), ((1, channels), F32)],
                 [vmem(inverse.shape, F32), pltpu.SemaphoreType.DMA((2,))],
-                [table_spec, res, *in_hbm(jnp.asarray(inverse.astype(np.float32)), skip_gain[None])],
+                [table_spec, table, res, *in_hbm(jnp.asarray(inverse.astype(np.float32)), skip_gain[None])],
                 (50_000_000, 1_500_000),
-                [vmem, vmem, hbm, hbm],
+                [vmem, vmem, vmem, hbm, hbm],
             )
         if hop == hops[1]:
-            part, query = lax.optimization_barrier((part, query))
+            part, query, filt = lax.optimization_barrier((part, query, filt))
             mixed_own, mixed_mate = call(
                 functools.partial(mixed_kernel, block_len),
                 [((half, block_len), BF16)] * 2,
@@ -439,14 +463,24 @@
         if hop == hops[2]:
             part, mixed_mate = lax.optimization_barrier((part, mixed_mate))
             mixed_moved = xor_permute(mixed_mate, ("ctx", "dp"), core)
+        if hop == hops[3]:
+            part, mixed_moved = lax.optimization_barrier((part, mixed_moved))
+            (mixed,) = call(
+                output_kernel,
+                [((channels, block_len), BF16)],
+                [pltpu.SemaphoreType.DMA((2,))],
+                [mixed_own, mixed_moved],
+                (0, 800_000),
+                out_spaces=[hbm],
+            )
         part = part + xor_permute(part, ("ctx", "dp"), hop)
-    grad, rate, mixed = call(
+    part, mixed = lax.optimization_barrier((part, mixed))
+    grad, rate = call(
         functools.partial(result_kernel, modes),
-        [((modes, channels), F32), ((1, modes), F32), ((channels, block_len), BF16)],
-        [pltpu.SemaphoreType.DMA((2,))],
-        [part, xor_permute(part, ("ctx", "dp"), core), mixed_own, mixed_moved],
-        (0, 800_000),
-        out_spaces=[vmem, vmem, hbm],
+        [((modes, channels), F32), ((1, modes), F32)],
+        [],
+        [part, xor_permute(part, ("ctx", "dp"), core)],
+        (0, 200_000),
     )
     return (mixed[None], grad.T, rate[0])
 

time: 27.2 us -> 26.4 us (0.971)
  waiting for transfers between devices: 8.54 us -> 7.08 us
  Pallas kernels: 7.64 us -> 8.09 us
  starting transfers between devices: 10.1 us -> 10.4 us
    ppermute x9, waiting for transfers between devices: 8.54 us -> 7.08 us  [xor_permute(): return lax.ppermute(block, axis, [(i, i ^ mask) for i in range(size)])]
    pallas_call x5 -> x7, Pallas kernels: 7.64 us -> 8.09 us  [call(): pl.pallas_call(kernel, out_shape=[jax.ShapeDtypeStruct(shape, dtype) for...]
  transfers between devices with their start and end apart: 9 -> 9, of which waited for: 6 -> 6; matrix products, arithmetic and copies ran while one was open for 0% -> 0% of each run, Pallas kernels for 12% -> 17%
where the time goes in v5:
time: 26.4 us; the launch traced here: 26.2 us
  starting transfers between devices  10.4 us (39%)
  Pallas kernels  8.09 us (31%)
  waiting for transfers between devices  7.08 us (27%)
  between operations  0.69 us (3%)
    ppermute x9, starting transfers between devices, xor_permute(): return lax.ppermute(block, axis, [(i, i ^ mask) for i in range(size)])  10.4 us
    pallas_call x7, Pallas kernels, call(): pl.pallas_call(kernel, out_shape=[jax.ShapeDtypeStruct(shape, dtype) for...  8.09 us
    ppermute x9, waiting for transfers between devices, xor_permute(): return lax.ppermute(block, axis, [(i, i ^ mask) for i in range(size)])  7.08 us
  transfers between devices with their start and end apart: 9, of which 6 were waited for; matrix products, arithmetic and copies ran while one was open for 0% of the time, Pallas kernels for 17%

profile of v5, /device:TPU:0, one launch (start us, length us, event | category | flops | bytes accessed | tf_op | source)
XLA Modules:
  0.0 26.2 jit_solution(3079347029348392386)
XLA Ops:
  0.6 2.5 %collective-permute-start = (s32[1,128]{1,0:T(1,128)}, s32[1,128]{1,0:T(1,128)S(1)}, u32[]{:S(2)}, u32[]{:S(2)}) collective-permute-start(s32[1,128]{1,0:T(1,128)} %refs_3_.1), channel_id=1, source_target_pairs={{0,24},{8,16},{16,8},{24,0},{1,25},{9,17},{17,9},{25,1},{2,26},{10... | collective-permute-start | bytes 1544 | tf_op jit(solution)/shard_map/ppermute | solution.py:22
  3.1 0.0 copy-start
  3.1 1.5 %shard_map.121 = (s32[1,128]{1,0:T(1,128)S(1)}, f32[7,3072]{1,0:T(8,128)S(1)}, f32[16,1024]{1,0:T(8,128)S(1)}, f32[256,256]{1,0:T(8,128)S(1)}, f32[768,128]{1,0:...) custom-call(f32[1,16]{1,0:T(1,128)} %bitcast.14, f32[768,128]{1,0:T(8,128)} %constant.6.clone.refs_1_, ...), custom_call_target="tpu_custom_call" | custom-call | flops 10000000000 | bytes 40000000 | tf_op jit(solution)/shard_map/pallas_call | solution.py:322
  4.6 0.7 %collective-permute-start.1 = (bf16[512,128]{1,0:T(8,128)(2,1)S(1)}, bf16[512,128]{1,0:T(8,128)(2,1)S(1)}, u32[]{:S(2)}, u32[]{:S(2)}) collective-permute-start(bf16[512,128]{1,0:T(8,128)(2,1)S(1)} %get-tuple-element.51), channel_id=1, source_target_pairs={{0,8},{8,0},{16,24},{24,16},{1,9},{9,1},{17,25},{25,17},{2,10},{10... | collective-permute-start | bytes 393224 | tf_op jit(solution)/shard_map/ppermute | solution.py:22
  5.3 0.0 collective-permute-done.refs_1_
  5.3 0.1 collective-permute-start.2
  5.4 0.3 %shard_map.122 = (bf16[512,128]{1,0:T(8,128)(2,1)S(1)}, bf16[128,384]{1,0:T(8,128)(2,1)S(1)}, bf16[128,128]{1,0:T(8,128)(2,1)S(1)}, bf16[64,256]{1,0:T(8,128)(2,1)S(1)}, f32[256,128]{1,0:T(8,128)S(1)}) custom-call(f32[768,128]{1,0:T(8,128)S(1)} %get-tuple-element.44.table_ref, f32[256,256]{1,0:T(8,128)S(1)} %get-tuple-element.45.fwd_ref), custom_call_target="tpu_custom_call" | custom-call | flops 300000000 | bytes 1000000 | tf_op jit(solution)/shard_map/pallas_call | solution.py:322
  5.7 0.8 %collective-permute-done.2.refs_2_ = s32[2,128]{1,0:T(2,128)S(1)} collective-permute-done((s32[2,128]{1,0:T(2,128)S(1)}, s32[2,128]{1,0:T(2,128)S(1)}, u32[]{:S(2)}, u32[]{:S(2)}) %collective-permute-start.2) | collective-permute-done | bytes 1056 | tf_op jit(solution)/shard_map/ppermute | solution.py:22
  6.5 0.0 collective-permute-done.1.mate_ref
  6.5 0.0 copy-done
  6.5 2.9 %shard_map.123 = (f32[72,128]{1,0:T(8,128)S(1)}, f32[128,1024]{1,0:T(8,128)S(1)}, bf16[128,1024]{1,0:T(8,128)(2,1)S(1)}, f32[256,1024]{1,0:T(8,128)S(1)}, f32[32,1024]{1,0:T(8,128)S(1)}) custom-call(bf16[3072,512]{1,0:T(8,128)(2,1)S(1)} %copy-done, f32[7,3072]{1,0:T(8,128)S(1)} %get-tuple-element.40.short_ref, f32[16,1024]{1,0:T(8,128)S(1)} %get-tuple-element.57.res_ref, ...), custom_call_target="tpu_custom_call" | custom-call | flops 1073741824 | bytes 6000000 | tf_op jit(solution)/shard_map/pallas_call | solution.py:322
  9.5 1.3 %collective-permute-start.3 = (f32[72,128]{1,0:T(8,128)S(1)}, f32[72,128]{1,0:T(8,128)S(1)}, u32[]{:S(2)}, u32[]{:S(2)}) collective-permute-start(f32[72,128]{1,0:T(8,128)S(1)} %get-tuple-element.54), channel_id=1, source_target_pairs={{0,9},{1,8},{2,11},{3,10},{4,13},{5,12},{6,15},{7,14},{8,1},{9,0},... | collective-permute-start | bytes 110600 | tf_op jit(solution)/shard_map/ppermute | solution.py:22
  10.8 1.0 %shard_map.124 = (f32[256,512]{1,0:T(8,128)S(1)}, bf16[256,288]{1,0:T(8,128)(2,1)S(1)}, f32[1,1024]{1,0:T(1,128)S(1)}) custom-call(f32[256,128]{1,0:T(8,128)S(1)} %get-tuple-element.56.spec_ref, f32[768,128]{1,0:T(8,128)S(1)} %get-tuple-element.44.table_ref, f32[16,1024]{1,0:T(8,128)S(1)} %get-tuple-element.57.res_ref, f32[128,256]{1,0:T(8,128)} %constant.8.clone.inv_ref, ...), custom_call_target="tpu_custom_call" | custom-call | flops 50000000 | bytes 1500000 | tf_op jit(solution)/shard_map/pallas_call | solution.py:322
  11.8 1.2 %collective-permute-done.3 = f32[72,128]{1,0:T(8,128)S(1)} collective-permute-done((f32[72,128]{1,0:T(8,128)S(1)}, f32[72,128]{1,0:T(8,128)S(1)}, u32[]{:S(2)}, u32[]{:S(2)}) %collective-permute-start.3) | collective-permute-done | bytes 36896 | tf_op jit(solution)/shard_map/ppermute | solution.py:22
  13.0 1.3 %collective-permute-start.4 = (f32[72,128]{1,0:T(8,128)S(1)}, f32[72,128]{1,0:T(8,128)S(1)}, u32[]{:S(2)}, u32[]{:S(2)}) collective-permute-start(f32[72,128]{1,0:T(8,128)S(1)} %add.12), channel_id=1, source_target_pairs={{0,10},{1,11},{2,8},{3,9},{4,14},{5,15},{6,12},{7,13},{8,2},{9,3},... | collective-permute-start | bytes 110600 | tf_op jit(solution)/shard_map/ppermute | solution.py:22
  14.3 1.1 %shard_map.125 = (bf16[512,128]{1,0:T(8,128)(2,1)S(1)}, bf16[512,128]{1,0:T(8,128)(2,1)S(1)}) custom-call(f32[128,1024]{1,0:T(8,128)S(1)} %get-tuple-element.60.query_ref, bf16[128,1024]{1,0:T(8,128)(2,1)S(1)} %get-tuple-element.61.gated_ref, f32[256,1024]{1,0:T(8,128)S(1)} %get-tuple-element.62.spec_ref, f32[256,512]{1,0:T(8,128)S(1)} %get-tuple-element.63.filt_ref, ...), custom_call_target="tpu_custom_call" | custom-call | flops 300000000 | bytes 3000000 | tf_op jit(solution)/shard_map/pallas_call | solution.py:322
  15.3 1.1 %collective-permute-done.4 = f32[72,128]{1,0:T(8,128)S(1)} collective-permute-done((f32[72,128]{1,0:T(8,128)S(1)}, f32[72,128]{1,0:T(8,128)S(1)}, u32[]{:S(2)}, u32[]{:S(2)}) %collective-permute-start.4) | collective-permute-done | bytes 36896 | tf_op jit(solution)/shard_map/ppermute | solution.py:22
  16.5 0.1 collective-permute-start.6
  16.6 2.6 %collective-permute-start.5 = (f32[72,128]{1,0:T(8,128)S(1)}, f32[72,128]{1,0:T(8,128)S(1)}, u32[]{:S(2)}, u32[]{:S(2)}) collective-permute-start(f32[72,128]{1,0:T(8,128)S(1)} %add.13), channel_id=1, source_target_pairs={{0,12},{1,13},{2,14},{3,15},{4,8},{5,9},{6,10},{7,11},{8,4},{9,5},... | collective-permute-start | bytes 110600 | tf_op jit(solution)/shard_map/ppermute | solution.py:22
  19.2 1.7 %collective-permute-done.5 = f32[72,128]{1,0:T(8,128)S(1)} collective-permute-done((f32[72,128]{1,0:T(8,128)S(1)}, f32[72,128]{1,0:T(8,128)S(1)}, u32[]{:S(2)}, u32[]{:S(2)}) %collective-permute-start.5) | collective-permute-done | bytes 36896 | tf_op jit(solution)/shard_map/ppermute | solution.py:22
  20.9 0.0 collective-permute-done.6.mate_ref
  20.9 1.4 %collective-permute-start.7 = (f32[72,128]{1,0:T(8,128)S(1)}, f32[72,128]{1,0:T(8,128)S(1)}, u32[]{:S(2)}, u32[]{:S(2)}) collective-permute-start(f32[72,128]{1,0:T(8,128)S(1)} %add.14), channel_id=1, source_target_pairs={{0,24},{1,25},{2,26},{3,27},{4,28},{5,29},{6,30},{7,31},{8,16},{9,... | collective-permute-start | bytes 110600 | tf_op jit(solution)/shard_map/ppermute | solution.py:22
  22.3 0.7 %shard_map.126 = bf16[1024,128]{1,0:T(8,128)(2,1)} custom-call(bf16[512,128]{1,0:T(8,128)(2,1)S(1)} %get-tuple-element.71.own_ref, bf16[512,128]{1,0:T(8,128)(2,1)S(1)} %collective-permute-done.6.mate_ref), custom_call_target="tpu_custom_call" | custom-call | bytes 800000 | tf_op jit(solution)/shard_map/pallas_call | solution.py:322
  23.0 1.3 %collective-permute-done.7 = f32[72,128]{1,0:T(8,128)S(1)} collective-permute-done((f32[72,128]{1,0:T(8,128)S(1)}, f32[72,128]{1,0:T(8,128)S(1)}, u32[]{:S(2)}, u32[]{:S(2)}) %collective-permute-start.7) | collective-permute-done | bytes 36896 | tf_op jit(solution)/shard_map/ppermute | solution.py:22
  24.4 0.3 %collective-permute-start.8 = (f32[72,128]{1,0:T(8,128)S(1)}, f32[72,128]{1,0:T(8,128)S(1)}, u32[]{:S(2)}, u32[]{:S(2)}) collective-permute-start(f32[72,128]{1,0:T(8,128)S(1)} %add.15.part_ref), channel_id=1, source_target_pairs={{0,8},{1,9},{2,10},{3,11},{4,12},{5,13},{6,14},{7,15},{8,0},{9,1},... | collective-permute-start | bytes 110600 | tf_op jit(solution)/shard_map/ppermute | solution.py:22
  24.7 0.9 %collective-permute-done.8.moved_ref = f32[72,128]{1,0:T(8,128)S(1)} collective-permute-done((f32[72,128]{1,0:T(8,128)S(1)}, f32[72,128]{1,0:T(8,128)S(1)}, u32[]{:S(2)}, u32[]{:S(2)}) %collective-permute-start.8) | collective-permute-done | bytes 36896 | tf_op jit(solution)/shard_map/ppermute | solution.py:22
  25.6 0.6 %shard_map.127 = (f32[16,1024]{1,0:T(8,128)}, f32[1,16]{1,0:T(1,128)}) custom-call(f32[72,128]{1,0:T(8,128)S(1)} %add.15.part_ref, f32[72,128]{1,0:T(8,128)S(1)} %collective-permute-done.8.moved_ref), custom_call_target="tpu_custom_call" | custom-call | bytes 200000 | tf_op jit(solution)/shard_map/pallas_call | solution.py:322
  (5 shorter events, 0.0 us)
Async XLA Ops:
  0.6 4.7 %collective-permute-start = (s32[1,128]{1,0:T(1,128)}, s32[1,128]{1,0:T(1,128)S(1)}, u32[]{:S(2)}, u32[]{:S(2)}) collective-permute-start(s32[1,128]{1,0:T(1,128)} %refs_3_.1), channel_id=1, source_target_pairs={{0,24},{8,16},{16,8},{24,0},{1,25},{9,17},{17,9},{25,1},{2,26},{10... | collective-permute-start | bytes 1544 | tf_op jit(solution)/shard_map/ppermute | solution.py:22
  3.1 3.4 %copy-start = (bf16[3072,512]{1,0:T(8,128)(2,1)S(1)}, bf16[3072,512]{1,0:T(8,128)(2,1)}, u32[]{:S(2)}) copy-start(bf16[3072,512]{1,0:T(8,128)(2,1)} %table_ref.1) | copy-start | bytes 9437188
  4.6 2.0 %collective-permute-start.1 = (bf16[512,128]{1,0:T(8,128)(2,1)S(1)}, bf16[512,128]{1,0:T(8,128)(2,1)S(1)}, u32[]{:S(2)}, u32[]{:S(2)}) collective-permute-start(bf16[512,128]{1,0:T(8,128)(2,1)S(1)} %get-tuple-element.51), channel_id=1, source_target_pairs={{0,8},{8,0},{16,24},{24,16},{1,9},{9,1},{17,25},{25,17},{2,10},{10... | collective-permute-start | bytes 393224 | tf_op jit(solution)/shard_map/ppermute | solution.py:22
  5.3 1.2 %collective-permute-start.2 = (s32[2,128]{1,0:T(2,128)S(1)}, s32[2,128]{1,0:T(2,128)S(1)}, u32[]{:S(2)}, u32[]{:S(2)}) collective-permute-start(s32[2,128]{1,0:T(2,128)S(1)} %pad_add_fusion), channel_id=1, source_target_pairs={{0,8},{8,0},{16,24},{24,16},{1,9},{9,1},{17,25},{25,17},{2,10},{10... | collective-permute-start | bytes 3080 | tf_op jit(solution)/shard_map/ppermute | solution.py:22
  9.5 3.5 %collective-permute-start.3 = (f32[72,128]{1,0:T(8,128)S(1)}, f32[72,128]{1,0:T(8,128)S(1)}, u32[]{:S(2)}, u32[]{:S(2)}) collective-permute-start(f32[72,128]{1,0:T(8,128)S(1)} %get-tuple-element.54), channel_id=1, source_target_pairs={{0,9},{1,8},{2,11},{3,10},{4,13},{5,12},{6,15},{7,14},{8,1},{9,0},... | collective-permute-start | bytes 110600 | tf_op jit(solution)/shard_map/ppermute | solution.py:22
  13.0 3.5 %collective-permute-start.4 = (f32[72,128]{1,0:T(8,128)S(1)}, f32[72,128]{1,0:T(8,128)S(1)}, u32[]{:S(2)}, u32[]{:S(2)}) collective-permute-start(f32[72,128]{1,0:T(8,128)S(1)} %add.12), channel_id=1, source_target_pairs={{0,10},{1,11},{2,8},{3,9},{4,14},{5,15},{6,12},{7,13},{8,2},{9,3},... | collective-permute-start | bytes 110600 | tf_op jit(solution)/shard_map/ppermute | solution.py:22
  16.5 4.4 %collective-permute-start.6 = (bf16[512,128]{1,0:T(8,128)(2,1)S(1)}, bf16[512,128]{1,0:T(8,128)(2,1)S(1)}, u32[]{:S(2)}, u32[]{:S(2)}) collective-permute-start(bf16[512,128]{1,0:T(8,128)(2,1)S(1)} %get-tuple-element.69), channel_id=1, source_target_pairs={{0,8},{1,9},{2,10},{3,11},{4,12},{5,13},{6,14},{7,15},{8,0},{9,1},... | collective-permute-start | bytes 393224 | tf_op jit(solution)/shard_map/ppermute | solution.py:22
  16.6 4.3 %collective-permute-start.5 = (f32[72,128]{1,0:T(8,128)S(1)}, f32[72,128]{1,0:T(8,128)S(1)}, u32[]{:S(2)}, u32[]{:S(2)}) collective-permute-start(f32[72,128]{1,0:T(8,128)S(1)} %add.13), channel_id=1, source_target_pairs={{0,12},{1,13},{2,14},{3,15},{4,8},{5,9},{6,10},{7,11},{8,4},{9,5},... | collective-permute-start | bytes 110600 | tf_op jit(solution)/shard_map/ppermute | solution.py:22
  20.9 3.5 %collective-permute-start.7 = (f32[72,128]{1,0:T(8,128)S(1)}, f32[72,128]{1,0:T(8,128)S(1)}, u32[]{:S(2)}, u32[]{:S(2)}) collective-permute-start(f32[72,128]{1,0:T(8,128)S(1)} %add.14), channel_id=1, source_target_pairs={{0,24},{1,25},{2,26},{3,27},{4,28},{5,29},{6,30},{7,31},{8,16},{9,... | collective-permute-start | bytes 110600 | tf_op jit(solution)/shard_map/ppermute | solution.py:22
  24.4 1.2 %collective-permute-start.8 = (f32[72,128]{1,0:T(8,128)S(1)}, f32[72,128]{1,0:T(8,128)S(1)}, u32[]{:S(2)}, u32[]{:S(2)}) collective-permute-start(f32[72,128]{1,0:T(8,128)S(1)} %add.15.part_ref), channel_id=1, source_target_pairs={{0,8},{1,9},{2,10},{3,11},{4,12},{5,13},{6,14},{7,15},{8,0},{9,1},... | collective-permute-start | bytes 110600 | tf_op jit(solution)/shard_map/ppermute | solution.py:22

commit v6 on v5

--- a/solution.py
+++ b/solution.py
@@ -353,6 +353,10 @@
         grad_ref[:, pl.ds(half + tile * LANES, LANES)] = jnp.where(second == 1, part, moved)
     last = half // LANES * modes
     rate_ref[...] = (part_ref[last : last + 1, :] + moved_ref[last : last + 1, :])[:, :modes]
+
+
+def rounded(value):
+    return lax.reduce_precision(value, 8, 7)
 
 
 def per_device(token_ids, feature_table, short_weight, residue, rates, skip_gain, grad_out):
@@ -440,6 +444,10 @@
     )
     core = lax.axis_size("dp")
     hops = [mask | core for mask in masks_of(blocks * core) if mask != core]
+    rows = half // LANES * modes
+    rate = part[rows : rows + 1]
+    part = part[:rows]
+    filler = jnp.zeros((14, LANES), BF16)
     for hop in hops:
         if hop == hops[0]:
             part, res = lax.optimization_barrier((part, res))
@@ -473,7 +481,13 @@
                 (0, 800_000),
                 out_spaces=[hbm],
             )
-        part = part + xor_permute(part, ("ctx", "dp"), hop)
+        part, upper = rounded(part), rounded(rate)
+        lower = rounded(rate - upper)
+        sent = jnp.concatenate([part.astype(BF16), upper.astype(BF16), lower.astype(BF16), filler], axis=0)
+        moved = xor_permute(sent, ("ctx", "dp"), hop).astype(F32)
+        part = part + moved[:rows]
+        rate = upper + lower + (moved[rows : rows + 1] + moved[rows + 1 : rows + 2])
+    part = jnp.concatenate([part, rate, jnp.zeros((SUBLANES - 1, LANES), F32)], axis=0)
     part, mixed = lax.optimization_barrier((part, mixed))
     grad, rate = call(
         functools.partial(result_kernel, modes),

time: 26.4 us -> 26.1 us (0.989)
  waiting for transfers between devices: 7.08 us -> 6.23 us
  other arithmetic: 0.03 us -> 0.54 us
  starting transfers between devices: 10.4 us -> 10.1 us
    ppermute x9, waiting for transfers between devices: 7.08 us -> 6.23 us  [xor_permute(): return lax.ppermute(block, axis, [(i, i ^ mask) for i in range(size)])]
    concatenate x0 -> x5, other arithmetic: none -> 0.4 us  [the longest x4 0.32 us: per_device(): jnp.concatenate([part.astype(BF16), upper.astype(BF16), lower.astype(BF16...]
  transfers between devices with their start and end apart: 9 -> 9, of which waited for: 6 -> 6; matrix products, arithmetic and copies ran while one was open for 0% -> 1% of each run, Pallas kernels for 17% -> 17%
where the time goes in v6:
time: 26.1 us; the launch traced here: 25.9 us
  starting transfers between devices  10.1 us (39%)
  Pallas kernels  8.08 us (31%)
  waiting for transfers between devices  6.23 us (24%)
  between operations  0.77 us (3%)
  other arithmetic  0.54 us (2%)
    ppermute x9, starting transfers between devices, xor_permute(): return lax.ppermute(block, axis, [(i, i ^ mask) for i in range(size)])  10.1 us
    pallas_call x7, Pallas kernels, call(): pl.pallas_call(kernel, out_shape=[jax.ShapeDtypeStruct(shape, dtype) for...  8.08 us
    ppermute x9, waiting for transfers between devices, xor_permute(): return lax.ppermute(block, axis, [(i, i ^ mask) for i in range(size)])  6.23 us
  transfers between devices with their start and end apart: 9, of which 6 were waited for; matrix products, arithmetic and copies ran while one was open for 1% of the time, Pallas kernels for 17%

profile of v6, /device:TPU:0, one launch (start us, length us, event | category | flops | bytes accessed | tf_op | source)
XLA Modules:
  0.0 25.9 jit_solution(3658776258276235811)
XLA Ops:
  0.6 2.5 %collective-permute-start = (s32[1,128]{1,0:T(1,128)}, s32[1,128]{1,0:T(1,128)S(1)}, u32[]{:S(2)}, u32[]{:S(2)}) collective-permute-start(s32[1,128]{1,0:T(1,128)} %refs_3_.1), channel_id=1, source_target_pairs={{0,24},{8,16},{16,8},{24,0},{1,25},{9,17},{17,9},{25,1},{2,26},{10... | collective-permute-start | bytes 1544 | tf_op jit(solution)/shard_map/ppermute | solution.py:22
  3.1 1.5 %shard_map.121 = (s32[1,128]{1,0:T(1,128)S(1)}, f32[7,3072]{1,0:T(8,128)S(1)}, f32[16,1024]{1,0:T(8,128)S(1)}, f32[256,256]{1,0:T(8,128)S(1)}, f32[768,128]{1,0:...) custom-call(f32[1,16]{1,0:T(1,128)} %bitcast.14, f32[768,128]{1,0:T(8,128)} %constant.10.clone.refs_1_, ...), custom_call_target="tpu_custom_call" | custom-call | flops 10000000000 | bytes 40000000 | tf_op jit(solution)/shard_map/pallas_call | solution.py:322
  4.6 0.7 %collective-permute-start.1 = (bf16[512,128]{1,0:T(8,128)(2,1)S(1)}, bf16[512,128]{1,0:T(8,128)(2,1)S(1)}, u32[]{:S(2)}, u32[]{:S(2)}) collective-permute-start(bf16[512,128]{1,0:T(8,128)(2,1)S(1)} %get-tuple-element.51), channel_id=1, source_target_pairs={{0,8},{8,0},{16,24},{24,16},{1,9},{9,1},{17,25},{25,17},{2,10},{10... | collective-permute-start | bytes 393224 | tf_op jit(solution)/shard_map/ppermute | solution.py:22
  5.3 0.1 pad.18.clone
  5.4 0.0 collective-permute-done.refs_1_
  5.4 0.1 collective-permute-start.2
  5.5 0.3 %shard_map.122 = (bf16[512,128]{1,0:T(8,128)(2,1)S(1)}, bf16[128,384]{1,0:T(8,128)(2,1)S(1)}, bf16[128,128]{1,0:T(8,128)(2,1)S(1)}, bf16[64,256]{1,0:T(8,128)(2,1)S(1)}, f32[256,128]{1,0:T(8,128)S(1)}) custom-call(f32[768,128]{1,0:T(8,128)S(1)} %get-tuple-element.44.table_ref, f32[256,256]{1,0:T(8,128)S(1)} %get-tuple-element.45.fwd_ref), custom_call_target="tpu_custom_call" | custom-call | flops 300000000 | bytes 1000000 | tf_op jit(solution)/shard_map/pallas_call | solution.py:322
  5.8 0.8 %collective-permute-done.2.refs_2_ = s32[2,128]{1,0:T(2,128)S(1)} collective-permute-done((s32[2,128]{1,0:T(2,128)S(1)}, s32[2,128]{1,0:T(2,128)S(1)}, u32[]{:S(2)}, u32[]{:S(2)}) %collective-permute-start.2) | collective-permute-done | bytes 1056 | tf_op jit(solution)/shard_map/ppermute | solution.py:22
  6.6 0.0 collective-permute-done.1.mate_ref
  6.6 2.9 %shard_map.123 = (f32[72,128]{1,0:T(8,128)S(1)}, f32[128,1024]{1,0:T(8,128)S(1)}, bf16[128,1024]{1,0:T(8,128)(2,1)S(1)}, f32[256,1024]{1,0:T(8,128)S(1)}, f32[32,1024]{1,0:T(8,128)S(1)}) custom-call(bf16[3072,512]{1,0:T(8,128)(2,1)S(1)} %copy-done, f32[7,3072]{1,0:T(8,128)S(1)} %get-tuple-element.40.short_ref, f32[16,1024]{1,0:T(8,128)S(1)} %get-tuple-element.57.res_ref, ...), custom_call_target="tpu_custom_call" | custom-call | flops 1073741824 | bytes 6000000 | tf_op jit(solution)/shard_map/pallas_call | solution.py:322
  9.6 0.1 maximum_maximum_fusion.1
  9.6 1.3 %collective-permute-start.3 = (bf16[80,128]{1,0:T(8,128)(2,1)S(1)}, bf16[80,128]{1,0:T(8,128)(2,1)S(1)}, u32[]{:S(2)}, u32[]{:S(2)}) collective-permute-start(bf16[80,128]{1,0:T(8,128)(2,1)S(1)} %maximum_maximum_fusion.1), channel_id=1, source_target_pairs={{0,9},{1,8},{2,11},{3,10},{4,13},{5,12},{6,15},{7,14},{8,1},{9,0},... | collective-permute-start | bytes 61448 | tf_op jit(solution)/shard_map/ppermute | solution.py:22
  11.0 1.0 %shard_map.124 = (f32[256,512]{1,0:T(8,128)S(1)}, bf16[256,288]{1,0:T(8,128)(2,1)S(1)}, f32[1,1024]{1,0:T(1,128)S(1)}) custom-call(f32[256,128]{1,0:T(8,128)S(1)} %get-tuple-element.56.spec_ref, f32[768,128]{1,0:T(8,128)S(1)} %get-tuple-element.44.table_ref, f32[16,1024]{1,0:T(8,128)S(1)} %get-tuple-element.57.res_ref, f32[128,256]{1,0:T(8,128)} %constant.12.clone.inv_ref, ...), custom_call_target="tpu_custom_call" | custom-call | flops 50000000 | bytes 1500000 | tf_op jit(solution)/shard_map/pallas_call | solution.py:322
  12.0 0.9 %collective-permute-done.3 = bf16[80,128]{1,0:T(8,128)(2,1)S(1)} collective-permute-done((bf16[80,128]{1,0:T(8,128)(2,1)S(1)}, bf16[80,128]{1,0:T(8,128)(2,1)S(1)}, u32[]{:S(2)}, u32[]{:S(2)}) %collective-permute-start.3) | collective-permute-done | bytes 20512 | tf_op jit(solution)/shard_map/ppermute | solution.py:22
  12.9 0.1 maximum_maximum_fusion.2
  13.0 1.4 %collective-permute-start.4 = (bf16[80,128]{1,0:T(8,128)(2,1)S(1)}, bf16[80,128]{1,0:T(8,128)(2,1)S(1)}, u32[]{:S(2)}, u32[]{:S(2)}) collective-permute-start(bf16[80,128]{1,0:T(8,128)(2,1)S(1)} %maximum_maximum_fusion.2), channel_id=1, source_target_pairs={{0,10},{1,11},{2,8},{3,9},{4,14},{5,15},{6,12},{7,13},{8,2},{9,3},... | collective-permute-start | bytes 61448 | tf_op jit(solution)/shard_map/ppermute | solution.py:22
  14.4 1.1 %shard_map.125 = (bf16[512,128]{1,0:T(8,128)(2,1)S(1)}, bf16[512,128]{1,0:T(8,128)(2,1)S(1)}) custom-call(f32[128,1024]{1,0:T(8,128)S(1)} %get-tuple-element.60.query_ref, bf16[128,1024]{1,0:T(8,128)(2,1)S(1)} %get-tuple-element.61.gated_ref, f32[256,1024]{1,0:T(8,128)S(1)} %get-tuple-element.62.spec_ref, f32[256,512]{1,0:T(8,128)S(1)} %get-tuple-element.63.filt_ref, ...), custom_call_target="tpu_custom_call" | custom-call | flops 300000000 | bytes 3000000 | tf_op jit(solution)/shard_map/pallas_call | solution.py:322
  15.5 0.8 %collective-permute-done.4 = bf16[80,128]{1,0:T(8,128)(2,1)S(1)} collective-permute-done((bf16[80,128]{1,0:T(8,128)(2,1)S(1)}, bf16[80,128]{1,0:T(8,128)(2,1)S(1)}, u32[]{:S(2)}, u32[]{:S(2)}) %collective-permute-start.4) | collective-permute-done | bytes 20512 | tf_op jit(solution)/shard_map/ppermute | solution.py:22
  16.3 0.1 maximum_maximum_fusion.3
  16.4 2.4 %collective-permute-start.5 = (bf16[80,128]{1,0:T(8,128)(2,1)S(1)}, bf16[80,128]{1,0:T(8,128)(2,1)S(1)}, u32[]{:S(2)}, u32[]{:S(2)}) collective-permute-start(bf16[80,128]{1,0:T(8,128)(2,1)S(1)} %maximum_maximum_fusion.3), channel_id=1, source_target_pairs={{0,12},{1,13},{2,14},{3,15},{4,8},{5,9},{6,10},{7,11},{8,4},{9,5},... | collective-permute-start | bytes 61448 | tf_op jit(solution)/shard_map/ppermute | solution.py:22
  18.8 0.3 %collective-permute-start.6 = (bf16[512,128]{1,0:T(8,128)(2,1)S(1)}, bf16[512,128]{1,0:T(8,128)(2,1)S(1)}, u32[]{:S(2)}, u32[]{:S(2)}) collective-permute-start(bf16[512,128]{1,0:T(8,128)(2,1)S(1)} %get-tuple-element.69), channel_id=1, source_target_pairs={{0,8},{1,9},{2,10},{3,11},{4,12},{5,13},{6,14},{7,15},{8,0},{9,1},... | collective-permute-start | bytes 393224 | tf_op jit(solution)/shard_map/ppermute | solution.py:22
  19.2 1.4 %collective-permute-done.5 = bf16[80,128]{1,0:T(8,128)(2,1)S(1)} collective-permute-done((bf16[80,128]{1,0:T(8,128)(2,1)S(1)}, bf16[80,128]{1,0:T(8,128)(2,1)S(1)}, u32[]{:S(2)}, u32[]{:S(2)}) %collective-permute-start.5) | collective-permute-done | bytes 20512 | tf_op jit(solution)/shard_map/ppermute | solution.py:22
  20.6 0.0 collective-permute-done.6.mate_ref
  20.6 0.1 maximum_maximum_fusion.4
  20.7 1.1 %collective-permute-start.7 = (bf16[80,128]{1,0:T(8,128)(2,1)S(1)}, bf16[80,128]{1,0:T(8,128)(2,1)S(1)}, u32[]{:S(2)}, u32[]{:S(2)}) collective-permute-start(bf16[80,128]{1,0:T(8,128)(2,1)S(1)} %maximum_maximum_fusion.4), channel_id=1, source_target_pairs={{0,24},{1,25},{2,26},{3,27},{4,28},{5,29},{6,30},{7,31},{8,16},{9,... | collective-permute-start | bytes 61448 | tf_op jit(solution)/shard_map/ppermute | solution.py:22
  21.8 0.1 pad.2.clone
  21.9 0.7 %shard_map.126 = bf16[1024,128]{1,0:T(8,128)(2,1)} custom-call(bf16[512,128]{1,0:T(8,128)(2,1)S(1)} %get-tuple-element.71.own_ref, bf16[512,128]{1,0:T(8,128)(2,1)S(1)} %collective-permute-done.6.mate_ref), custom_call_target="tpu_custom_call" | custom-call | bytes 800000 | tf_op jit(solution)/shard_map/pallas_call | solution.py:322
  22.6 1.3 %collective-permute-done.7 = bf16[80,128]{1,0:T(8,128)(2,1)S(1)} collective-permute-done((bf16[80,128]{1,0:T(8,128)(2,1)S(1)}, bf16[80,128]{1,0:T(8,128)(2,1)S(1)}, u32[]{:S(2)}, u32[]{:S(2)}) %collective-permute-start.7) | collective-permute-done | bytes 20512 | tf_op jit(solution)/shard_map/ppermute | solution.py:22
  24.0 0.1 maximum_maximum_fusion.part_ref
  24.0 0.2 collective-permute-start.8
  24.3 1.0 %collective-permute-done.8.moved_ref = f32[72,128]{1,0:T(8,128)S(1)} collective-permute-done((f32[72,128]{1,0:T(8,128)S(1)}, f32[72,128]{1,0:T(8,128)S(1)}, u32[]{:S(2)}, u32[]{:S(2)}) %collective-permute-start.8) | collective-permute-done | bytes 36896 | tf_op jit(solution)/shard_map/ppermute | solution.py:22
  25.3 0.6 %shard_map.127 = (f32[16,1024]{1,0:T(8,128)}, f32[1,16]{1,0:T(1,128)}) custom-call(f32[72,128]{1,0:T(8,128)S(1)} %maximum_maximum_fusion.part_ref, f32[72,128]{1,0:T(8,128)S(1)} %collective-permute-done.8.moved_ref), custom_call_target="tpu_custom_call" | custom-call | bytes 200000 | tf_op jit(solution)/shard_map/pallas_call | solution.py:322
  (26 shorter events, 0.2 us)
Async XLA Ops:
  0.6 4.8 %collective-permute-start = (s32[1,128]{1,0:T(1,128)}, s32[1,128]{1,0:T(1,128)S(1)}, u32[]{:S(2)}, u32[]{:S(2)}) collective-permute-start(s32[1,128]{1,0:T(1,128)} %refs_3_.1), channel_id=1, source_target_pairs={{0,24},{8,16},{16,8},{24,0},{1,25},{9,17},{17,9},{25,1},{2,26},{10... | collective-permute-start | bytes 1544 | tf_op jit(solution)/shard_map/ppermute | solution.py:22
  3.1 3.5 %copy-start = (bf16[3072,512]{1,0:T(8,128)(2,1)S(1)}, bf16[3072,512]{1,0:T(8,128)(2,1)}, u32[]{:S(2)}) copy-start(bf16[3072,512]{1,0:T(8,128)(2,1)} %table_ref.1) | copy-start | bytes 9437188
  4.6 2.0 %collective-permute-start.1 = (bf16[512,128]{1,0:T(8,128)(2,1)S(1)}, bf16[512,128]{1,0:T(8,128)(2,1)S(1)}, u32[]{:S(2)}, u32[]{:S(2)}) collective-permute-start(bf16[512,128]{1,0:T(8,128)(2,1)S(1)} %get-tuple-element.51), channel_id=1, source_target_pairs={{0,8},{8,0},{16,24},{24,16},{1,9},{9,1},{17,25},{25,17},{2,10},{10... | collective-permute-start | bytes 393224 | tf_op jit(solution)/shard_map/ppermute | solution.py:22
  5.4 1.2 %collective-permute-start.2 = (s32[2,128]{1,0:T(2,128)S(1)}, s32[2,128]{1,0:T(2,128)S(1)}, u32[]{:S(2)}, u32[]{:S(2)}) collective-permute-start(s32[2,128]{1,0:T(2,128)S(1)} %pad_add_fusion), channel_id=1, source_target_pairs={{0,8},{8,0},{16,24},{24,16},{1,9},{9,1},{17,25},{25,17},{2,10},{10... | collective-permute-start | bytes 3080 | tf_op jit(solution)/shard_map/ppermute | solution.py:22
  9.6 3.2 %collective-permute-start.3 = (bf16[80,128]{1,0:T(8,128)(2,1)S(1)}, bf16[80,128]{1,0:T(8,128)(2,1)S(1)}, u32[]{:S(2)}, u32[]{:S(2)}) collective-permute-start(bf16[80,128]{1,0:T(8,128)(2,1)S(1)} %maximum_maximum_fusion.1), channel_id=1, source_target_pairs={{0,9},{1,8},{2,11},{3,10},{4,13},{5,12},{6,15},{7,14},{8,1},{9,0},... | collective-permute-start | bytes 61448 | tf_op jit(solution)/shard_map/ppermute | solution.py:22
  13.0 3.2 %collective-permute-start.4 = (bf16[80,128]{1,0:T(8,128)(2,1)S(1)}, bf16[80,128]{1,0:T(8,128)(2,1)S(1)}, u32[]{:S(2)}, u32[]{:S(2)}) collective-permute-start(bf16[80,128]{1,0:T(8,128)(2,1)S(1)} %maximum_maximum_fusion.2), channel_id=1, source_target_pairs={{0,10},{1,11},{2,8},{3,9},{4,14},{5,15},{6,12},{7,13},{8,2},{9,3},... | collective-permute-start | bytes 61448 | tf_op jit(solution)/shard_map/ppermute | solution.py:22
  16.4 4.1 %collective-permute-start.5 = (bf16[80,128]{1,0:T(8,128)(2,1)S(1)}, bf16[80,128]{1,0:T(8,128)(2,1)S(1)}, u32[]{:S(2)}, u32[]{:S(2)}) collective-permute-start(bf16[80,128]{1,0:T(8,128)(2,1)S(1)} %maximum_maximum_fusion.3), channel_id=1, source_target_pairs={{0,12},{1,13},{2,14},{3,15},{4,8},{5,9},{6,10},{7,11},{8,4},{9,5},... | collective-permute-start | bytes 61448 | tf_op jit(solution)/shard_map/ppermute | solution.py:22
  18.8 1.8 %collective-permute-start.6 = (bf16[512,128]{1,0:T(8,128)(2,1)S(1)}, bf16[512,128]{1,0:T(8,128)(2,1)S(1)}, u32[]{:S(2)}, u32[]{:S(2)}) collective-permute-start(bf16[512,128]{1,0:T(8,128)(2,1)S(1)} %get-tuple-element.69), channel_id=1, source_target_pairs={{0,8},{1,9},{2,10},{3,11},{4,12},{5,13},{6,14},{7,15},{8,0},{9,1},... | collective-permute-start | bytes 393224 | tf_op jit(solution)/shard_map/ppermute | solution.py:22
  20.7 3.2 %collective-permute-start.7 = (bf16[80,128]{1,0:T(8,128)(2,1)S(1)}, bf16[80,128]{1,0:T(8,128)(2,1)S(1)}, u32[]{:S(2)}, u32[]{:S(2)}) collective-permute-start(bf16[80,128]{1,0:T(8,128)(2,1)S(1)} %maximum_maximum_fusion.4), channel_id=1, source_target_pairs={{0,24},{1,25},{2,26},{3,27},{4,28},{5,29},{6,30},{7,31},{8,16},{9,... | collective-permute-start | bytes 61448 | tf_op jit(solution)/shard_map/ppermute | solution.py:22
  24.0 1.2 %collective-permute-start.8 = (f32[72,128]{1,0:T(8,128)S(1)}, f32[72,128]{1,0:T(8,128)S(1)}, u32[]{:S(2)}, u32[]{:S(2)}) collective-permute-start(f32[72,128]{1,0:T(8,128)S(1)} %maximum_maximum_fusion.part_ref), channel_id=1, source_target_pairs={{0,8},{1,9},{2,10},{3,11},{4,12},{5,13},{6,14},{7,15},{8,0},{9,1},... | collective-permute-start | bytes 110600 | tf_op jit(solution)/shard_map/ppermute | solution.py:22

commit v7 on v6

--- a/solution.py
+++ b/solution.py
@@ -257,7 +257,7 @@
         slope = slope[:, :GROUP] + slope[:, GROUP:]
         for side in range(GROUP // LANES):
             at = (group * GROUP + side * LANES) // LANES * modes
-            part_ref[pl.ds(at, modes), :] = grad[:, side * LANES : (side + 1) * LANES]
+            part_ref[pl.ds(at, modes), :] = grad[:, side * LANES : (side + 1) * LANES].astype(BF16)
         return rate + jnp.sum(res * slope, axis=1, keepdims=True)
 
     feats = features(0)
@@ -267,7 +267,10 @@
         feats = ahead
     wide = jnp.broadcast_to(rate, (modes, LANES))
     square = jnp.concatenate([wide, jnp.zeros((LANES - modes, LANES), F32)], axis=0).T
-    part_ref[pl.ds(half // LANES * modes, SUBLANES), :] = square[:SUBLANES]
+    upper, lower = halves(jnp.broadcast_to(square[:1], (2 * SUBLANES, LANES)))
+    row = lax.broadcasted_iota(jnp.int32, (2 * SUBLANES, LANES), 0)
+    tail = jnp.where(row == 0, upper.astype(F32), jnp.where(row == 1, lower.astype(F32), 0.0))
+    part_ref[pl.ds(half // LANES * modes, 2 * SUBLANES), :] = tail.astype(BF16)
 
 
 def filter_kernel(modes, block_len, spec_ref, table_ref, res_ref, inv_ref, skip_ref, filt_ref, inv_out, skip_out, inv, copied):
@@ -429,7 +432,7 @@
     part, query, gated, spec, state = call(
         functools.partial(main_kernel, modes, blocks, block_len, taps, channels),
         [
-            ((half // LANES * modes + SUBLANES, LANES), F32),
+            ((half // LANES * modes + 2 * SUBLANES, LANES), BF16),
             ((block_len, channels), F32),
             ((block_len, channels), BF16),
             ((period, channels), F32),
@@ -445,12 +448,11 @@
     core = lax.axis_size("dp")
     hops = [mask | core for mask in masks_of(blocks * core) if mask != core]
     rows = half // LANES * modes
-    rate = part[rows : rows + 1]
-    part = part[:rows]
+    sent = part
     filler = jnp.zeros((14, LANES), BF16)
     for hop in hops:
         if hop == hops[0]:
-            part, res = lax.optimization_barrier((part, res))
+            sent, res = lax.optimization_barrier((sent, res))
             filt, inv, skip = call(
                 functools.partial(filter_kernel, modes, block_len),
                 [((period, half), F32), ((2 * block_len, period + 2 * modes), BF16), ((1, channels), F32)],
@@ -481,9 +483,12 @@
                 (0, 800_000),
                 out_spaces=[hbm],
             )
-        part, upper = rounded(part), rounded(rate)
-        lower = rounded(rate - upper)
-        sent = jnp.concatenate([part.astype(BF16), upper.astype(BF16), lower.astype(BF16), filler], axis=0)
+        if hop == hops[0]:
+            part, upper, lower = (sent[at].astype(F32) for at in (slice(rows), slice(rows, rows + 1), slice(rows + 1, rows + 2)))
+        else:
+            part, upper = rounded(part), rounded(rate)
+            lower = rounded(rate - upper)
+            sent = jnp.concatenate([part.astype(BF16), upper.astype(BF16), lower.astype(BF16), filler], axis=0)
         moved = xor_permute(sent, ("ctx", "dp"), hop).astype(F32)
         part = part + moved[:rows]
         rate = upper + lower + (moved[rows : rows + 1] + moved[rows + 1 : rows + 2])

time: 26.1 us -> 25.9 us (level)
  transfers between devices with their start and end apart: 9 -> 9, of which waited for: 6 -> 6; matrix products, arithmetic and copies ran while one was open for 1% -> 1% of each run, Pallas kernels for 17% -> 18%
where the time goes in v7:
time: 25.9 us; the launch traced here: 25.7 us
  starting transfers between devices  10.2 us (39%)
  Pallas kernels  8.09 us (31%)
  waiting for transfers between devices  6.09 us (24%)
  between operations  0.77 us (3%)
  other arithmetic  0.44 us (2%)
    ppermute x9, starting transfers between devices, xor_permute(): return lax.ppermute(block, axis, [(i, i ^ mask) for i in range(size)])  10.2 us
    pallas_call x7, Pallas kernels, call(): pl.pallas_call(kernel, out_shape=[jax.ShapeDtypeStruct(shape, dtype) for...  8.09 us
    ppermute x9, waiting for transfers between devices, xor_permute(): return lax.ppermute(block, axis, [(i, i ^ mask) for i in range(size)])  6.09 us
  transfers between devices with their start and end apart: 9, of which 6 were waited for; matrix products, arithmetic and copies ran while one was open for 1% of the time, Pallas kernels for 18%

profile of v7, /device:TPU:0, one launch (start us, length us, event | category | flops | bytes accessed | tf_op | source)
XLA Modules:
  0.0 25.7 jit_solution(2989160812537107619)
XLA Ops:
  0.6 2.5 %collective-permute-start = (s32[1,128]{1,0:T(1,128)}, s32[1,128]{1,0:T(1,128)S(1)}, u32[]{:S(2)}, u32[]{:S(2)}) collective-permute-start(s32[1,128]{1,0:T(1,128)} %refs_3_.1), channel_id=1, source_target_pairs={{0,24},{8,16},{16,8},{24,0},{1,25},{9,17},{17,9},{25,1},{2,26},{10... | collective-permute-start | bytes 1544 | tf_op jit(solution)/shard_map/ppermute | solution.py:22
  3.1 1.5 %shard_map.121 = (s32[1,128]{1,0:T(1,128)S(1)}, f32[7,3072]{1,0:T(8,128)S(1)}, f32[16,1024]{1,0:T(8,128)S(1)}, f32[256,256]{1,0:T(8,128)S(1)}, f32[768,128]{1,0:...) custom-call(f32[1,16]{1,0:T(1,128)} %bitcast.14, f32[768,128]{1,0:T(8,128)} %constant.10.clone.refs_1_, ...), custom_call_target="tpu_custom_call" | custom-call | flops 10000000000 | bytes 40000000 | tf_op jit(solution)/shard_map/pallas_call | solution.py:325
  4.6 0.7 %collective-permute-start.1 = (bf16[512,128]{1,0:T(8,128)(2,1)S(1)}, bf16[512,128]{1,0:T(8,128)(2,1)S(1)}, u32[]{:S(2)}, u32[]{:S(2)}) collective-permute-start(bf16[512,128]{1,0:T(8,128)(2,1)S(1)} %get-tuple-element.51), channel_id=1, source_target_pairs={{0,8},{8,0},{16,24},{24,16},{1,9},{9,1},{17,25},{25,17},{2,10},{10... | collective-permute-start | bytes 393224 | tf_op jit(solution)/shard_map/ppermute | solution.py:22
  5.3 0.0 collective-permute-done.refs_1_
  5.3 0.1 collective-permute-start.2
  5.4 0.3 %shard_map.122 = (bf16[512,128]{1,0:T(8,128)(2,1)S(1)}, bf16[128,384]{1,0:T(8,128)(2,1)S(1)}, bf16[128,128]{1,0:T(8,128)(2,1)S(1)}, bf16[64,256]{1,0:T(8,128)(2,1)S(1)}, f32[256,128]{1,0:T(8,128)S(1)}) custom-call(f32[768,128]{1,0:T(8,128)S(1)} %get-tuple-element.44.table_ref, f32[256,256]{1,0:T(8,128)S(1)} %get-tuple-element.45.fwd_ref), custom_call_target="tpu_custom_call" | custom-call | flops 300000000 | bytes 1000000 | tf_op jit(solution)/shard_map/pallas_call | solution.py:325
  5.7 0.8 %collective-permute-done.2.refs_2_ = s32[2,128]{1,0:T(2,128)S(1)} collective-permute-done((s32[2,128]{1,0:T(2,128)S(1)}, s32[2,128]{1,0:T(2,128)S(1)}, u32[]{:S(2)}, u32[]{:S(2)}) %collective-permute-start.2) | collective-permute-done | bytes 1056 | tf_op jit(solution)/shard_map/ppermute | solution.py:22
  6.5 0.0 collective-permute-done.1.mate_ref
  6.5 0.0 copy-done
  6.5 2.9 %shard_map.123 = (bf16[80,128]{1,0:T(8,128)(2,1)S(1)}, f32[128,1024]{1,0:T(8,128)S(1)}, bf16[128,1024]{1,0:T(8,128)(2,1)S(1)}, f32[256,1024]{1,0:T(8,128)S(1)}, f32[32,1024]{1,0:T(8,128)S(1)}) custom-call(bf16[3072,512]{1,0:T(8,128)(2,1)S(1)} %copy-done, f32[7,3072]{1,0:T(8,128)S(1)} %get-tuple-element.40.short_ref, ...), custom_call_target="tpu_custom_call" | custom-call | flops 1073741824 | bytes 6000000 | tf_op jit(solution)/shard_map/pallas_call | solution.py:325
  9.5 1.3 %collective-permute-start.3 = (bf16[80,128]{1,0:T(8,128)(2,1)S(1)}, bf16[80,128]{1,0:T(8,128)(2,1)S(1)}, u32[]{:S(2)}, u32[]{:S(2)}) collective-permute-start(bf16[80,128]{1,0:T(8,128)(2,1)S(1)} %get-tuple-element.54), channel_id=1, source_target_pairs={{0,9},{1,8},{2,11},{3,10},{4,13},{5,12},{6,15},{7,14},{8,1},{9,0},... | collective-permute-start | bytes 61448 | tf_op jit(solution)/shard_map/ppermute | solution.py:22
  10.8 0.1 pad.14.clone
  10.8 1.0 %shard_map.124 = (f32[256,512]{1,0:T(8,128)S(1)}, bf16[256,288]{1,0:T(8,128)(2,1)S(1)}, f32[1,1024]{1,0:T(1,128)S(1)}) custom-call(f32[256,128]{1,0:T(8,128)S(1)} %get-tuple-element.56.spec_ref, f32[768,128]{1,0:T(8,128)S(1)} %get-tuple-element.44.table_ref, f32[16,1024]{1,0:T(8,128)S(1)} %get-tuple-element.57.res_ref, f32[128,256]{1,0:T(8,128)} %constant.12.clone.inv_ref, ...), custom_call_target="tpu_custom_call" | custom-call | flops 50000000 | bytes 1500000 | tf_op jit(solution)/shard_map/pallas_call | solution.py:325
  11.8 0.8 %collective-permute-done.3 = bf16[80,128]{1,0:T(8,128)(2,1)S(1)} collective-permute-done((bf16[80,128]{1,0:T(8,128)(2,1)S(1)}, bf16[80,128]{1,0:T(8,128)(2,1)S(1)}, u32[]{:S(2)}, u32[]{:S(2)}) %collective-permute-start.3) | collective-permute-done | bytes 20512 | tf_op jit(solution)/shard_map/ppermute | solution.py:22
  12.7 0.1 maximum_maximum_fusion.1
  12.8 1.4 %collective-permute-start.4 = (bf16[80,128]{1,0:T(8,128)(2,1)S(1)}, bf16[80,128]{1,0:T(8,128)(2,1)S(1)}, u32[]{:S(2)}, u32[]{:S(2)}) collective-permute-start(bf16[80,128]{1,0:T(8,128)(2,1)S(1)} %maximum_maximum_fusion.1), channel_id=1, source_target_pairs={{0,10},{1,11},{2,8},{3,9},{4,14},{5,15},{6,12},{7,13},{8,2},{9,3},... | collective-permute-start | bytes 61448 | tf_op jit(solution)/shard_map/ppermute | solution.py:22
  14.2 1.0 %shard_map.125 = (bf16[512,128]{1,0:T(8,128)(2,1)S(1)}, bf16[512,128]{1,0:T(8,128)(2,1)S(1)}) custom-call(f32[128,1024]{1,0:T(8,128)S(1)} %get-tuple-element.60.query_ref, bf16[128,1024]{1,0:T(8,128)(2,1)S(1)} %get-tuple-element.61.gated_ref, f32[256,1024]{1,0:T(8,128)S(1)} %get-tuple-element.62.spec_ref, f32[256,512]{1,0:T(8,128)S(1)} %get-tuple-element.63.filt_ref, ...), custom_call_target="tpu_custom_call" | custom-call | flops 300000000 | bytes 3000000 | tf_op jit(solution)/shard_map/pallas_call | solution.py:325
  15.3 0.8 %collective-permute-done.4 = bf16[80,128]{1,0:T(8,128)(2,1)S(1)} collective-permute-done((bf16[80,128]{1,0:T(8,128)(2,1)S(1)}, bf16[80,128]{1,0:T(8,128)(2,1)S(1)}, u32[]{:S(2)}, u32[]{:S(2)}) %collective-permute-start.4) | collective-permute-done | bytes 20512 | tf_op jit(solution)/shard_map/ppermute | solution.py:22
  16.1 0.1 maximum_maximum_fusion.2
  16.2 2.4 %collective-permute-start.5 = (bf16[80,128]{1,0:T(8,128)(2,1)S(1)}, bf16[80,128]{1,0:T(8,128)(2,1)S(1)}, u32[]{:S(2)}, u32[]{:S(2)}) collective-permute-start(bf16[80,128]{1,0:T(8,128)(2,1)S(1)} %maximum_maximum_fusion.2), channel_id=1, source_target_pairs={{0,12},{1,13},{2,14},{3,15},{4,8},{5,9},{6,10},{7,11},{8,4},{9,5},... | collective-permute-start | bytes 61448 | tf_op jit(solution)/shard_map/ppermute | solution.py:22
  18.6 0.3 %collective-permute-start.6 = (bf16[512,128]{1,0:T(8,128)(2,1)S(1)}, bf16[512,128]{1,0:T(8,128)(2,1)S(1)}, u32[]{:S(2)}, u32[]{:S(2)}) collective-permute-start(bf16[512,128]{1,0:T(8,128)(2,1)S(1)} %get-tuple-element.69), channel_id=1, source_target_pairs={{0,8},{1,9},{2,10},{3,11},{4,12},{5,13},{6,14},{7,15},{8,0},{9,1},... | collective-permute-start | bytes 393224 | tf_op jit(solution)/shard_map/ppermute | solution.py:22
  18.9 1.4 %collective-permute-done.5 = bf16[80,128]{1,0:T(8,128)(2,1)S(1)} collective-permute-done((bf16[80,128]{1,0:T(8,128)(2,1)S(1)}, bf16[80,128]{1,0:T(8,128)(2,1)S(1)}, u32[]{:S(2)}, u32[]{:S(2)}) %collective-permute-start.5) | collective-permute-done | bytes 20512 | tf_op jit(solution)/shard_map/ppermute | solution.py:22
  20.4 0.0 collective-permute-done.6.mate_ref
  20.4 0.1 maximum_maximum_fusion.3
  20.5 1.2 %collective-permute-start.7 = (bf16[80,128]{1,0:T(8,128)(2,1)S(1)}, bf16[80,128]{1,0:T(8,128)(2,1)S(1)}, u32[]{:S(2)}, u32[]{:S(2)}) collective-permute-start(bf16[80,128]{1,0:T(8,128)(2,1)S(1)} %maximum_maximum_fusion.3), channel_id=1, source_target_pairs={{0,24},{1,25},{2,26},{3,27},{4,28},{5,29},{6,30},{7,31},{8,16},{9,... | collective-permute-start | bytes 61448 | tf_op jit(solution)/shard_map/ppermute | solution.py:22
  21.7 0.1 pad.2.clone
  21.8 0.7 %shard_map.126 = bf16[1024,128]{1,0:T(8,128)(2,1)} custom-call(bf16[512,128]{1,0:T(8,128)(2,1)S(1)} %get-tuple-element.71.own_ref, bf16[512,128]{1,0:T(8,128)(2,1)S(1)} %collective-permute-done.6.mate_ref), custom_call_target="tpu_custom_call" | custom-call | bytes 800000 | tf_op jit(solution)/shard_map/pallas_call | solution.py:325
  22.5 1.2 %collective-permute-done.7 = bf16[80,128]{1,0:T(8,128)(2,1)S(1)} collective-permute-done((bf16[80,128]{1,0:T(8,128)(2,1)S(1)}, bf16[80,128]{1,0:T(8,128)(2,1)S(1)}, u32[]{:S(2)}, u32[]{:S(2)}) %collective-permute-start.7) | collective-permute-done | bytes 20512 | tf_op jit(solution)/shard_map/ppermute | solution.py:22
  23.8 0.1 maximum_maximum_fusion.part_ref
  23.8 0.2 collective-permute-start.8
  24.0 1.0 %collective-permute-done.8.moved_ref = f32[72,128]{1,0:T(8,128)S(1)} collective-permute-done((f32[72,128]{1,0:T(8,128)S(1)}, f32[72,128]{1,0:T(8,128)S(1)}, u32[]{:S(2)}, u32[]{:S(2)}) %collective-permute-start.8) | collective-permute-done | bytes 36896 | tf_op jit(solution)/shard_map/ppermute | solution.py:22
  25.1 0.6 %shard_map.127 = (f32[16,1024]{1,0:T(8,128)}, f32[1,16]{1,0:T(1,128)}) custom-call(f32[72,128]{1,0:T(8,128)S(1)} %maximum_maximum_fusion.part_ref, f32[72,128]{1,0:T(8,128)S(1)} %collective-permute-done.8.moved_ref), custom_call_target="tpu_custom_call" | custom-call | bytes 200000 | tf_op jit(solution)/shard_map/pallas_call | solution.py:325
  (22 shorter events, 0.1 us)
Async XLA Ops:
  0.6 4.7 %collective-permute-start = (s32[1,128]{1,0:T(1,128)}, s32[1,128]{1,0:T(1,128)S(1)}, u32[]{:S(2)}, u32[]{:S(2)}) collective-permute-start(s32[1,128]{1,0:T(1,128)} %refs_3_.1), channel_id=1, source_target_pairs={{0,24},{8,16},{16,8},{24,0},{1,25},{9,17},{17,9},{25,1},{2,26},{10... | collective-permute-start | bytes 1544 | tf_op jit(solution)/shard_map/ppermute | solution.py:22
  3.1 3.4 %copy-start = (bf16[3072,512]{1,0:T(8,128)(2,1)S(1)}, bf16[3072,512]{1,0:T(8,128)(2,1)}, u32[]{:S(2)}) copy-start(bf16[3072,512]{1,0:T(8,128)(2,1)} %table_ref.1) | copy-start | bytes 9437188
  4.6 2.0 %collective-permute-start.1 = (bf16[512,128]{1,0:T(8,128)(2,1)S(1)}, bf16[512,128]{1,0:T(8,128)(2,1)S(1)}, u32[]{:S(2)}, u32[]{:S(2)}) collective-permute-start(bf16[512,128]{1,0:T(8,128)(2,1)S(1)} %get-tuple-element.51), channel_id=1, source_target_pairs={{0,8},{8,0},{16,24},{24,16},{1,9},{9,1},{17,25},{25,17},{2,10},{10... | collective-permute-start | bytes 393224 | tf_op jit(solution)/shard_map/ppermute | solution.py:22
  5.3 1.2 %collective-permute-start.2 = (s32[2,128]{1,0:T(2,128)S(1)}, s32[2,128]{1,0:T(2,128)S(1)}, u32[]{:S(2)}, u32[]{:S(2)}) collective-permute-start(s32[2,128]{1,0:T(2,128)S(1)} %pad_add_fusion), channel_id=1, source_target_pairs={{0,8},{8,0},{16,24},{24,16},{1,9},{9,1},{17,25},{25,17},{2,10},{10... | collective-permute-start | bytes 3080 | tf_op jit(solution)/shard_map/ppermute | solution.py:22
  9.5 3.2 %collective-permute-start.3 = (bf16[80,128]{1,0:T(8,128)(2,1)S(1)}, bf16[80,128]{1,0:T(8,128)(2,1)S(1)}, u32[]{:S(2)}, u32[]{:S(2)}) collective-permute-start(bf16[80,128]{1,0:T(8,128)(2,1)S(1)} %get-tuple-element.54), channel_id=1, source_target_pairs={{0,9},{1,8},{2,11},{3,10},{4,13},{5,12},{6,15},{7,14},{8,1},{9,0},... | collective-permute-start | bytes 61448 | tf_op jit(solution)/shard_map/ppermute | solution.py:22
  12.8 3.2 %collective-permute-start.4 = (bf16[80,128]{1,0:T(8,128)(2,1)S(1)}, bf16[80,128]{1,0:T(8,128)(2,1)S(1)}, u32[]{:S(2)}, u32[]{:S(2)}) collective-permute-start(bf16[80,128]{1,0:T(8,128)(2,1)S(1)} %maximum_maximum_fusion.1), channel_id=1, source_target_pairs={{0,10},{1,11},{2,8},{3,9},{4,14},{5,15},{6,12},{7,13},{8,2},{9,3},... | collective-permute-start | bytes 61448 | tf_op jit(solution)/shard_map/ppermute | solution.py:22
  16.2 4.1 %collective-permute-start.5 = (bf16[80,128]{1,0:T(8,128)(2,1)S(1)}, bf16[80,128]{1,0:T(8,128)(2,1)S(1)}, u32[]{:S(2)}, u32[]{:S(2)}) collective-permute-start(bf16[80,128]{1,0:T(8,128)(2,1)S(1)} %maximum_maximum_fusion.2), channel_id=1, source_target_pairs={{0,12},{1,13},{2,14},{3,15},{4,8},{5,9},{6,10},{7,11},{8,4},{9,5},... | collective-permute-start | bytes 61448 | tf_op jit(solution)/shard_map/ppermute | solution.py:22
  18.6 1.8 %collective-permute-start.6 = (bf16[512,128]{1,0:T(8,128)(2,1)S(1)}, bf16[512,128]{1,0:T(8,128)(2,1)S(1)}, u32[]{:S(2)}, u32[]{:S(2)}) collective-permute-start(bf16[512,128]{1,0:T(8,128)(2,1)S(1)} %get-tuple-element.69), channel_id=1, source_target_pairs={{0,8},{1,9},{2,10},{3,11},{4,12},{5,13},{6,14},{7,15},{8,0},{9,1},... | collective-permute-start | bytes 393224 | tf_op jit(solution)/shard_map/ppermute | solution.py:22
  20.5 3.2 %collective-permute-start.7 = (bf16[80,128]{1,0:T(8,128)(2,1)S(1)}, bf16[80,128]{1,0:T(8,128)(2,1)S(1)}, u32[]{:S(2)}, u32[]{:S(2)}) collective-permute-start(bf16[80,128]{1,0:T(8,128)(2,1)S(1)} %maximum_maximum_fusion.3), channel_id=1, source_target_pairs={{0,24},{1,25},{2,26},{3,27},{4,28},{5,29},{6,30},{7,31},{8,16},{9,... | collective-permute-start | bytes 61448 | tf_op jit(solution)/shard_map/ppermute | solution.py:22
  23.8 1.2 %collective-permute-start.8 = (f32[72,128]{1,0:T(8,128)S(1)}, f32[72,128]{1,0:T(8,128)S(1)}, u32[]{:S(2)}, u32[]{:S(2)}) collective-permute-start(f32[72,128]{1,0:T(8,128)S(1)} %maximum_maximum_fusion.part_ref), channel_id=1, source_target_pairs={{0,8},{1,9},{2,10},{3,11},{4,12},{5,13},{6,14},{7,15},{8,0},{9,1},... | collective-permute-start | bytes 110600 | tf_op jit(solution)/shard_map/ppermute | solution.py:22

commit v8 on v7

--- a/solution.py
+++ b/solution.py
@@ -241,9 +241,9 @@
         cross_re = jnp.where(leading, rere, rere + imim)
         cross_im = jnp.where(leading, imim, left_re * right_im - left_im * right_re)
         cross = jnp.concatenate([cross_re, cross_im], axis=0)
-        cross_hi, cross_lo = halves(cross)
+        cross_hi = cross.astype(BF16)
         near = near_ref[...]
-        terms = dot(near, cross_hi) + dot(near, cross_lo)
+        terms = dot(near, cross_hi)
         terms = terms[: 2 * modes] + terms[2 * modes :]
         sc, ss, sc1, ss1 = (state[i * modes : (i + 1) * modes] for i in range(4))
         dc, ds, dc1, ds1 = (dstate[i * modes : (i + 1) * modes] for i in range(4))

time: 25.9 us -> 25.8 us (level)
  no operation moved by 1% of the time
where the time goes in v8:
time: 25.8 us; the launch traced here: 25.6 us
  starting transfers between devices  10.2 us (40%)
  Pallas kernels  8 us (31%)
  waiting for transfers between devices  6.08 us (24%)
  between operations  0.77 us (3%)
  other arithmetic  0.44 us (2%)
    ppermute x9, starting transfers between devices, xor_permute(): return lax.ppermute(block, axis, [(i, i ^ mask) for i in range(size)])  10.2 us
    pallas_call x7, Pallas kernels, call(): pl.pallas_call(kernel, out_shape=[jax.ShapeDtypeStruct(shape, dtype) for...  8 us
    ppermute x9, waiting for transfers between devices, xor_permute(): return lax.ppermute(block, axis, [(i, i ^ mask) for i in range(size)])  6.08 us
  transfers between devices with their start and end apart: 9, of which 6 were waited for; matrix products, arithmetic and copies ran while one was open for 1% of the time, Pallas kernels for 18%

profile of v8, /device:TPU:0, one launch (start us, length us, event | category | flops | bytes accessed | tf_op | source)
XLA Modules:
  0.0 25.6 jit_solution(16130896999172439146)
XLA Ops:
  0.6 2.5 %collective-permute-start = (s32[1,128]{1,0:T(1,128)}, s32[1,128]{1,0:T(1,128)S(1)}, u32[]{:S(2)}, u32[]{:S(2)}) collective-permute-start(s32[1,128]{1,0:T(1,128)} %refs_3_.1), channel_id=1, source_target_pairs={{0,24},{8,16},{16,8},{24,0},{1,25},{9,17},{17,9},{25,1},{2,26},{10... | collective-permute-start | bytes 1544 | tf_op jit(solution)/shard_map/ppermute | solution.py:22
  3.1 1.5 %shard_map.121 = (s32[1,128]{1,0:T(1,128)S(1)}, f32[7,3072]{1,0:T(8,128)S(1)}, f32[16,1024]{1,0:T(8,128)S(1)}, f32[256,256]{1,0:T(8,128)S(1)}, f32[768,128]{1,0:...) custom-call(f32[1,16]{1,0:T(1,128)} %bitcast.14, f32[768,128]{1,0:T(8,128)} %constant.10.clone.refs_1_, ...), custom_call_target="tpu_custom_call" | custom-call | flops 10000000000 | bytes 40000000 | tf_op jit(solution)/shard_map/pallas_call | solution.py:325
  4.6 0.7 %collective-permute-start.1 = (bf16[512,128]{1,0:T(8,128)(2,1)S(1)}, bf16[512,128]{1,0:T(8,128)(2,1)S(1)}, u32[]{:S(2)}, u32[]{:S(2)}) collective-permute-start(bf16[512,128]{1,0:T(8,128)(2,1)S(1)} %get-tuple-element.51), channel_id=1, source_target_pairs={{0,8},{8,0},{16,24},{24,16},{1,9},{9,1},{17,25},{25,17},{2,10},{10... | collective-permute-start | bytes 393224 | tf_op jit(solution)/shard_map/ppermute | solution.py:22
  5.3 0.0 collective-permute-done.refs_1_
  5.3 0.1 collective-permute-start.2
  5.4 0.3 %shard_map.122 = (bf16[512,128]{1,0:T(8,128)(2,1)S(1)}, bf16[128,384]{1,0:T(8,128)(2,1)S(1)}, bf16[128,128]{1,0:T(8,128)(2,1)S(1)}, bf16[64,256]{1,0:T(8,128)(2,1)S(1)}, f32[256,128]{1,0:T(8,128)S(1)}) custom-call(f32[768,128]{1,0:T(8,128)S(1)} %get-tuple-element.44.table_ref, f32[256,256]{1,0:T(8,128)S(1)} %get-tuple-element.45.fwd_ref), custom_call_target="tpu_custom_call" | custom-call | flops 300000000 | bytes 1000000 | tf_op jit(solution)/shard_map/pallas_call | solution.py:325
  5.7 0.8 %collective-permute-done.2.refs_2_ = s32[2,128]{1,0:T(2,128)S(1)} collective-permute-done((s32[2,128]{1,0:T(2,128)S(1)}, s32[2,128]{1,0:T(2,128)S(1)}, u32[]{:S(2)}, u32[]{:S(2)}) %collective-permute-start.2) | collective-permute-done | bytes 1056 | tf_op jit(solution)/shard_map/ppermute | solution.py:22
  6.5 0.0 collective-permute-done.1.mate_ref
  6.5 0.0 copy-done
  6.5 2.8 %shard_map.123 = (bf16[80,128]{1,0:T(8,128)(2,1)S(1)}, f32[128,1024]{1,0:T(8,128)S(1)}, bf16[128,1024]{1,0:T(8,128)(2,1)S(1)}, f32[256,1024]{1,0:T(8,128)S(1)}, f32[32,1024]{1,0:T(8,128)S(1)}) custom-call(bf16[3072,512]{1,0:T(8,128)(2,1)S(1)} %copy-done, f32[7,3072]{1,0:T(8,128)S(1)} %get-tuple-element.40.short_ref, ...), custom_call_target="tpu_custom_call" | custom-call | flops 1073741824 | bytes 6000000 | tf_op jit(solution)/shard_map/pallas_call | solution.py:325
  9.4 1.3 %collective-permute-start.3 = (bf16[80,128]{1,0:T(8,128)(2,1)S(1)}, bf16[80,128]{1,0:T(8,128)(2,1)S(1)}, u32[]{:S(2)}, u32[]{:S(2)}) collective-permute-start(bf16[80,128]{1,0:T(8,128)(2,1)S(1)} %get-tuple-element.54), channel_id=1, source_target_pairs={{0,9},{1,8},{2,11},{3,10},{4,13},{5,12},{6,15},{7,14},{8,1},{9,0},... | collective-permute-start | bytes 61448 | tf_op jit(solution)/shard_map/ppermute | solution.py:22
  10.7 0.1 pad.14.clone
  10.8 1.0 %shard_map.124 = (f32[256,512]{1,0:T(8,128)S(1)}, bf16[256,288]{1,0:T(8,128)(2,1)S(1)}, f32[1,1024]{1,0:T(1,128)S(1)}) custom-call(f32[256,128]{1,0:T(8,128)S(1)} %get-tuple-element.56.spec_ref, f32[768,128]{1,0:T(8,128)S(1)} %get-tuple-element.44.table_ref, f32[16,1024]{1,0:T(8,128)S(1)} %get-tuple-element.57.res_ref, f32[128,256]{1,0:T(8,128)} %constant.12.clone.inv_ref, ...), custom_call_target="tpu_custom_call" | custom-call | flops 50000000 | bytes 1500000 | tf_op jit(solution)/shard_map/pallas_call | solution.py:325
  11.8 0.8 %collective-permute-done.3 = bf16[80,128]{1,0:T(8,128)(2,1)S(1)} collective-permute-done((bf16[80,128]{1,0:T(8,128)(2,1)S(1)}, bf16[80,128]{1,0:T(8,128)(2,1)S(1)}, u32[]{:S(2)}, u32[]{:S(2)}) %collective-permute-start.3) | collective-permute-done | bytes 20512 | tf_op jit(solution)/shard_map/ppermute | solution.py:22
  12.7 0.1 maximum_maximum_fusion.1
  12.7 1.4 %collective-permute-start.4 = (bf16[80,128]{1,0:T(8,128)(2,1)S(1)}, bf16[80,128]{1,0:T(8,128)(2,1)S(1)}, u32[]{:S(2)}, u32[]{:S(2)}) collective-permute-start(bf16[80,128]{1,0:T(8,128)(2,1)S(1)} %maximum_maximum_fusion.1), channel_id=1, source_target_pairs={{0,10},{1,11},{2,8},{3,9},{4,14},{5,15},{6,12},{7,13},{8,2},{9,3},... | collective-permute-start | bytes 61448 | tf_op jit(solution)/shard_map/ppermute | solution.py:22
  14.1 1.0 %shard_map.125 = (bf16[512,128]{1,0:T(8,128)(2,1)S(1)}, bf16[512,128]{1,0:T(8,128)(2,1)S(1)}) custom-call(f32[128,1024]{1,0:T(8,128)S(1)} %get-tuple-element.60.query_ref, bf16[128,1024]{1,0:T(8,128)(2,1)S(1)} %get-tuple-element.61.gated_ref, f32[256,1024]{1,0:T(8,128)S(1)} %get-tuple-element.62.spec_ref, f32[256,512]{1,0:T(8,128)S(1)} %get-tuple-element.63.filt_ref, ...), custom_call_target="tpu_custom_call" | custom-call | flops 300000000 | bytes 3000000 | tf_op jit(solution)/shard_map/pallas_call | solution.py:325
  15.2 0.8 %collective-permute-done.4 = bf16[80,128]{1,0:T(8,128)(2,1)S(1)} collective-permute-done((bf16[80,128]{1,0:T(8,128)(2,1)S(1)}, bf16[80,128]{1,0:T(8,128)(2,1)S(1)}, u32[]{:S(2)}, u32[]{:S(2)}) %collective-permute-start.4) | collective-permute-done | bytes 20512 | tf_op jit(solution)/shard_map/ppermute | solution.py:22
  16.0 0.1 maximum_maximum_fusion.2
  16.1 2.4 %collective-permute-start.5 = (bf16[80,128]{1,0:T(8,128)(2,1)S(1)}, bf16[80,128]{1,0:T(8,128)(2,1)S(1)}, u32[]{:S(2)}, u32[]{:S(2)}) collective-permute-start(bf16[80,128]{1,0:T(8,128)(2,1)S(1)} %maximum_maximum_fusion.2), channel_id=1, source_target_pairs={{0,12},{1,13},{2,14},{3,15},{4,8},{5,9},{6,10},{7,11},{8,4},{9,5},... | collective-permute-start | bytes 61448 | tf_op jit(solution)/shard_map/ppermute | solution.py:22
  18.5 0.3 %collective-permute-start.6 = (bf16[512,128]{1,0:T(8,128)(2,1)S(1)}, bf16[512,128]{1,0:T(8,128)(2,1)S(1)}, u32[]{:S(2)}, u32[]{:S(2)}) collective-permute-start(bf16[512,128]{1,0:T(8,128)(2,1)S(1)} %get-tuple-element.69), channel_id=1, source_target_pairs={{0,8},{1,9},{2,10},{3,11},{4,12},{5,13},{6,14},{7,15},{8,0},{9,1},... | collective-permute-start | bytes 393224 | tf_op jit(solution)/shard_map/ppermute | solution.py:22
  18.9 1.4 %collective-permute-done.5 = bf16[80,128]{1,0:T(8,128)(2,1)S(1)} collective-permute-done((bf16[80,128]{1,0:T(8,128)(2,1)S(1)}, bf16[80,128]{1,0:T(8,128)(2,1)S(1)}, u32[]{:S(2)}, u32[]{:S(2)}) %collective-permute-start.5) | collective-permute-done | bytes 20512 | tf_op jit(solution)/shard_map/ppermute | solution.py:22
  20.3 0.0 collective-permute-done.6.mate_ref
  20.3 0.1 maximum_maximum_fusion.3
  20.4 1.2 %collective-permute-start.7 = (bf16[80,128]{1,0:T(8,128)(2,1)S(1)}, bf16[80,128]{1,0:T(8,128)(2,1)S(1)}, u32[]{:S(2)}, u32[]{:S(2)}) collective-permute-start(bf16[80,128]{1,0:T(8,128)(2,1)S(1)} %maximum_maximum_fusion.3), channel_id=1, source_target_pairs={{0,24},{1,25},{2,26},{3,27},{4,28},{5,29},{6,30},{7,31},{8,16},{9,... | collective-permute-start | bytes 61448 | tf_op jit(solution)/shard_map/ppermute | solution.py:22
  21.6 0.1 pad.2.clone
  21.7 0.7 %shard_map.126 = bf16[1024,128]{1,0:T(8,128)(2,1)} custom-call(bf16[512,128]{1,0:T(8,128)(2,1)S(1)} %get-tuple-element.71.own_ref, bf16[512,128]{1,0:T(8,128)(2,1)S(1)} %collective-permute-done.6.mate_ref), custom_call_target="tpu_custom_call" | custom-call | bytes 800000 | tf_op jit(solution)/shard_map/pallas_call | solution.py:325
  22.4 1.2 %collective-permute-done.7 = bf16[80,128]{1,0:T(8,128)(2,1)S(1)} collective-permute-done((bf16[80,128]{1,0:T(8,128)(2,1)S(1)}, bf16[80,128]{1,0:T(8,128)(2,1)S(1)}, u32[]{:S(2)}, u32[]{:S(2)}) %collective-permute-start.7) | collective-permute-done | bytes 20512 | tf_op jit(solution)/shard_map/ppermute | solution.py:22
  23.7 0.1 maximum_maximum_fusion.part_ref
  23.8 0.2 collective-permute-start.8
  24.0 1.0 %collective-permute-done.8.moved_ref = f32[72,128]{1,0:T(8,128)S(1)} collective-permute-done((f32[72,128]{1,0:T(8,128)S(1)}, f32[72,128]{1,0:T(8,128)S(1)}, u32[]{:S(2)}, u32[]{:S(2)}) %collective-permute-start.8) | collective-permute-done | bytes 36896 | tf_op jit(solution)/shard_map/ppermute | solution.py:22
  25.0 0.6 %shard_map.127 = (f32[16,1024]{1,0:T(8,128)}, f32[1,16]{1,0:T(1,128)}) custom-call(f32[72,128]{1,0:T(8,128)S(1)} %maximum_maximum_fusion.part_ref, f32[72,128]{1,0:T(8,128)S(1)} %collective-permute-done.8.moved_ref), custom_call_target="tpu_custom_call" | custom-call | bytes 200000 | tf_op jit(solution)/shard_map/pallas_call | solution.py:325
  (22 shorter events, 0.1 us)
Async XLA Ops:
  0.6 4.7 %collective-permute-start = (s32[1,128]{1,0:T(1,128)}, s32[1,128]{1,0:T(1,128)S(1)}, u32[]{:S(2)}, u32[]{:S(2)}) collective-permute-start(s32[1,128]{1,0:T(1,128)} %refs_3_.1), channel_id=1, source_target_pairs={{0,24},{8,16},{16,8},{24,0},{1,25},{9,17},{17,9},{25,1},{2,26},{10... | collective-permute-start | bytes 1544 | tf_op jit(solution)/shard_map/ppermute | solution.py:22
  3.1 3.4 %copy-start = (bf16[3072,512]{1,0:T(8,128)(2,1)S(1)}, bf16[3072,512]{1,0:T(8,128)(2,1)}, u32[]{:S(2)}) copy-start(bf16[3072,512]{1,0:T(8,128)(2,1)} %table_ref.1) | copy-start | bytes 9437188
  4.6 2.0 %collective-permute-start.1 = (bf16[512,128]{1,0:T(8,128)(2,1)S(1)}, bf16[512,128]{1,0:T(8,128)(2,1)S(1)}, u32[]{:S(2)}, u32[]{:S(2)}) collective-permute-start(bf16[512,128]{1,0:T(8,128)(2,1)S(1)} %get-tuple-element.51), channel_id=1, source_target_pairs={{0,8},{8,0},{16,24},{24,16},{1,9},{9,1},{17,25},{25,17},{2,10},{10... | collective-permute-start | bytes 393224 | tf_op jit(solution)/shard_map/ppermute | solution.py:22
  5.3 1.2 %collective-permute-start.2 = (s32[2,128]{1,0:T(2,128)S(1)}, s32[2,128]{1,0:T(2,128)S(1)}, u32[]{:S(2)}, u32[]{:S(2)}) collective-permute-start(s32[2,128]{1,0:T(2,128)S(1)} %pad_add_fusion), channel_id=1, source_target_pairs={{0,8},{8,0},{16,24},{24,16},{1,9},{9,1},{17,25},{25,17},{2,10},{10... | collective-permute-start | bytes 3080 | tf_op jit(solution)/shard_map/ppermute | solution.py:22
  9.4 3.2 %collective-permute-start.3 = (bf16[80,128]{1,0:T(8,128)(2,1)S(1)}, bf16[80,128]{1,0:T(8,128)(2,1)S(1)}, u32[]{:S(2)}, u32[]{:S(2)}) collective-permute-start(bf16[80,128]{1,0:T(8,128)(2,1)S(1)} %get-tuple-element.54), channel_id=1, source_target_pairs={{0,9},{1,8},{2,11},{3,10},{4,13},{5,12},{6,15},{7,14},{8,1},{9,0},... | collective-permute-start | bytes 61448 | tf_op jit(solution)/shard_map/ppermute | solution.py:22
  12.7 3.2 %collective-permute-start.4 = (bf16[80,128]{1,0:T(8,128)(2,1)S(1)}, bf16[80,128]{1,0:T(8,128)(2,1)S(1)}, u32[]{:S(2)}, u32[]{:S(2)}) collective-permute-start(bf16[80,128]{1,0:T(8,128)(2,1)S(1)} %maximum_maximum_fusion.1), channel_id=1, source_target_pairs={{0,10},{1,11},{2,8},{3,9},{4,14},{5,15},{6,12},{7,13},{8,2},{9,3},... | collective-permute-start | bytes 61448 | tf_op jit(solution)/shard_map/ppermute | solution.py:22
  16.1 4.1 %collective-permute-start.5 = (bf16[80,128]{1,0:T(8,128)(2,1)S(1)}, bf16[80,128]{1,0:T(8,128)(2,1)S(1)}, u32[]{:S(2)}, u32[]{:S(2)}) collective-permute-start(bf16[80,128]{1,0:T(8,128)(2,1)S(1)} %maximum_maximum_fusion.2), channel_id=1, source_target_pairs={{0,12},{1,13},{2,14},{3,15},{4,8},{5,9},{6,10},{7,11},{8,4},{9,5},... | collective-permute-start | bytes 61448 | tf_op jit(solution)/shard_map/ppermute | solution.py:22
  18.5 1.8 %collective-permute-start.6 = (bf16[512,128]{1,0:T(8,128)(2,1)S(1)}, bf16[512,128]{1,0:T(8,128)(2,1)S(1)}, u32[]{:S(2)}, u32[]{:S(2)}) collective-permute-start(bf16[512,128]{1,0:T(8,128)(2,1)S(1)} %get-tuple-element.69), channel_id=1, source_target_pairs={{0,8},{1,9},{2,10},{3,11},{4,12},{5,13},{6,14},{7,15},{8,0},{9,1},... | collective-permute-start | bytes 393224 | tf_op jit(solution)/shard_map/ppermute | solution.py:22
  20.4 3.2 %collective-permute-start.7 = (bf16[80,128]{1,0:T(8,128)(2,1)S(1)}, bf16[80,128]{1,0:T(8,128)(2,1)S(1)}, u32[]{:S(2)}, u32[]{:S(2)}) collective-permute-start(bf16[80,128]{1,0:T(8,128)(2,1)S(1)} %maximum_maximum_fusion.3), channel_id=1, source_target_pairs={{0,24},{1,25},{2,26},{3,27},{4,28},{5,29},{6,30},{7,31},{8,16},{9,... | collective-permute-start | bytes 61448 | tf_op jit(solution)/shard_map/ppermute | solution.py:22
  23.8 1.2 %collective-permute-start.8 = (f32[72,128]{1,0:T(8,128)S(1)}, f32[72,128]{1,0:T(8,128)S(1)}, u32[]{:S(2)}, u32[]{:S(2)}) collective-permute-start(f32[72,128]{1,0:T(8,128)S(1)} %maximum_maximum_fusion.part_ref), channel_id=1, source_target_pairs={{0,8},{1,9},{2,10},{3,11},{4,12},{5,13},{6,14},{7,15},{8,0},{9,1},... | collective-permute-start | bytes 110600 | tf_op jit(solution)/shard_map/ppermute | solution.py:22
